TPU v7x, 512 devices: a whole 4x4x16 slice. The times are simulated.
512 devices in a mesh: grp: 16 (over x, y), gx: 16 (over z_lo, core), gy: 2 (over z_hi).
Axes of the slice: x: 4, y: 4, z: 16 (z_hi: 2, z_lo: 8; z = z_hi * 8 + z_lo), core: 2. Of those that a mesh axis runs over, the one named last changes fastest.
Arguments:
- air: float32 [2, 32, 512, 1536], P(None, None, ('grp', 'gx'), 'gy'), may hold values from -6 to 6
- kdiff: float32 [512, 1536], P(('grp', 'gx'), 'gy'), may hold values from 0.02 to 0.2
- u_wind: float32 [32], replicated, may hold values from -0.15 to 0.15
- v_wind: float32 [32], replicated, may hold values from -0.15 to 0.15
- elev: float32 [2048, 6144], P(('grp', 'gx'), 'gy'), may hold values from 0 to 1
- cond: float32 [2048, 6144], P(('grp', 'gx'), 'gy'), may hold values from 0.01 to 0.1
- rain_factor: float32 [2048, 6144], P(('grp', 'gx'), 'gy'), may hold values from 0.5 to 2
- land_mask: int32 [2048, 6144], P(('grp', 'gx'), 'gy'), may hold values 0 or 1
- flow_code: int32 [2048, 6144], P(('grp', 'gx'), 'gy'), may hold values from 0 to 3
- depth_init: float32 [2048, 6144], P(('grp', 'gx'), 'gy'), may hold values from 0 to 0.5
- soil_init: float32 [2048, 6144], P(('grp', 'gx'), 'gy'), may hold values from 0 to 1
- link_cell: int32 [131072], P(('grp', 'gx', 'gy')), may hold values from 0 to 24575
- link_down: int32 [131072], P(('grp', 'gx', 'gy')), may hold values from 0 to 512, as said below
- link_flow: float32 [131072], P(('grp', 'gx', 'gy')), may hold values from 0 to 1
Outputs:
- air_out: float32 [2, 32, 512, 1536], P(None, None, ('grp', 'gx'), 'gy')
- depth_out: float32 [2048, 6144], P(('grp', 'gx'), 'gy')
- soil_coarse: float32 [512, 1536], P(('grp', 'gx'), 'gy')
- channel_flow: float32 [131072], P(('grp', 'gx', 'gy'))
Inputs may be any that keep to these rules, and one draw needn't show every extreme that they name: `link_down`: for a link of device d with value v: v < 256 names link v of the same device, 256 <= v < 512 names link v - 256 of the device with the next grp+gx index and the same gy, 512 is an outlet; devices of the last grp+gx index hold no values in the middle range. `link_cell`: A cell of the link's own device's block of the terrain grid, as row * 3072 + column.
All inputs are finite; a program needn't handle non-finite values. No bound on the sum of `land_mask` on one device may be relied on, other than what follows from the above.
Results may differ from a plain program's by a relative error of at most 0.00025.
Values sent between devices are 32-bit elements; how exact they have to be, the bound alone decides.
No kernel may reach another device: no remote copies, remote signals or barrier semaphores. Data moves between devices by JAX's collectives and lax.ppermute only.
A program may use at most 64 MiB of HBM per device.

v0:
```python
import jax
import jax.numpy as jnp
from jax import lax
from jax.sharding import PartitionSpec as P

ASTEPS = 2
HSTEPS = 4
COUPLE = 2


def shifted(value, axis, steps):
    count = lax.axis_size(axis)
    first, last = (max(0, -steps), min(count, count - steps))
    return lax.ppermute(value, axis, [(source, source + steps) for source in range(first, last)])


def padded_2(block, sides, width):
    for axis, dim in sides:
        count = lax.axis_size(axis)
        forward = [(i, i + 1) for i in range(count - 1)]
        backward = [(target, source) for source, target in forward]
        low = lax.ppermute(
            lax.slice_in_dim(block, block.shape[dim] - width, None, axis=dim), axis, forward
        )
        high = lax.ppermute(lax.slice_in_dim(block, 0, width, axis=dim), axis, backward)
        block = jnp.concatenate([low, block, high], axis=dim)
    return block


def advance(padded, kd_region, u_wind, v_wind):
    centre = padded[:, :, 1:-1, 1:-1]
    north = padded[:, :, :-2, 1:-1]
    south = padded[:, :, 2:, 1:-1]
    west = padded[:, :, 1:-1, :-2]
    east = padded[:, :, 1:-1, 2:]
    lap = north + south + west + east - 4.0 * centre
    return (
        centre
        + kd_region * lap
        - 0.5 * u_wind[:, None, None] * (east - west)
        - 0.5 * v_wind[:, None, None] * (south - north)
    )


def route_links(flow, routing, lateral, links):
    routed = jnp.dot(
        flow, routing, precision=lax.Precision.HIGHEST, preferred_element_type=jnp.float32
    )
    arriving = shifted(routed[links:], ("grp", "gx"), 1)
    return flow + 0.5 * (routed[:links] + arriving - flow) + lateral


def shards(
    air,
    kdiff,
    u_wind,
    v_wind,
    elev,
    cond,
    rain_factor,
    land_mask,
    flow_code,
    depth_init,
    soil_init,
    link_cell,
    link_down,
    link_flow,
):
    rows = air.shape[2]
    cols = air.shape[3]
    links = link_flow.shape[0]
    depth = depth_init
    soil = soil_init
    flow = link_flow
    mask = land_mask.astype(jnp.float32)
    reach = 1
    codes = padded_2(flow_code, ((("grp", "gx"), 0), ("gy", 1)), reach)
    columns = jnp.arange(2 * links, dtype=jnp.int32)
    routing = (link_down[:, None] == columns[None, :]).astype(jnp.float32)
    soil_coarse = jnp.zeros((rows, cols), jnp.float32)
    for cycle in range(COUPLE):
        for step in range(ASTEPS):
            padded = padded_2(air, ((("grp", "gx"), 2), ("gy", 3)), 1)
            air = advance(padded, kdiff, u_wind, v_wind)
        ground = air[1, 0]
        rain = 0.05 * ground * ground
        air = air.at[1, 0].add(-rain)
        rain_fine = jnp.repeat(jnp.repeat(rain, 4, axis=0), 4, axis=1) * rain_factor
        for step in range(HSTEPS):
            eta = elev + depth
            out = 0.2 * depth
            padded = padded_2(jnp.stack([eta, out]), ((("grp", "gx"), 1), ("gy", 2)), 1)
            pe = padded[0]
            po = padded[1]
            inflow = (
                po[1:-1, :-2] * (codes[1:-1, :-2] == 0)
                + po[1:-1, 2:] * (codes[1:-1, 2:] == 2)
                + po[2:, 1:-1] * (codes[2:, 1:-1] == 1)
                + po[:-2, 1:-1] * (codes[:-2, 1:-1] == 3)
            )
            lap = pe[:-2, 1:-1] + pe[2:, 1:-1] + pe[1:-1, :-2] + pe[1:-1, 2:] - 4.0 * eta
            lateral = 0.1 * depth.reshape(-1)[link_cell]
            flow = route_links(flow, routing, lateral, links)
            soil = soil + 0.05 * mask * depth - 0.02 * soil
            depth = mask * (depth + rain_fine - out + inflow - 0.05 * depth + cond * lap)
        soil_coarse = soil.reshape(rows, 4, cols, 4).mean(axis=(1, 3))
        air = air.at[1, 0].add(0.1 * soil_coarse * jax.nn.sigmoid(air[0, 0]))
    return (air, depth, soil_coarse, flow)


def solution(mesh):
    placed = (
        P(None, None, ("grp", "gx"), "gy"),
        P(("grp", "gx"), "gy"),
        P(),
        P(),
        P(("grp", "gx"), "gy"),
        P(("grp", "gx"), "gy"),
        P(("grp", "gx"), "gy"),
        P(("grp", "gx"), "gy"),
        P(("grp", "gx"), "gy"),
        P(("grp", "gx"), "gy"),
        P(("grp", "gx"), "gy"),
        P(("grp", "gx", "gy")),
        P(("grp", "gx", "gy")),
        P(("grp", "gx", "gy")),
    )
    return jax.shard_map(
        shards,
        mesh=mesh,
        in_specs=placed,
        out_specs=(
            P(None, None, ("grp", "gx"), "gy"),
            P(("grp", "gx"), "gy"),
            P(("grp", "gx"), "gy"),
            P(("grp", "gx", "gy")),
        ),
        check_vma=False,
    )
```

profile of v0, /device:TPU:6, one launch (start us, length us, event | category | flops | bytes accessed | tf_op | source)
XLA Modules:
  0.0 524.7 jit_solution(12133732001643337818)
XLA Ops:
  2.2 1.9 collective-permute-start
  4.1 15.3 %collective-permute-start.1 = (f32[2,32,1,768]{3,2,1,0:T(1,128)S(1)}, f32[2,32,1,768]{3,2,1,0:T(1,128)S(1)}, u32[]{:S(2)}, u32[]{:S(2)}) collective-permute-start(f32[2,32,1,768]{3,2,1,0:T(1,128)S(1)} %get-tuple-element.103), channel_id=1, source_target_pairs={{2,0},{4,2},{6,4},{8,6},{10,8},{12,10},{14,12},{16,14},{18,16},{20... | collective-permute-start | bytes 589832 | tf_op jit(solution)/shard_map/ppermute | solution.py:25
  20.5 1.9 collective-permute-start.11
  23.4 1.9 collective-permute-start.8
  26.4 1.9 collective-permute-start.52
  32.4 8.5 %collective-permute-done.52 = f32[256]{0:T(256)S(1)} collective-permute-done((f32[256]{0:T(256)S(1)}, f32[256]{0:T(256)S(1)}, u32[]{:S(2)}, u32[]{:S(2)}) %collective-permute-start.52) | collective-permute-done | bytes 1056 | tf_op jit(solution)/shard_map/ppermute | solution.py:14
  40.9 4.8 collective-permute-start.9
  46.6 2.4 collective-permute-start.12
  49.0 1.9 collective-permute-start.53
  52.2 13.7 %collective-permute-start.2 = (f32[2,32,4,1]{3,2,1,0:T(4,128)S(1)}, f32[2,32,4,1]{3,2,1,0:T(4,128)S(1)}, u32[]{:S(2)}, u32[]{:S(2)}) collective-permute-start(f32[2,32,4,1]{3,2,1,0:T(4,128)S(1)} %get-tuple-element.94), channel_id=1, source_target_pairs={{0,1},{2,3},{4,5},{6,7},{8,9},{10,11},{12,13},{14,15},{16,17},{18,... | collective-permute-start | bytes 3080 | tf_op jit(solution)/shard_map/ppermute | solution.py:22
  67.2 13.3 %collective-permute-start.13 = (f32[2,10,1]{2,0,1:T(2,128)S(1)}, f32[2,10,1]{2,0,1:T(2,128)S(1)}, u32[]{:S(2)}, u32[]{:S(2)}) collective-permute-start(f32[2,10,1]{2,0,1:T(2,128)S(1)} %get-tuple-element.135), channel_id=1, source_target_pairs={{0,1},{2,3},{4,5},{6,7},{8,9},{10,11},{12,13},{14,15},{16,17},{18,... | collective-permute-start | bytes 248 | tf_op jit(solution)/shard_map/ppermute | solution.py:22
  81.9 13.8 %collective-permute-start.10 = (s32[10,1]{1,0:T(8,128)}, s32[10,1]{1,0:T(8,128)}, u32[]{:S(2)}, u32[]{:S(2)}) collective-permute-start(s32[10,1]{1,0:T(8,128)} %get-tuple-element.153), channel_id=1, source_target_pairs={{0,1},{2,3},{4,5},{6,7},{8,9},{10,11},{12,13},{14,15},{16,17},{18,... | collective-permute-start | bytes 128 | tf_op jit(solution)/shard_map/ppermute | solution.py:22
  97.5 3.5 multiply_subtract_fusion.3
  101.3 1.9 collective-permute-start.4
  103.3 13.3 %collective-permute-start.5 = (f32[2,32,1,768]{3,2,1,0:T(1,128)S(1)}, f32[2,32,1,768]{3,2,1,0:T(1,128)S(1)}, u32[]{:S(2)}, u32[]{:S(2)}) collective-permute-start(f32[2,32,1,768]{3,2,1,0:T(1,128)S(1)} %get-tuple-element.101), channel_id=1, source_target_pairs={{2,0},{4,2},{6,4},{8,6},{10,8},{12,10},{14,12},{16,14},{18,16},{20... | collective-permute-start | bytes 589832 | tf_op jit(solution)/shard_map/ppermute | solution.py:25
  118.0 4.2 collective-permute-done.5
  122.6 13.0 %collective-permute-start.6 = (f32[2,32,4,1]{3,2,1,0:T(4,128)S(1)}, f32[2,32,4,1]{3,2,1,0:T(4,128)S(1)}, u32[]{:S(2)}, u32[]{:S(2)}) collective-permute-start(f32[2,32,4,1]{3,2,1,0:T(4,128)S(1)} %get-tuple-element.92), channel_id=1, source_target_pairs={{0,1},{2,3},{4,5},{6,7},{8,9},{10,11},{12,13},{14,15},{16,17},{18,... | collective-permute-start | bytes 3080 | tf_op jit(solution)/shard_map/ppermute | solution.py:22
  138.1 13.1 %collective-permute-done.7 = f32[2,32,4,1]{3,2,1,0:T(4,128)S(1)} collective-permute-done((f32[2,32,4,1]{3,2,1,0:T(4,128)S(1)}, f32[2,32,4,1]{3,2,1,0:T(4,128)S(1)}, u32[]{:S(2)}, u32[]{:S(2)}) %collective-permute-start.7) | collective-permute-done | bytes 1056 | tf_op jit(solution)/shard_map/ppermute | solution.py:25
  151.2 3.5 multiply_subtract_fusion.2
  157.1 1.9 collective-permute-start.16
  159.1 13.3 %collective-permute-start.17 = (f32[2,1,3072]{2,0,1:T(2,128)S(1)}, f32[2,1,3072]{2,0,1:T(2,128)S(1)}, u32[]{:S(2)}, u32[]{:S(2)}) collective-permute-start(f32[2,1,3072]{2,0,1:T(2,128)S(1)} %copy.541), channel_id=1, source_target_pairs={{2,0},{4,2},{6,4},{8,6},{10,8},{12,10},{14,12},{16,14},{18,16},{20... | collective-permute-start | bytes 73736 | tf_op jit(solution)/shard_map/ppermute | solution.py:25
  175.2 1.9 collective-permute-start.54
  180.9 12.9 %collective-permute-done.19 = f32[2,10,1]{2,0,1:T(2,128)S(1)} collective-permute-done((f32[2,10,1]{2,0,1:T(2,128)S(1)}, f32[2,10,1]{2,0,1:T(2,128)S(1)}, u32[]{:S(2)}, u32[]{:S(2)}) %collective-permute-start.19) | collective-permute-done | bytes 112 | tf_op jit(solution)/shard_map/ppermute | solution.py:25
  196.7 2.1 collective-permute-start.20
  199.2 1.9 collective-permute-start.55
  201.1 13.3 %collective-permute-start.21 = (f32[2,1,3072]{2,0,1:T(2,128)S(1)}, f32[2,1,3072]{2,0,1:T(2,128)S(1)}, u32[]{:S(2)}, u32[]{:S(2)}) collective-permute-start(f32[2,1,3072]{2,0,1:T(2,128)S(1)} %copy.546), channel_id=1, source_target_pairs={{2,0},{4,2},{6,4},{8,6},{10,8},{12,10},{14,12},{16,14},{18,16},{20... | collective-permute-start | bytes 73736 | tf_op jit(solution)/shard_map/ppermute | solution.py:25
  219.0 13.0 %collective-permute-done.23 = f32[2,10,1]{2,0,1:T(2,128)S(1)} collective-permute-done((f32[2,10,1]{2,0,1:T(2,128)S(1)}, f32[2,10,1]{2,0,1:T(2,128)S(1)}, u32[]{:S(2)}, u32[]{:S(2)}) %collective-permute-start.23) | collective-permute-done | bytes 112 | tf_op jit(solution)/shard_map/ppermute | solution.py:25
  242.4 13.2 %collective-permute-start.33 = (f32[2,1,3072]{2,0,1:T(2,128)}, f32[2,1,3072]{2,0,1:T(2,128)}, u32[]{:S(2)}, u32[]{:S(2)}) collective-permute-start(f32[2,1,3072]{2,0,1:T(2,128)} %copy.551), channel_id=1, source_target_pairs={{2,0},{4,2},{6,4},{8,6},{10,8},{12,10},{14,12},{16,14},{18,16},{20... | collective-permute-start | bytes 73736 | tf_op jit(solution)/shard_map/ppermute | solution.py:25
  255.6 4.1 reshape.213
  265.5 13.3 %collective-permute-start.25 = (f32[2,32,1,768]{3,2,1,0:T(1,128)S(1)}, f32[2,32,1,768]{3,2,1,0:T(1,128)S(1)}, u32[]{:S(2)}, u32[]{:S(2)}) collective-permute-start(f32[2,32,1,768]{3,2,1,0:T(1,128)S(1)} %get-tuple-element.99), channel_id=1, source_target_pairs={{2,0},{4,2},{6,4},{8,6},{10,8},{12,10},{14,12},{16,14},{18,16},{20... | collective-permute-start | bytes 589832 | tf_op jit(solution)/shard_map/ppermute | solution.py:25
  284.4 14.0 %collective-permute-done.35 = f32[2,10,1]{2,0,1:T(2,128)S(1)} collective-permute-done((f32[2,10,1]{2,0,1:T(2,128)S(1)}, f32[2,10,1]{2,0,1:T(2,128)S(1)}, u32[]{:S(2)}, u32[]{:S(2)}) %collective-permute-start.35) | collective-permute-done | bytes 112 | tf_op jit(solution)/shard_map/ppermute | solution.py:25
  307.8 13.3 %collective-permute-start.37 = (f32[2,1,3072]{2,0,1:T(2,128)S(1)}, f32[2,1,3072]{2,0,1:T(2,128)S(1)}, u32[]{:S(2)}, u32[]{:S(2)}) collective-permute-start(f32[2,1,3072]{2,0,1:T(2,128)S(1)} %copy.558), channel_id=1, source_target_pairs={{2,0},{4,2},{6,4},{8,6},{10,8},{12,10},{14,12},{16,14},{18,16},{20... | collective-permute-start | bytes 73736 | tf_op jit(solution)/shard_map/ppermute | solution.py:25
  325.4 14.9 %collective-permute-done.27 = f32[2,32,4,1]{3,2,1,0:T(4,128)S(1)} collective-permute-done((f32[2,32,4,1]{3,2,1,0:T(4,128)S(1)}, f32[2,32,4,1]{3,2,1,0:T(4,128)S(1)}, u32[]{:S(2)}, u32[]{:S(2)}) %collective-permute-start.27) | collective-permute-done | bytes 1056 | tf_op jit(solution)/shard_map/ppermute | solution.py:25
  340.4 3.5 multiply_subtract_fusion.1
  344.2 1.9 collective-permute-start.28
  346.1 13.3 %collective-permute-start.29 = (f32[2,32,1,768]{3,2,1,0:T(1,128)S(1)}, f32[2,32,1,768]{3,2,1,0:T(1,128)S(1)}, u32[]{:S(2)}, u32[]{:S(2)}) collective-permute-start(f32[2,32,1,768]{3,2,1,0:T(1,128)S(1)} %get-tuple-element.97), channel_id=1, source_target_pairs={{2,0},{4,2},{6,4},{8,6},{10,8},{12,10},{14,12},{16,14},{18,16},{20... | collective-permute-start | bytes 589832 | tf_op jit(solution)/shard_map/ppermute | solution.py:25
  362.7 12.5 %collective-permute-done.39 = f32[2,10,1]{2,0,1:T(2,128)S(1)} collective-permute-done((f32[2,10,1]{2,0,1:T(2,128)S(1)}, f32[2,10,1]{2,0,1:T(2,128)S(1)}, u32[]{:S(2)}, u32[]{:S(2)}) %collective-permute-start.39) | collective-permute-done | bytes 112 | tf_op jit(solution)/shard_map/ppermute | solution.py:25
  380.2 13.1 %collective-permute-done.31 = f32[2,32,4,1]{3,2,1,0:T(4,128)S(1)} collective-permute-done((f32[2,32,4,1]{3,2,1,0:T(4,128)S(1)}, f32[2,32,4,1]{3,2,1,0:T(4,128)S(1)}, u32[]{:S(2)}, u32[]{:S(2)}) %collective-permute-start.31) | collective-permute-done | bytes 1056 | tf_op jit(solution)/shard_map/ppermute | solution.py:25
  393.2 3.6 multiply_subtract_fusion
  401.9 1.9 collective-permute-start.58
  403.9 1.9 collective-permute-start.40
  405.9 13.3 %collective-permute-start.41 = (f32[2,1,3072]{2,0,1:T(2,128)S(1)}, f32[2,1,3072]{2,0,1:T(2,128)S(1)}, u32[]{:S(2)}, u32[]{:S(2)}) collective-permute-start(f32[2,1,3072]{2,0,1:T(2,128)S(1)} %copy.563), channel_id=1, source_target_pairs={{2,0},{4,2},{6,4},{8,6},{10,8},{12,10},{14,12},{16,14},{18,16},{20... | collective-permute-start | bytes 73736 | tf_op jit(solution)/shard_map/ppermute | solution.py:25
  423.6 12.9 %collective-permute-done.43 = f32[2,10,1]{2,0,1:T(2,128)S(1)} collective-permute-done((f32[2,10,1]{2,0,1:T(2,128)S(1)}, f32[2,10,1]{2,0,1:T(2,128)S(1)}, u32[]{:S(2)}, u32[]{:S(2)}) %collective-permute-start.43) | collective-permute-done | bytes 112 | tf_op jit(solution)/shard_map/ppermute | solution.py:25
  444.3 13.3 %collective-permute-start.45 = (f32[2,1,3072]{2,0,1:T(2,128)S(1)}, f32[2,1,3072]{2,0,1:T(2,128)S(1)}, u32[]{:S(2)}, u32[]{:S(2)}) collective-permute-start(f32[2,1,3072]{2,0,1:T(2,128)S(1)} %copy.568), channel_id=1, source_target_pairs={{2,0},{4,2},{6,4},{8,6},{10,8},{12,10},{14,12},{16,14},{18,16},{20... | collective-permute-start | bytes 73736 | tf_op jit(solution)/shard_map/ppermute | solution.py:25
  462.1 12.9 %collective-permute-done.47 = f32[2,10,1]{2,0,1:T(2,128)S(1)} collective-permute-done((f32[2,10,1]{2,0,1:T(2,128)S(1)}, f32[2,10,1]{2,0,1:T(2,128)S(1)}, u32[]{:S(2)}, u32[]{:S(2)}) %collective-permute-start.47) | collective-permute-done | bytes 112 | tf_op jit(solution)/shard_map/ppermute | solution.py:25
  480.7 13.2 %collective-permute-start.49 = (f32[2,1,3072]{2,0,1:T(2,128)}, f32[2,1,3072]{2,0,1:T(2,128)}, u32[]{:S(2)}, u32[]{:S(2)}) collective-permute-start(f32[2,1,3072]{2,0,1:T(2,128)} %copy.573), channel_id=1, source_target_pairs={{2,0},{4,2},{6,4},{8,6},{10,8},{12,10},{14,12},{16,14},{18,16},{20... | collective-permute-start | bytes 73736 | tf_op jit(solution)/shard_map/ppermute | solution.py:25
  494.0 4.1 reshape.216
  510.1 12.9 %collective-permute-done.51 = f32[2,10,1]{2,0,1:T(2,128)S(1)} collective-permute-done((f32[2,10,1]{2,0,1:T(2,128)S(1)}, f32[2,10,1]{2,0,1:T(2,128)S(1)}, u32[]{:S(2)}, u32[]{:S(2)}) %collective-permute-start.51) | collective-permute-done | bytes 112 | tf_op jit(solution)/shard_map/ppermute | solution.py:25
  (385 shorter events, 120.4 us)
Async XLA Ops:
  2.2 49.6 %collective-permute-start = (f32[2,32,1,768]{3,2,1,0:T(1,128)S(1)}, f32[2,32,1,768]{3,2,1,0:T(1,128)S(1)}, u32[]{:S(2)}, u32[]{:S(2)}) collective-permute-start(f32[2,32,1,768]{3,2,1,0:T(1,128)S(1)} %get-tuple-element.102), channel_id=1, source_target_pairs={{0,2},{2,4},{4,6},{6,8},{8,10},{10,12},{12,14},{14,16},{16,18},{18... | collective-permute-start | bytes 589832 | tf_op jit(solution)/shard_map/ppermute | solution.py:22
  4.1 47.7 %collective-permute-start.1 = (f32[2,32,1,768]{3,2,1,0:T(1,128)S(1)}, f32[2,32,1,768]{3,2,1,0:T(1,128)S(1)}, u32[]{:S(2)}, u32[]{:S(2)}) collective-permute-start(f32[2,32,1,768]{3,2,1,0:T(1,128)S(1)} %get-tuple-element.103), channel_id=1, source_target_pairs={{2,0},{4,2},{6,4},{8,6},{10,8},{12,10},{14,12},{16,14},{18,16},{20... | collective-permute-start | bytes 589832 | tf_op jit(solution)/shard_map/ppermute | solution.py:25
  20.5 31.2 %collective-permute-start.11 = (f32[2,1,3072]{2,0,1:T(2,128)S(1)}, f32[2,1,3072]{2,0,1:T(2,128)S(1)}, u32[]{:S(2)}, u32[]{:S(2)}) collective-permute-start(f32[2,1,3072]{2,0,1:T(2,128)S(1)} %copy.535), channel_id=1, source_target_pairs={{0,2},{2,4},{4,6},{6,8},{8,10},{10,12},{12,14},{14,16},{16,18},{18... | collective-permute-start | bytes 73736 | tf_op jit(solution)/shard_map/ppermute | solution.py:22
  23.4 23.2 %collective-permute-start.8 = (s32[1,3072]{1,0:T(1,128)S(1)}, s32[1,3072]{1,0:T(1,128)S(1)}, u32[]{:S(2)}, u32[]{:S(2)}) collective-permute-start(s32[1,3072]{1,0:T(1,128)S(1)} %get-tuple-element.158), channel_id=1, source_target_pairs={{0,2},{2,4},{4,6},{6,8},{8,10},{10,12},{12,14},{14,16},{16,18},{18... | collective-permute-start | bytes 36872 | tf_op jit(solution)/shard_map/ppermute | solution.py:22
  26.4 14.5 %collective-permute-start.52 = (f32[256]{0:T(256)S(1)}, f32[256]{0:T(256)S(1)}, u32[]{:S(2)}, u32[]{:S(2)}) collective-permute-start(f32[256]{0:T(256)S(1)} %slice.831), channel_id=1, source_target_pairs={{0,2},{2,4},{4,6},{6,8},{8,10},{10,12},{12,14},{14,16},{16,18},{18... | collective-permute-start | bytes 3080 | tf_op jit(solution)/shard_map/ppermute | solution.py:14
  49.0 125.1 %collective-permute-start.53 = (f32[256]{0:T(256)}, f32[256]{0:T(256)}, u32[]{:S(2)}, u32[]{:S(2)}) collective-permute-start(f32[256]{0:T(256)} %slice.833), channel_id=1, source_target_pairs={{0,2},{2,4},{4,6},{6,8},{8,10},{10,12},{12,14},{14,16},{16,18},{18... | collective-permute-start | bytes 3080 | tf_op jit(solution)/shard_map/ppermute | solution.py:14
  52.2 45.3 %collective-permute-start.2 = (f32[2,32,4,1]{3,2,1,0:T(4,128)S(1)}, f32[2,32,4,1]{3,2,1,0:T(4,128)S(1)}, u32[]{:S(2)}, u32[]{:S(2)}) collective-permute-start(f32[2,32,4,1]{3,2,1,0:T(4,128)S(1)} %get-tuple-element.94), channel_id=1, source_target_pairs={{0,1},{2,3},{4,5},{6,7},{8,9},{10,11},{12,13},{14,15},{16,17},{18,... | collective-permute-start | bytes 3080 | tf_op jit(solution)/shard_map/ppermute | solution.py:22
  65.9 31.6 %collective-permute-start.3 = (f32[2,32,4,1]{3,2,1,0:T(4,128)S(1)}, f32[2,32,4,1]{3,2,1,0:T(4,128)S(1)}, u32[]{:S(2)}, u32[]{:S(2)}) collective-permute-start(f32[2,32,4,1]{3,2,1,0:T(4,128)S(1)} %get-tuple-element.95), channel_id=1, source_target_pairs={{1,0},{3,2},{5,4},{7,6},{9,8},{11,10},{13,12},{15,14},{17,16},{19,... | collective-permute-start | bytes 3080 | tf_op jit(solution)/shard_map/ppermute | solution.py:25
  67.2 14.6 %collective-permute-start.13 = (f32[2,10,1]{2,0,1:T(2,128)S(1)}, f32[2,10,1]{2,0,1:T(2,128)S(1)}, u32[]{:S(2)}, u32[]{:S(2)}) collective-permute-start(f32[2,10,1]{2,0,1:T(2,128)S(1)} %get-tuple-element.135), channel_id=1, source_target_pairs={{0,1},{2,3},{4,5},{6,7},{8,9},{10,11},{12,13},{14,15},{16,17},{18,... | collective-permute-start | bytes 248 | tf_op jit(solution)/shard_map/ppermute | solution.py:22
  80.5 15.2 %collective-permute-start.14 = (f32[2,10,1]{2,0,1:T(2,128)S(1)}, f32[2,10,1]{2,0,1:T(2,128)S(1)}, u32[]{:S(2)}, u32[]{:S(2)}) collective-permute-start(f32[2,10,1]{2,0,1:T(2,128)S(1)} %get-tuple-element.134), channel_id=1, source_target_pairs={{1,0},{3,2},{5,4},{7,6},{9,8},{11,10},{13,12},{15,14},{17,16},{19,... | collective-permute-start | bytes 248 | tf_op jit(solution)/shard_map/ppermute | solution.py:25
  81.9 73.8 %collective-permute-start.10 = (s32[10,1]{1,0:T(8,128)}, s32[10,1]{1,0:T(8,128)}, u32[]{:S(2)}, u32[]{:S(2)}) collective-permute-start(s32[10,1]{1,0:T(8,128)} %get-tuple-element.153), channel_id=1, source_target_pairs={{0,1},{2,3},{4,5},{6,7},{8,9},{10,11},{12,13},{14,15},{16,17},{18,... | collective-permute-start | bytes 128 | tf_op jit(solution)/shard_map/ppermute | solution.py:22
  95.7 60.0 %collective-permute-start.15 = (s32[10,1]{1,0:T(8,128)}, s32[10,1]{1,0:T(8,128)}, u32[]{:S(2)}, u32[]{:S(2)}) collective-permute-start(s32[10,1]{1,0:T(8,128)} %get-tuple-element.152), channel_id=1, source_target_pairs={{1,0},{3,2},{5,4},{7,6},{9,8},{11,10},{13,12},{15,14},{17,16},{19,... | collective-permute-start | bytes 128 | tf_op jit(solution)/shard_map/ppermute | solution.py:25
  101.3 16.7 %collective-permute-start.4 = (f32[2,32,1,768]{3,2,1,0:T(1,128)S(1)}, f32[2,32,1,768]{3,2,1,0:T(1,128)S(1)}, u32[]{:S(2)}, u32[]{:S(2)}) collective-permute-start(f32[2,32,1,768]{3,2,1,0:T(1,128)S(1)} %get-tuple-element.100), channel_id=1, source_target_pairs={{0,2},{2,4},{4,6},{6,8},{8,10},{10,12},{12,14},{14,16},{16,18},{18... | collective-permute-start | bytes 589832 | tf_op jit(solution)/shard_map/ppermute | solution.py:22
  103.3 19.0 %collective-permute-start.5 = (f32[2,32,1,768]{3,2,1,0:T(1,128)S(1)}, f32[2,32,1,768]{3,2,1,0:T(1,128)S(1)}, u32[]{:S(2)}, u32[]{:S(2)}) collective-permute-start(f32[2,32,1,768]{3,2,1,0:T(1,128)S(1)} %get-tuple-element.101), channel_id=1, source_target_pairs={{2,0},{4,2},{6,4},{8,6},{10,8},{12,10},{14,12},{16,14},{18,16},{20... | collective-permute-start | bytes 589832 | tf_op jit(solution)/shard_map/ppermute | solution.py:25
  122.6 15.5 %collective-permute-start.6 = (f32[2,32,4,1]{3,2,1,0:T(4,128)S(1)}, f32[2,32,4,1]{3,2,1,0:T(4,128)S(1)}, u32[]{:S(2)}, u32[]{:S(2)}) collective-permute-start(f32[2,32,4,1]{3,2,1,0:T(4,128)S(1)} %get-tuple-element.92), channel_id=1, source_target_pairs={{0,1},{2,3},{4,5},{6,7},{8,9},{10,11},{12,13},{14,15},{16,17},{18,... | collective-permute-start | bytes 3080 | tf_op jit(solution)/shard_map/ppermute | solution.py:22
  135.6 15.6 %collective-permute-start.7 = (f32[2,32,4,1]{3,2,1,0:T(4,128)S(1)}, f32[2,32,4,1]{3,2,1,0:T(4,128)S(1)}, u32[]{:S(2)}, u32[]{:S(2)}) collective-permute-start(f32[2,32,4,1]{3,2,1,0:T(4,128)S(1)} %get-tuple-element.93), channel_id=1, source_target_pairs={{1,0},{3,2},{5,4},{7,6},{9,8},{11,10},{13,12},{15,14},{17,16},{19,... | collective-permute-start | bytes 3080 | tf_op jit(solution)/shard_map/ppermute | solution.py:25
  157.1 20.6 %collective-permute-start.16 = (f32[2,1,3072]{2,0,1:T(2,128)S(1)}, f32[2,1,3072]{2,0,1:T(2,128)S(1)}, u32[]{:S(2)}, u32[]{:S(2)}) collective-permute-start(f32[2,1,3072]{2,0,1:T(2,128)S(1)} %copy.540), channel_id=1, source_target_pairs={{0,2},{2,4},{4,6},{6,8},{8,10},{10,12},{12,14},{14,16},{16,18},{18... | collective-permute-start | bytes 73736 | tf_op jit(solution)/shard_map/ppermute | solution.py:22
  159.1 18.9 %collective-permute-start.17 = (f32[2,1,3072]{2,0,1:T(2,128)S(1)}, f32[2,1,3072]{2,0,1:T(2,128)S(1)}, u32[]{:S(2)}, u32[]{:S(2)}) collective-permute-start(f32[2,1,3072]{2,0,1:T(2,128)S(1)} %copy.541), channel_id=1, source_target_pairs={{2,0},{4,2},{6,4},{8,6},{10,8},{12,10},{14,12},{16,14},{18,16},{20... | collective-permute-start | bytes 73736 | tf_op jit(solution)/shard_map/ppermute | solution.py:25
  175.2 23.7 %collective-permute-start.54 = (f32[256]{0:T(256)S(1)}, f32[256]{0:T(256)S(1)}, u32[]{:S(2)}, u32[]{:S(2)}) collective-permute-start(f32[256]{0:T(256)S(1)} %slice.835), channel_id=1, source_target_pairs={{0,2},{2,4},{4,6},{6,8},{8,10},{10,12},{12,14},{14,16},{16,18},{18... | collective-permute-start | bytes 3080 | tf_op jit(solution)/shard_map/ppermute | solution.py:14
  179.5 14.3 %collective-permute-start.19 = (f32[2,10,1]{2,0,1:T(2,128)S(1)}, f32[2,10,1]{2,0,1:T(2,128)S(1)}, u32[]{:S(2)}, u32[]{:S(2)}) collective-permute-start(f32[2,10,1]{2,0,1:T(2,128)S(1)} %get-tuple-element.132), channel_id=1, source_target_pairs={{1,0},{3,2},{5,4},{7,6},{9,8},{11,10},{13,12},{15,14},{17,16},{19,... | collective-permute-start | bytes 248 | tf_op jit(solution)/shard_map/ppermute | solution.py:25
  196.7 17.7 %collective-permute-start.20 = (f32[2,1,3072]{2,0,1:T(2,128)S(1)}, f32[2,1,3072]{2,0,1:T(2,128)S(1)}, u32[]{:S(2)}, u32[]{:S(2)}) collective-permute-start(f32[2,1,3072]{2,0,1:T(2,128)S(1)} %copy.545), channel_id=1, source_target_pairs={{0,2},{2,4},{4,6},{6,8},{8,10},{10,12},{12,14},{14,16},{16,18},{18... | collective-permute-start | bytes 73736 | tf_op jit(solution)/shard_map/ppermute | solution.py:22
  199.2 37.1 %collective-permute-start.55 = (f32[256]{0:T(256)S(1)}, f32[256]{0:T(256)S(1)}, u32[]{:S(2)}, u32[]{:S(2)}) collective-permute-start(f32[256]{0:T(256)S(1)} %slice.837), channel_id=1, source_target_pairs={{0,2},{2,4},{4,6},{6,8},{8,10},{10,12},{12,14},{14,16},{16,18},{18... | collective-permute-start | bytes 3080 | tf_op jit(solution)/shard_map/ppermute | solution.py:14
  201.1 14.8 %collective-permute-start.21 = (f32[2,1,3072]{2,0,1:T(2,128)S(1)}, f32[2,1,3072]{2,0,1:T(2,128)S(1)}, u32[]{:S(2)}, u32[]{:S(2)}) collective-permute-start(f32[2,1,3072]{2,0,1:T(2,128)S(1)} %copy.546), channel_id=1, source_target_pairs={{2,0},{4,2},{6,4},{8,6},{10,8},{12,10},{14,12},{16,14},{18,16},{20... | collective-permute-start | bytes 73736 | tf_op jit(solution)/shard_map/ppermute | solution.py:25
  217.6 14.4 %collective-permute-start.23 = (f32[2,10,1]{2,0,1:T(2,128)S(1)}, f32[2,10,1]{2,0,1:T(2,128)S(1)}, u32[]{:S(2)}, u32[]{:S(2)}) collective-permute-start(f32[2,10,1]{2,0,1:T(2,128)S(1)} %get-tuple-element.130), channel_id=1, source_target_pairs={{1,0},{3,2},{5,4},{7,6},{9,8},{11,10},{13,12},{15,14},{17,16},{19,... | collective-permute-start | bytes 248 | tf_op jit(solution)/shard_map/ppermute | solution.py:25
  237.3 66.9 %collective-permute-start.56 = (f32[256]{0:T(256)}, f32[256]{0:T(256)}, u32[]{:S(2)}, u32[]{:S(2)}) collective-permute-start(f32[256]{0:T(256)} %slice.839), channel_id=1, source_target_pairs={{0,2},{2,4},{4,6},{6,8},{8,10},{10,12},{12,14},{14,16},{16,18},{18... | collective-permute-start | bytes 3080 | tf_op jit(solution)/shard_map/ppermute | solution.py:14
  239.8 39.0 %collective-permute-start.32 = (f32[2,1,3072]{2,0,1:T(2,128)}, f32[2,1,3072]{2,0,1:T(2,128)}, u32[]{:S(2)}, u32[]{:S(2)}) collective-permute-start(f32[2,1,3072]{2,0,1:T(2,128)} %copy.550), channel_id=1, source_target_pairs={{0,2},{2,4},{4,6},{6,8},{8,10},{10,12},{12,14},{14,16},{16,18},{18... | collective-permute-start | bytes 73736 | tf_op jit(solution)/shard_map/ppermute | solution.py:22
  242.4 38.3 %collective-permute-start.33 = (f32[2,1,3072]{2,0,1:T(2,128)}, f32[2,1,3072]{2,0,1:T(2,128)}, u32[]{:S(2)}, u32[]{:S(2)}) collective-permute-start(f32[2,1,3072]{2,0,1:T(2,128)} %copy.551), channel_id=1, source_target_pairs={{2,0},{4,2},{6,4},{8,6},{10,8},{12,10},{14,12},{16,14},{18,16},{20... | collective-permute-start | bytes 73736 | tf_op jit(solution)/shard_map/ppermute | solution.py:25
  263.6 57.7 %collective-permute-start.24 = (f32[2,32,1,768]{3,2,1,0:T(1,128)S(1)}, f32[2,32,1,768]{3,2,1,0:T(1,128)S(1)}, u32[]{:S(2)}, u32[]{:S(2)}) collective-permute-start(f32[2,32,1,768]{3,2,1,0:T(1,128)S(1)} %get-tuple-element.98), channel_id=1, source_target_pairs={{0,2},{2,4},{4,6},{6,8},{8,10},{10,12},{12,14},{14,16},{16,18},{18... | collective-permute-start | bytes 589832 | tf_op jit(solution)/shard_map/ppermute | solution.py:22
  265.5 55.8 %collective-permute-start.25 = (f32[2,32,1,768]{3,2,1,0:T(1,128)S(1)}, f32[2,32,1,768]{3,2,1,0:T(1,128)S(1)}, u32[]{:S(2)}, u32[]{:S(2)}) collective-permute-start(f32[2,32,1,768]{3,2,1,0:T(1,128)S(1)} %get-tuple-element.99), channel_id=1, source_target_pairs={{2,0},{4,2},{6,4},{8,6},{10,8},{12,10},{14,12},{16,14},{18,16},{20... | collective-permute-start | bytes 589832 | tf_op jit(solution)/shard_map/ppermute | solution.py:25
  283.1 15.4 %collective-permute-start.35 = (f32[2,10,1]{2,0,1:T(2,128)S(1)}, f32[2,10,1]{2,0,1:T(2,128)S(1)}, u32[]{:S(2)}, u32[]{:S(2)}) collective-permute-start(f32[2,10,1]{2,0,1:T(2,128)S(1)} %get-tuple-element.128), channel_id=1, source_target_pairs={{1,0},{3,2},{5,4},{7,6},{9,8},{11,10},{13,12},{15,14},{17,16},{19,... | collective-permute-start | bytes 248 | tf_op jit(solution)/shard_map/ppermute | solution.py:25
  302.3 18.8 %collective-permute-start.36 = (f32[2,1,3072]{2,0,1:T(2,128)S(1)}, f32[2,1,3072]{2,0,1:T(2,128)S(1)}, u32[]{:S(2)}, u32[]{:S(2)}) collective-permute-start(f32[2,1,3072]{2,0,1:T(2,128)S(1)} %copy.557), channel_id=1, source_target_pairs={{0,2},{2,4},{4,6},{6,8},{8,10},{10,12},{12,14},{14,16},{16,18},{18... | collective-permute-start | bytes 73736 | tf_op jit(solution)/shard_map/ppermute | solution.py:22
  305.9 95.0 %collective-permute-start.57 = (f32[256]{0:T(256)}, f32[256]{0:T(256)}, u32[]{:S(2)}, u32[]{:S(2)}) collective-permute-start(f32[256]{0:T(256)} %slice.841), channel_id=1, source_target_pairs={{0,2},{2,4},{4,6},{6,8},{8,10},{10,12},{12,14},{14,16},{16,18},{18... | collective-permute-start | bytes 3080 | tf_op jit(solution)/shard_map/ppermute | solution.py:14
  307.8 16.4 %collective-permute-start.37 = (f32[2,1,3072]{2,0,1:T(2,128)S(1)}, f32[2,1,3072]{2,0,1:T(2,128)S(1)}, u32[]{:S(2)}, u32[]{:S(2)}) collective-permute-start(f32[2,1,3072]{2,0,1:T(2,128)S(1)} %copy.558), channel_id=1, source_target_pairs={{2,0},{4,2},{6,4},{8,6},{10,8},{12,10},{14,12},{16,14},{18,16},{20... | collective-permute-start | bytes 73736 | tf_op jit(solution)/shard_map/ppermute | solution.py:25
  322.9 17.4 %collective-permute-start.27 = (f32[2,32,4,1]{3,2,1,0:T(4,128)S(1)}, f32[2,32,4,1]{3,2,1,0:T(4,128)S(1)}, u32[]{:S(2)}, u32[]{:S(2)}) collective-permute-start(f32[2,32,4,1]{3,2,1,0:T(4,128)S(1)} %get-tuple-element.91), channel_id=1, source_target_pairs={{1,0},{3,2},{5,4},{7,6},{9,8},{11,10},{13,12},{15,14},{17,16},{19,... | collective-permute-start | bytes 3080 | tf_op jit(solution)/shard_map/ppermute | solution.py:25
  344.2 31.5 %collective-permute-start.28 = (f32[2,32,1,768]{3,2,1,0:T(1,128)S(1)}, f32[2,32,1,768]{3,2,1,0:T(1,128)S(1)}, u32[]{:S(2)}, u32[]{:S(2)}) collective-permute-start(f32[2,32,1,768]{3,2,1,0:T(1,128)S(1)} %get-tuple-element.96), channel_id=1, source_target_pairs={{0,2},{2,4},{4,6},{6,8},{8,10},{10,12},{12,14},{14,16},{16,18},{18... | collective-permute-start | bytes 589832 | tf_op jit(solution)/shard_map/ppermute | solution.py:22
  346.1 29.6 %collective-permute-start.29 = (f32[2,32,1,768]{3,2,1,0:T(1,128)S(1)}, f32[2,32,1,768]{3,2,1,0:T(1,128)S(1)}, u32[]{:S(2)}, u32[]{:S(2)}) collective-permute-start(f32[2,32,1,768]{3,2,1,0:T(1,128)S(1)} %get-tuple-element.97), channel_id=1, source_target_pairs={{2,0},{4,2},{6,4},{8,6},{10,8},{12,10},{14,12},{16,14},{18,16},{20... | collective-permute-start | bytes 589832 | tf_op jit(solution)/shard_map/ppermute | solution.py:25
  360.9 14.3 %collective-permute-start.39 = (f32[2,10,1]{2,0,1:T(2,128)S(1)}, f32[2,10,1]{2,0,1:T(2,128)S(1)}, u32[]{:S(2)}, u32[]{:S(2)}) collective-permute-start(f32[2,10,1]{2,0,1:T(2,128)S(1)} %get-tuple-element.126), channel_id=1, source_target_pairs={{1,0},{3,2},{5,4},{7,6},{9,8},{11,10},{13,12},{15,14},{17,16},{19,... | collective-permute-start | bytes 248 | tf_op jit(solution)/shard_map/ppermute | solution.py:25
  377.7 15.6 %collective-permute-start.31 = (f32[2,32,4,1]{3,2,1,0:T(4,128)S(1)}, f32[2,32,4,1]{3,2,1,0:T(4,128)S(1)}, u32[]{:S(2)}, u32[]{:S(2)}) collective-permute-start(f32[2,32,4,1]{3,2,1,0:T(4,128)S(1)} %get-tuple-element.89), channel_id=1, source_target_pairs={{1,0},{3,2},{5,4},{7,6},{9,8},{11,10},{13,12},{15,14},{17,16},{19,... | collective-permute-start | bytes 3080 | tf_op jit(solution)/shard_map/ppermute | solution.py:25
  401.9 39.4 %collective-permute-start.58 = (f32[256]{0:T(256)S(1)}, f32[256]{0:T(256)S(1)}, u32[]{:S(2)}, u32[]{:S(2)}) collective-permute-start(f32[256]{0:T(256)S(1)} %slice.843), channel_id=1, source_target_pairs={{0,2},{2,4},{4,6},{6,8},{8,10},{10,12},{12,14},{14,16},{16,18},{18... | collective-permute-start | bytes 3080 | tf_op jit(solution)/shard_map/ppermute | solution.py:14
  403.9 15.3 %collective-permute-start.40 = (f32[2,1,3072]{2,0,1:T(2,128)S(1)}, f32[2,1,3072]{2,0,1:T(2,128)S(1)}, u32[]{:S(2)}, u32[]{:S(2)}) collective-permute-start(f32[2,1,3072]{2,0,1:T(2,128)S(1)} %copy.562), channel_id=1, source_target_pairs={{0,2},{2,4},{4,6},{6,8},{8,10},{10,12},{12,14},{14,16},{16,18},{18... | collective-permute-start | bytes 73736 | tf_op jit(solution)/shard_map/ppermute | solution.py:22
  405.9 14.8 %collective-permute-start.41 = (f32[2,1,3072]{2,0,1:T(2,128)S(1)}, f32[2,1,3072]{2,0,1:T(2,128)S(1)}, u32[]{:S(2)}, u32[]{:S(2)}) collective-permute-start(f32[2,1,3072]{2,0,1:T(2,128)S(1)} %copy.563), channel_id=1, source_target_pairs={{2,0},{4,2},{6,4},{8,6},{10,8},{12,10},{14,12},{16,14},{18,16},{20... | collective-permute-start | bytes 73736 | tf_op jit(solution)/shard_map/ppermute | solution.py:25
  422.2 14.3 %collective-permute-start.43 = (f32[2,10,1]{2,0,1:T(2,128)S(1)}, f32[2,10,1]{2,0,1:T(2,128)S(1)}, u32[]{:S(2)}, u32[]{:S(2)}) collective-permute-start(f32[2,10,1]{2,0,1:T(2,128)S(1)} %get-tuple-element.124), channel_id=1, source_target_pairs={{1,0},{3,2},{5,4},{7,6},{9,8},{11,10},{13,12},{15,14},{17,16},{19,... | collective-permute-start | bytes 248 | tf_op jit(solution)/shard_map/ppermute | solution.py:25
  439.4 18.1 %collective-permute-start.44 = (f32[2,1,3072]{2,0,1:T(2,128)S(1)}, f32[2,1,3072]{2,0,1:T(2,128)S(1)}, u32[]{:S(2)}, u32[]{:S(2)}) collective-permute-start(f32[2,1,3072]{2,0,1:T(2,128)S(1)} %copy.567), channel_id=1, source_target_pairs={{0,2},{2,4},{4,6},{6,8},{8,10},{10,12},{12,14},{14,16},{16,18},{18... | collective-permute-start | bytes 73736 | tf_op jit(solution)/shard_map/ppermute | solution.py:22
  442.3 60.8 %collective-permute-start.59 = (f32[256]{0:T(256)}, f32[256]{0:T(256)}, u32[]{:S(2)}, u32[]{:S(2)}) collective-permute-start(f32[256]{0:T(256)} %slice.845), channel_id=1, source_target_pairs={{0,2},{2,4},{4,6},{6,8},{8,10},{10,12},{12,14},{14,16},{16,18},{18... | collective-permute-start | bytes 3080 | tf_op jit(solution)/shard_map/ppermute | solution.py:14
  444.3 14.8 %collective-permute-start.45 = (f32[2,1,3072]{2,0,1:T(2,128)S(1)}, f32[2,1,3072]{2,0,1:T(2,128)S(1)}, u32[]{:S(2)}, u32[]{:S(2)}) collective-permute-start(f32[2,1,3072]{2,0,1:T(2,128)S(1)} %copy.568), channel_id=1, source_target_pairs={{2,0},{4,2},{6,4},{8,6},{10,8},{12,10},{14,12},{16,14},{18,16},{20... | collective-permute-start | bytes 73736 | tf_op jit(solution)/shard_map/ppermute | solution.py:25
  460.8 14.3 %collective-permute-start.47 = (f32[2,10,1]{2,0,1:T(2,128)S(1)}, f32[2,10,1]{2,0,1:T(2,128)S(1)}, u32[]{:S(2)}, u32[]{:S(2)}) collective-permute-start(f32[2,10,1]{2,0,1:T(2,128)S(1)} %get-tuple-element.122), channel_id=1, source_target_pairs={{1,0},{3,2},{5,4},{7,6},{9,8},{11,10},{13,12},{15,14},{17,16},{19,... | collective-permute-start | bytes 248 | tf_op jit(solution)/shard_map/ppermute | solution.py:25
  478.2 26.3 %collective-permute-start.48 = (f32[2,1,3072]{2,0,1:T(2,128)}, f32[2,1,3072]{2,0,1:T(2,128)}, u32[]{:S(2)}, u32[]{:S(2)}) collective-permute-start(f32[2,1,3072]{2,0,1:T(2,128)} %copy.572), channel_id=1, source_target_pairs={{0,2},{2,4},{4,6},{6,8},{8,10},{10,12},{12,14},{14,16},{16,18},{18... | collective-permute-start | bytes 73736 | tf_op jit(solution)/shard_map/ppermute | solution.py:22
  480.7 25.6 %collective-permute-start.49 = (f32[2,1,3072]{2,0,1:T(2,128)}, f32[2,1,3072]{2,0,1:T(2,128)}, u32[]{:S(2)}, u32[]{:S(2)}) collective-permute-start(f32[2,1,3072]{2,0,1:T(2,128)} %copy.573), channel_id=1, source_target_pairs={{2,0},{4,2},{6,4},{8,6},{10,8},{12,10},{14,12},{16,14},{18,16},{20... | collective-permute-start | bytes 73736 | tf_op jit(solution)/shard_map/ppermute | solution.py:25
  (72 other events, 2375.2 us)
where the time goes:
time: 527 us; the launch traced here: 525 us
  starting transfers between devices  280 us (53%)
  waiting for transfers between devices  154 us (29%)
  local copies, waits for them, and re-layouts  48.9 us (9%)
  other arithmetic  35.4 us (7%)
    ppermute x26, starting transfers between devices, padded_2(): lax.ppermute(lax.slice_in_dim(block, 0, width, axis=dim), axis, backward)  172 us
    ppermute x26, waiting for transfers between devices, padded_2(): lax.ppermute(lax.slice_in_dim(block, 0, width, axis=dim), axis, backward)  140 us
    ppermute x26, starting transfers between devices, padded_2(): lax.ppermute(lax.slice_in_dim(block, block.shape[dim] - width, None, axis...  92.5 us
    ppermute x8, starting transfers between devices, shifted(): lax.ppermute(value, axis, [(source, source + steps) for source in range(f...  15.3 us
    sub x4, other arithmetic, advance(): centre + kd_region * lap - 0.5 * u_wind[:, None, None] * (east - west)  14.1 us
    gather x8, local copies, waits for them, and re-layouts, shards(): lateral = 0.1 * depth.reshape(-1)[link_cell]  13.9 us
  transfers between devices with their start and end apart: 60, of which 27 were waited for; matrix products, arithmetic and copies ran while one was open for 15% of the time, Pallas kernels for 0%

commit v1 on v0

v1 whole, which is shorter than its diff:
```python
import jax
import jax.numpy as jnp
from jax import lax
from jax.experimental import pallas as pl
from jax.experimental.pallas import tpu as pltpu
from jax.sharding import PartitionSpec as P

ASTEPS = 2
HSTEPS = 4
COUPLE = 2
STEPS = HSTEPS * COUPLE

F32 = jnp.float32
BF16 = jnp.bfloat16
AXES = ("grp", "gx", "gy")
PARAMS = pltpu.CompilerParams(vmem_limit_bytes=48 * 1024 * 1024)

LINKS = 256
TR = 8
TC = 3072
TW = TC + 128
AC = 768
AW = AC + 128
FL = 64
Q0 = 32


def exchange(value, partner):
    pairs = []
    for r in range(256):
        for g in range(2):
            t, h = partner(r, g)
            if 0 <= t < 256:
                pairs.append((r * 2 + g, t * 2 + h))
    return lax.ppermute(value, AXES, pairs)


def outer(r):
    return r + 1 if r % 2 else r - 1


def pair_swap(value):
    return exchange(value, lambda r, g: (r ^ 1, g))


def chip_swap(value):
    return exchange(value, lambda r, g: (outer(r), g))


def near_swap(value):
    return exchange(
        value, lambda r, g: (outer(r), g if outer(r) // 16 == r // 16 else 1 - g)
    )


def gy_swap(value):
    return exchange(value, lambda r, g: (r, 1 - g))


def grp_shift(value):
    return exchange(value, lambda r, g: (r + 16, g))


def vmem():
    return pl.BlockSpec(memory_space=pltpu.VMEM)


def smem():
    return pl.BlockSpec(memory_space=pltpu.SMEM)


def call(body, out_shapes, scalars, arrays, scratch=()):
    return pl.pallas_call(
        body,
        out_shape=[jax.ShapeDtypeStruct(s, F32) for s in out_shapes],
        in_specs=[smem()] * len(scalars) + [vmem()] * len(arrays),
        out_specs=[vmem() for _ in out_shapes],
        scratch_shapes=[pltpu.VMEM(s, F32) for s in scratch],
        compiler_params=PARAMS,
    )(*scalars, *arrays)


def pack_body(info, air, kd, elev, cond, rf, mask, code, depth, soil, airc, msg_in, msg_out, strip):
    odd = info[0] == 1
    right = info[1] == 1
    for r in range(2):
        airc[r] = air[:, r, :]
    msg_in[...] = jnp.zeros((32, TC), F32)
    msg_out[...] = jnp.zeros((24, TC), F32)
    for ref, off, n in (
        (elev, 0, 4),
        (code, 4, 4),
        (depth, 8, 4),
        (cond, 12, 3),
        (rf, 15, 3),
        (mask, 18, 3),
    ):
        top = ref[0:n, :].astype(F32)
        low = ref[TR - n : TR, :].astype(F32)
        msg_in[off : off + n, :] = jnp.where(odd, top, low)
        msg_out[off : off + n, :] = jnp.where(odd, low, top)
    for msg in (msg_in, msg_out):
        for r in range(2):
            msg[21:22, r * AC : (r + 1) * AC] = airc[r, Q0 : Q0 + 1, :]
            msg[21:22, (2 + r) * AC : (3 + r) * AC] = airc[r, 0:1, :]
            msg[22:23, r * AC : (r + 1) * AC] = kd[r : r + 1, :]
    blocks = []
    for ref in (elev, cond, rf, mask, code, depth, soil):
        blocks.append(jnp.where(right, ref[:, 0:128], ref[:, TC - 128 : TC]).astype(F32))
    kblock = jnp.where(right, kd[:, 0:128], kd[:, AC - 128 : AC])
    square = jnp.concatenate(blocks + [kblock, jnp.zeros((70, 128), F32)], axis=0).T
    strip[0:16, :] = jnp.where(right, square[0:16], square[112:128])
    ablock = jnp.concatenate(
        [jnp.where(right, airc[r, :, 0:128], airc[r, :, AC - 128 : AC]) for r in range(2)], axis=0
    ).T
    strip[16:24, :] = jnp.where(right, ablock[0:8], ablock[120:128])
    for b in range(3):
        msg_in[24:32, b * 128 : (b + 1) * 128] = strip[8 * b : 8 * b + 8, :]


def land_strip(strip, right):
    zero = jnp.zeros((112, 128), F32)
    s = strip[0:16, :]
    return jnp.where(
        right, jnp.concatenate([zero, s], axis=0), jnp.concatenate([s, zero], axis=0)
    ).T


def air_strip(strip, right):
    zero = jnp.zeros((120, 128), F32)
    s = strip[16:24, :]
    return jnp.where(
        right, jnp.concatenate([zero, s], axis=0), jnp.concatenate([s, zero], axis=0)
    ).T


def lanes_inside(right, rows):
    lane = lax.broadcasted_iota(jnp.int32, (rows, AW), 1)
    edge = jnp.where(right, AW - 8, AC)
    halo = (lane >= edge) & (lane < edge + 8)
    return jnp.where((lane < AC) | halo, 1.0, 0.0).astype(F32)


def ring_mask(r, right):
    row = lax.broadcasted_iota(jnp.int32, (8, AW), 0)
    place = jnp.where(row < 5, r * 2 + row, r * 2 + row - 8)
    return jnp.where((place >= 0) & (place < 512), lanes_inside(right, 8), 0.0)


def ring_step(x, k, m, hu, hv):
    n = pltpu.roll(x, 1, 0)
    s = pltpu.roll(x, 7, 0)
    w = pltpu.roll(x, 1, 1)
    e = pltpu.roll(x, AW - 1, 1)
    return m * (x + k * (n + s + w + e - 4.0 * x) - hu * (e - w) - hv * (s - n))


def spread_matrix():
    i = lax.broadcasted_iota(jnp.int32, (128, 512), 0)
    j = lax.broadcasted_iota(jnp.int32, (128, 512), 1)
    return jnp.where(j // 4 == i, 1.0, 0.0).astype(BF16)


def two_parts(x):
    high = x.astype(BF16)
    low = (x - high.astype(F32)).astype(BF16)
    return jnp.concatenate([high, low], axis=0)


def spread_columns(rain, right):
    blocks = jnp.concatenate([rain[:, 128 * b : 128 * b + 128] for b in range(7)], axis=0)
    wide = jnp.dot(two_parts(blocks), spread_matrix(), preferred_element_type=F32)
    wide = wide[0:56] + wide[56:112]
    parts = [wide[8 * b : 8 * b + 8] for b in range(6)]
    last = wide[48:56]
    parts.append(jnp.where(right, last[:, 384:512], last[:, 0:128]))
    return jnp.concatenate(parts, axis=1)


def spread_rows(wide):
    row = lax.broadcasted_iota(jnp.int32, (8, TW), 0)
    own = jnp.where(row < 4, wide[0:1, :], wide[1:2, :])
    halo = jnp.where(row < 4, wide[2:3, :], wide[7:8, :])
    return jnp.concatenate([own, halo], axis=0)


def soil_mean(soil, right):
    zero = jnp.zeros((8, 384), F32)
    last = soil[:, TC:TW]
    last = jnp.where(
        right,
        jnp.concatenate([zero, last], axis=1),
        jnp.concatenate([last, zero], axis=1),
    )
    blocks = jnp.concatenate([soil[:, 512 * b : 512 * b + 512] for b in range(6)] + [last], axis=0)
    sums = lax.dot_general(
        two_parts(blocks),
        spread_matrix(),
        (((1,), (1,)), ((), ())),
        preferred_element_type=F32,
    )
    sums = sums[0:56] + sums[56:112]
    wide = jnp.concatenate([sums[8 * b : 8 * b + 8] for b in range(7)], axis=1)
    wide = wide + pltpu.roll(wide, 7, 0)
    wide = wide + pltpu.roll(wide, 6, 0)
    row = lax.broadcasted_iota(jnp.int32, (8, AW), 0)
    return jnp.where(row == 0, wide[0:1, :], jnp.where(row == 1, wide[4:5, :], 0.0)) * 0.0625


def lateral_of(depth, cells):
    row = lax.broadcasted_iota(jnp.int32, (8, 128), 0) * (TC // 128)
    out = []
    for h in range(2):
        cell = cells[h : h + 1, :]
        lane = jnp.broadcast_to(cell % 128, (8, 128))
        block = jnp.broadcast_to(cell // 128, (8, 128)) - row
        total = jnp.zeros((8, 128), F32)
        for b in range(TC // 128):
            got = jnp.take_along_axis(depth[:, 128 * b : 128 * b + 128], lane, axis=1)
            total = jnp.where(block == b, got, total)
        out.append(0.1 * jnp.sum(total, axis=0, keepdims=True))
    return jnp.concatenate(out, axis=1)


def hydro(coef, rq, ring, land, soil, cells, lat):
    for t in range(HSTEPS):
        d = ring[...]
        lat[t : t + 1, :] = lateral_of(ring[0:8, 0:TC], cells)
        soil[...] = soil[...] + 0.05 * land[...] * d[0:8] - 0.02 * soil[...]
        new = rq[...] + coef[0] * d
        new = new + coef[1] * pltpu.roll(d, 1, 1)
        new = new + coef[2] * pltpu.roll(d, TW - 1, 1)
        new = new + coef[3] * pltpu.roll(d, 1, 0)
        new = new + coef[4] * pltpu.roll(d, 15, 0)
        ring[...] = new


def rain_of(q):
    rain = 0.05 * q * q
    return rain, q - rain


def send_edges(odd, ring, q, t, msg_in, msg_out):
    top = ring[0:4, :]
    low = ring[4:8, :]
    for msg in (msg_in, msg_out):
        msg[4:8, :] = jnp.zeros((4, TW), F32)
        msg[4:5, 0:AW] = q[0:1]
        msg[4:5, AW : 2 * AW] = q[1:2]
        msg[4:5, 2 * AW : 3 * AW] = t[0:1]
        msg[5:6, 0:AW] = t[1:2]
    msg_in[0:4, :] = jnp.where(odd, top, low)
    msg_out[0:4, :] = jnp.where(odd, low, top)


def first_body(
    info, u, v, cells, own_msg, elev, cond, rf, mask, code, depth, soil0,
    pin, out, far, own_strip, pair_strip, out_strip, far_strip,
    coef, rain_w, static_w, land, ring, soil, lat, q_out, t_out, k_out, msg_in, msg_out,
    grid, rq, q8, t8, k8,
):
    odd = info[0] == 1
    right = info[1] == 1
    r = info[2]
    hu_t, hv_t = 0.5 * u[0], 0.5 * v[0]
    mine = land_strip(own_strip, right)
    pair = land_strip(pair_strip, right)
    beyond = land_strip(out_strip, right)
    north_strip = jnp.where(odd, pair, beyond)
    south_strip = jnp.where(odd, beyond, pair)
    grid[...] = jnp.zeros_like(grid)
    for a, (ref, off, n, block) in enumerate(
        (
            (elev, 0, 4, 0),
            (cond, 12, 3, 1),
            (rf, 15, 3, 2),
            (mask, 18, 3, 3),
            (code, 4, 4, 4),
            (depth, 8, 4, 5),
        )
    ):
        grid[a, 0:8, 0:TC] = ref[...].astype(F32)
        grid[a, 0:8, TC:TW] = mine[8 * block : 8 * block + 8]
        e_in = pin[off : off + n, :]
        e_out = out[off : off + n, :]
        grid[a, 8 : 8 + n, 0:TC] = jnp.where(odd, e_out, e_in)
        grid[a, 16 - n : 16, 0:TC] = jnp.where(odd, e_in, e_out)
        grid[a, 8 : 8 + n, TC:TW] = south_strip[8 * block : 8 * block + n]
        grid[a, 16 - n : 16, TC:TW] = north_strip[8 * block + 8 - n : 8 * block + 8]
    land[...] = grid[3, 0:8, :]
    soil[:, 0:TC] = soil0[...]
    soil[:, TC:TW] = mine[48:56]
    m = grid[3]
    eta = grid[0]
    lap = (
        pltpu.roll(eta, 1, 1)
        + pltpu.roll(eta, TW - 1, 1)
        + pltpu.roll(eta, 1, 0)
        + pltpu.roll(eta, 15, 0)
        - 4.0 * eta
    )
    mc = m * grid[1]
    codes = grid[4]
    share = 0.2 * m
    coef[0] = 0.75 * m - 4.0 * mc
    coef[1] = mc + jnp.where(pltpu.roll(codes, 1, 1) == 0.0, share, 0.0)
    coef[2] = mc + jnp.where(pltpu.roll(codes, TW - 1, 1) == 2.0, share, 0.0)
    coef[3] = mc + jnp.where(pltpu.roll(codes, 1, 0) == 3.0, share, 0.0)
    coef[4] = mc + jnp.where(pltpu.roll(codes, 15, 0) == 1.0, share, 0.0)
    rain_w[...] = m * grid[2]
    static_w[...] = mc * lap
    ring[...] = grid[5]
    air_mine = air_strip(own_strip, right)
    air_pair = air_strip(pair_strip, right)
    air_out = air_strip(out_strip, right)
    air_far = air_strip(far_strip, right)
    out2_strip = out_strip[24:48, :]
    air_out2 = air_strip(out2_strip, right)
    air_north = jnp.where(odd, air_pair, air_out)
    air_south = jnp.where(odd, air_out, air_pair)
    third_north = jnp.where(odd, air_far, air_out2)
    third_south = jnp.where(odd, air_out2, air_far)
    north = jnp.where(odd, pin[16:24, :], out[16:24, :])
    south = jnp.where(odd, out[16:24, :], pin[16:24, :])
    for ref in (q8, t8, k8):
        ref[...] = jnp.zeros_like(ref)
    for i in range(2):
        for place, msg, strip, cols in (
            (i, own_msg[16:24, :], air_mine, mine),
            (2 + i, south, air_south, south_strip),
            (6 + i, north, air_north, north_strip),
        ):
            q8[place : place + 1, 0:AC] = msg[5:6, i * AC : (i + 1) * AC]
            t8[place : place + 1, 0:AC] = msg[5:6, (2 + i) * AC : (3 + i) * AC]
            k8[place : place + 1, 0:AC] = msg[6:7, i * AC : (i + 1) * AC]
            q8[place : place + 1, AC:AW] = strip[i * FL + Q0 : i * FL + Q0 + 1]
            t8[place : place + 1, AC:AW] = strip[i * FL : i * FL + 1]
            k8[place : place + 1, AC:AW] = cols[56 + i : 57 + i]
    beyond_q = out[22:23, 2 * AC : 3 * AC]
    far_q = jnp.where(odd, far[21:22, AC : 2 * AC], far[21:22, 0:AC])
    q8[4:5, 0:AC] = jnp.where(odd, beyond_q, far_q)
    q8[5:6, 0:AC] = jnp.where(odd, far_q, beyond_q)
    q8[4:5, AC:AW] = third_south[Q0 : Q0 + 1]
    q8[5:6, AC:AW] = third_north[FL + Q0 : FL + Q0 + 1]
    m8 = ring_mask(r, right)
    k = k8[...]
    k_out[...] = k
    q, t = q8[...], t8[...]
    for _ in range(ASTEPS):
        q = ring_step(q, k, m8, hu_t, hv_t)
        t = ring_step(t, k, m8, hu_t, hv_t)
    rain, q = rain_of(q)
    rq[...] = static_w[...] + rain_w[...] * spread_rows(spread_columns(rain, right))
    hydro(coef, rq, ring, land, soil, cells[...], lat)
    coarse = soil_mean(soil[...], right)
    q = q + 0.1 * coarse * jax.nn.sigmoid(t)
    q_out[...] = q
    t_out[...] = t
    send_edges(odd, ring, q, t, msg_in, msg_out)


def second_body(
    info, u, v, cells, coef, rain_w, static_w, land, ring0, soil0, q0, t0, k0, pin, out, far,
    depth_out, coarse_out, q_out, lat,
    ring, soil, rq, q8, t8,
):
    odd = info[0] == 1
    right = info[1] == 1
    r = info[2]
    hu_t, hv_t = 0.5 * u[0], 0.5 * v[0]
    ring[0:8, :] = ring0[0:8, :]
    ring[8:12, :] = jnp.where(odd, out[0:4, :], pin[0:4, :])
    ring[12:16, :] = jnp.where(odd, pin[0:4, :], out[0:4, :])
    soil[...] = soil0[...]
    north = jnp.where(odd, pin[...], out[...])
    south = jnp.where(odd, out[...], pin[...])
    t8[...] = jnp.zeros_like(t8)
    q8[0:2, :] = q0[0:2, :]
    t8[0:2, :] = t0[0:2, :]
    for place, msg in ((2, south), (6, north)):
        q8[place : place + 1, :] = msg[4:5, 0:AW]
        q8[place + 1 : place + 2, :] = msg[4:5, AW : 2 * AW]
        t8[place : place + 1, :] = msg[4:5, 2 * AW : 3 * AW]
        t8[place + 1 : place + 2, :] = msg[5:6, 0:AW]
    beyond_q = out[5:6, AW : 2 * AW]
    far_q = jnp.where(odd, far[4:5, AW : 2 * AW], far[4:5, 0:AW])
    q8[4:5, :] = jnp.where(odd, beyond_q, far_q)
    q8[5:6, :] = jnp.where(odd, far_q, beyond_q)
    m8 = ring_mask(r, right)
    k = k0[...]
    q, t = q8[...], t8[...]
    for _ in range(ASTEPS):
        q = ring_step(q, k, m8, hu_t, hv_t)
        t = ring_step(t, k, m8, hu_t, hv_t)
    rain, q = rain_of(q)
    rq[...] = static_w[...] + rain_w[...] * spread_rows(spread_columns(rain, right))
    hydro(coef, rq, ring, land, soil, cells[...], lat)
    coarse = soil_mean(soil[...], right)
    q = q + 0.1 * coarse * jax.nn.sigmoid(t)
    depth_out[...] = ring[0:8, 0:TC]
    coarse_out[...] = coarse[0:2, 0:AC]
    q_out[...] = q[0:2, 0:AC]


def air_body(
    info, u, v, own, pin, out, far, k8, kfar, own_strip, pair_strip, out_strip, far_strip, qf,
    air_out,
    strips,
):
    odd = info[0] == 1
    right = info[1] == 1
    r = info[2]
    for i, (ref, lo) in enumerate(
        ((own_strip, 0), (pair_strip, 0), (out_strip, 0), (out_strip, 24), (far_strip, 0))
    ):
        strips[i] = air_strip(ref[lo : lo + 24, :], right)
    lanes = lanes_inside(right, 1)
    masks = {}
    for row in range(-3, 5):
        place = r * 2 + row
        inside = jnp.where((place >= 0) & (place < 512), 1.0, 0.0)
        masks[row] = lanes * inside
    kd = {row: k8[row % 8 : row % 8 + 1, :] for row in (-2, -1, 0, 1, 2, 3)}
    kd[-3] = kfar[0:1, :]
    kd[4] = kfar[1:2, :]
    kd = {row: kd[row] * masks[row] for row in kd}

    def group(g, carry):
        at = pl.ds(pl.multiple_of(g * 8, 8), 8)

        def whole(main, strip, i):
            return jnp.concatenate(
                [main, strips[strip, pl.ds(pl.multiple_of(g * 8 + i * FL, 8), 8), :]], axis=1
            )

        x = {0: whole(own[0, at, :], 0, 0), 1: whole(own[1, at, :], 0, 1)}
        p = [whole(pin[i, at, :], 1, i) for i in range(2)]
        o = [whole(out[i, at, :], 2, i) for i in range(2)]
        o2 = [whole(out[2 + i, at, :], 3, i) for i in range(2)]
        f = [whole(far[i, at, :], 4, i) for i in range(2)]
        for i in range(2):
            x[2 + i] = jnp.where(odd, o[i], p[i])
            x[4 + i] = jnp.where(odd, o2[i], f[i])
            x[-2 + i] = jnp.where(odd, p[i], o[i])
            x[-4 + i] = jnp.where(odd, f[i], o2[i])
        hu = 0.5 * u[at, 0:1]
        hv = 0.5 * v[at, 0:1]
        for step in range(ASTEPS * COUPLE):
            new = {}
            for row in range(-3 + step, 5 - step):
                c, n, s = x[row], x[row - 1], x[row + 1]
                w = pltpu.roll(c, 1, 1)
                e = pltpu.roll(c, AW - 1, 1)
                new[row] = (
                    masks[row] * (c - hu * (e - w) - hv * (s - n))
                    + kd[row] * (n + s + w + e - 4.0 * c)
                )
            x = new
        for i in range(2):
            air_out[at, i, :] = x[i][:, 0:AC]
        return carry

    lax.fori_loop(0, FL // 8, group, 0)
    for i in range(2):
        air_out[Q0 : Q0 + 1, i, :] = qf[i : i + 1, :]


def route_body(info, own, got, flow_out, hot):
    j = info[3]
    target = lax.broadcasted_iota(jnp.int32, (2 * LINKS, LINKS), 0).astype(F32)

    def slot(k):
        if k == 0:
            return own[...]
        return got[lax.rem(j - k + 16, 16)]

    data = [slot(k) for k in range(STEPS + 1)]
    flow = [d[8:9, :] for d in data]
    for k in range(STEPS + 1):
        hot[k] = jnp.where(target == data[k][9:10, :], 1.0, 0.0).astype(BF16)
    for t in range(STEPS):
        routed = []
        for k in range(STEPS - t + 1):
            f = flow[k]
            f1 = f.astype(BF16)
            rest = f - f1.astype(F32)
            f2 = rest.astype(BF16)
            f3 = (rest - f2.astype(F32)).astype(BF16)
            lhs = jnp.concatenate([f1, f2, f3, jnp.zeros((13, LINKS), BF16)], axis=0)
            first = 0 if k < STEPS - t else LINKS
            last = 2 * LINKS if k > 0 else LINKS
            y = lax.dot_general(
                lhs,
                hot[k, first:last, :],
                (((1,), (1,)), ((), ())),
                preferred_element_type=F32,
            )
            y = y[0:1] + y[1:2] + y[2:3]
            local = None if first else y[:, 0:LINKS]
            down = y[:, LINKS - first :] if last > LINKS else None
            routed.append((local, down))
        new = []
        for k in range(STEPS - t):
            arrived = routed[k][0] + routed[k + 1][1]
            new.append(flow[k] + 0.5 * (arrived - flow[k]) + data[k][t : t + 1, :])
        flow = new
    flow_out[...] = flow[0]


def shards(
    air, kdiff, u_wind, v_wind, elev, cond, rain_factor, land_mask, flow_code,
    depth_init, soil_init, link_cell, link_down, link_flow,
):
    gx = lax.axis_index("gx")
    row = lax.axis_index("grp") * 16 + gx
    odd = gx % 2
    info = jnp.stack([odd, lax.axis_index("gy"), row, gx]).astype(jnp.int32)
    end = ((gx == 0) | (gx == 15)).astype(F32)
    cells = link_cell.reshape(2, 128)
    ulev = jnp.broadcast_to(jnp.tile(u_wind, 2)[:, None], (FL, 128))
    vlev = jnp.broadcast_to(jnp.tile(v_wind, 2)[:, None], (FL, 128))

    airc, msg_in, msg_out, strip = call(
        pack_body,
        [(2, FL, AC), (32, TC), (24, TC), (24, 128)],
        [info],
        [air.reshape(FL, 2, AC), kdiff, elev, cond, rain_factor, land_mask, flow_code, depth_init, soil_init],
    )
    pin = pair_swap(msg_in)
    pair_strip = jnp.concatenate([pin[24:32, 128 * b : 128 * b + 128] for b in range(3)], axis=0)
    near = near_swap(jnp.concatenate([strip, pair_strip], axis=0))
    nearest = jnp.where(
        odd == 1,
        jnp.concatenate([pin[21, AC : 2 * AC], pin[22, AC : 2 * AC]]),
        jnp.concatenate([pin[21, 0:AC], pin[22, 0:AC]]),
    )
    msg_out = msg_out.at[22, 2 * AC :].set(nearest)
    out = chip_swap(msg_out)
    across = gy_swap(jnp.concatenate([strip, pair_strip, near], axis=0))
    out_strip = jnp.where(end > 0, near, across[48:96])
    far = pair_swap(out)
    far_strip = pair_swap(out_strip)
    own_strip = across[0:24]
    pair_strip = across[24:48]

    air_pair = pair_swap(airc)
    air_near = chip_swap(jnp.concatenate([airc, air_pair], axis=0))
    air_far = pair_swap(air_near[0:2])

    wide = (16, TW)
    (coef, rain_w, static_w, land, ring, soil, lat_a, q, t, k8, msg_in, msg_out) = call(
        first_body,
        [(5, 16, TW), wide, wide, (8, TW), wide, (8, TW), (HSTEPS, LINKS), (8, AW), (8, AW), (8, AW), (8, TW), (8, TW)],
        [info, u_wind, v_wind],
        [cells, msg_out, elev, cond, rain_factor, land_mask, flow_code, depth_init, soil_init, pin, out, far,
         own_strip, pair_strip, out_strip, far_strip],
        [(6, 16, TW), wide, (8, AW), (8, AW), (8, AW)],
    )
    kfar_out = out[22, 3 * AC :]
    kfar_far = jnp.where(odd == 1, far[22, AC : 2 * AC], far[22, 0:AC])
    pinb = pair_swap(msg_in)
    nearest = jnp.where(odd == 1, pinb[4, AW : 2 * AW], pinb[4, 0:AW])
    outb = chip_swap(msg_out.at[5, AW : 2 * AW].set(nearest))
    farb = pair_swap(outb)
    depth, coarse, qf, lat_b = call(
        second_body,
        [(TR, TC), (2, AC), (2, AC), (HSTEPS, LINKS)],
        [info, u_wind, v_wind],
        [cells, coef, rain_w, static_w, land, ring, soil, q, t, k8, pinb, outb, farb],
        [wide, (8, TW), wide, (8, AW), (8, AW)],
    )

    own = jnp.concatenate(
        [lat_a, lat_b, link_flow[None], link_down.astype(F32)[None], jnp.zeros((6, LINKS), F32)]
    )
    before = grp_shift(own)
    later = (jnp.arange(16) > gx)[:, None, None]
    got = lax.all_to_all(jnp.where(later, own[None], before[None]), "gx", 0, 0)

    kn = jnp.where(odd == 1, kfar_far, kfar_out)
    ks = jnp.where(odd == 1, kfar_out, kfar_far)
    kfar = kfar_rows(kn, ks, out_strip, far_strip, odd, lax.axis_index("gy"))
    (air_new,) = call(
        air_body,
        [(FL, 2, AC)],
        [info],
        [ulev, vlev, airc, air_pair, air_near, air_far, k8, kfar, own_strip, pair_strip, out_strip, far_strip, qf],
        [(5, 128, 128)],
    )
    (flow,) = route_call(info, own, got)
    return (air_new.reshape(2, 32, 2, AC), depth, coarse, flow.reshape(LINKS))


def kfar_rows(kn, ks, out_strip, far_strip, odd, gy):
    strip_n = jnp.where(odd == 1, far_strip[0:16, 57], out_strip[24:40, 57])
    strip_s = jnp.where(odd == 1, out_strip[24:40, 56], far_strip[0:16, 56])
    zero = jnp.zeros((112,), F32)

    def place(s):
        return jnp.where(gy == 1, jnp.concatenate([zero, s]), jnp.concatenate([s, zero]))

    return jnp.stack([jnp.concatenate([kn, place(strip_n)]), jnp.concatenate([ks, place(strip_s)])])


def route_call(info, own, got):
    return pl.pallas_call(
        route_body,
        out_shape=[jax.ShapeDtypeStruct((1, LINKS), F32)],
        in_specs=[smem(), vmem(), vmem()],
        out_specs=[vmem()],
        scratch_shapes=[pltpu.VMEM((STEPS + 1, 2 * LINKS, LINKS), BF16)],
        compiler_params=PARAMS,
    )(info, own, got)


def solution(mesh):
    placed = (
        P(None, None, ("grp", "gx"), "gy"),
        P(("grp", "gx"), "gy"),
        P(),
        P(),
        P(("grp", "gx"), "gy"),
        P(("grp", "gx"), "gy"),
        P(("grp", "gx"), "gy"),
        P(("grp", "gx"), "gy"),
        P(("grp", "gx"), "gy"),
        P(("grp", "gx"), "gy"),
        P(("grp", "gx"), "gy"),
        P(AXES),
        P(AXES),
        P(AXES),
    )
    return jax.shard_map(
        shards,
        mesh=mesh,
        in_specs=placed,
        out_specs=(
            P(None, None, ("grp", "gx"), "gy"),
            P(("grp", "gx"), "gy"),
            P(("grp", "gx"), "gy"),
            P(AXES),
        ),
        check_vma=False,
    )
```

time: 527 us -> 133 us (0.25)
  the two profiles are of different devices: /device:TPU:6 before, /device:TPU:7 now
where the time goes in v1:
time: 133 us; the launch traced here: 130 us
  starting transfers between devices  77.2 us (58%)
  waiting for transfers between devices  17.9 us (13%)
  local copies, waits for them, and re-layouts  17.2 us (13%)
  Pallas kernels  14.7 us (11%)
  other arithmetic  2.17 us (2%)
    ppermute x13, starting transfers between devices, exchange(): return lax.ppermute(value, AXES, pairs)  67.4 us
    unnamed x91, local copies, waits for them, and re-layouts  15 us
    ppermute x13, waiting for transfers between devices, exchange(): return lax.ppermute(value, AXES, pairs)  12.5 us
    pallas_call x4, Pallas kernels, call(): pl.pallas_call(body, out_shape=[jax.ShapeDtypeStruct(s, F32) for s in out...  10.9 us
    all_to_all x1, starting transfers between devices, shards(): got = lax.all_to_all(jnp.where(later, own[None], before[None]), 'gx', 0, 0)  9.73 us
    all_to_all x1, waiting for transfers between devices, shards(): got = lax.all_to_all(jnp.where(later, own[None], before[None]), 'gx', 0, 0)  5.38 us
    pallas_call x1, Pallas kernels, route_call(): pl.pallas_call(route_body, out_shape=[jax.ShapeDtypeStruct((1, LINKS), F3...  3.81 us
  transfers between devices with their start and end apart: 14, of which 6 were waited for; matrix products, arithmetic and copies ran while one was open for 3% of the time, Pallas kernels for 6%

profile of v1, /device:TPU:7, one launch (start us, length us, event | category | flops | bytes accessed | tf_op | source)
XLA Modules:
  0.0 130.4 jit_solution(6893144850234188620)
XLA Ops:
  0.7 0.6 copy-done.32
  1.3 1.0 copy-done
  2.3 0.9 copy-done.1
  3.2 0.9 copy-done.3
  4.1 0.9 copy-done.5
  5.0 0.9 copy-done.7
  5.9 0.9 copy-done.9
  6.8 0.9 copy-done.11
  7.7 0.9 copy-done.13
  8.6 0.9 shard_map.165
  9.5 2.6 %collective-permute-start.3 = (f32[32,3072]{1,0:T(8,128)S(1)}, f32[32,3072]{1,0:T(8,128)S(1)}, u32[]{:S(2)}, u32[]{:S(2)}) collective-permute-start(f32[32,3072]{1,0:T(8,128)S(1)} %get-tuple-element.50), channel_id=1, source_target_pairs={{0,2},{1,3},{2,0},{3,1},{4,6},{5,7},{6,4},{7,5},{8,10},{9,11},{10,... | collective-permute-start | bytes 1179656 | tf_op jit(solution)/shard_map/ppermute | solution.py:35
  12.1 1.3 %collective-permute-done.3.pin = f32[32,3072]{1,0:T(8,128)S(1)} collective-permute-done((f32[32,3072]{1,0:T(8,128)S(1)}, f32[32,3072]{1,0:T(8,128)S(1)}, u32[]{:S(2)}, u32[]{:S(2)}) %collective-permute-start.3) | collective-permute-done | bytes 393248 | tf_op jit(solution)/shard_map/ppermute | solution.py:35
  13.4 3.9 %collective-permute-start.6 = (f32[48,128]{1,0:T(8,128)S(1)}, f32[48,128]{1,0:T(8,128)S(1)}, u32[]{:S(2)}, u32[]{:S(2)}) collective-permute-start(f32[48,128]{1,0:T(8,128)S(1)} %pad_maximum_fusion.1), channel_id=1, source_target_pairs={{2,4},{3,5},{4,2},{5,3},{6,8},{7,9},{8,6},{9,7},{10,12},{11,13},{1... | collective-permute-start | bytes 73736 | tf_op jit(solution)/shard_map/ppermute | solution.py:35
  17.8 1.9 %collective-permute-start.4 = (f32[24,3072]{1,0:T(8,128)S(1)}, f32[24,3072]{1,0:T(8,128)S(1)}, u32[]{:S(2)}, u32[]{:S(2)}) collective-permute-start(f32[24,3072]{1,0:T(8,128)S(1)} %scatter.6.own_msg), channel_id=1, source_target_pairs={{2,4},{3,5},{4,2},{5,3},{6,8},{7,9},{8,6},{9,7},{10,12},{11,13},{1... | collective-permute-start | bytes 884744 | tf_op jit(solution)/shard_map/ppermute | solution.py:35
  19.7 15.4 %collective-permute-start.7 = (f32[96,128]{1,0:T(8,128)S(1)}, f32[96,128]{1,0:T(8,128)S(1)}, u32[]{:S(2)}, u32[]{:S(2)}) collective-permute-start(f32[96,128]{1,0:T(8,128)S(1)} %constant_dynamic-update-slice_fusion), channel_id=1, source_target_pairs={{0,1},{1,0},{2,3},{3,2},{4,5},{5,4},{6,7},{7,6},{8,9},{9,8},{10,11... | collective-permute-start | bytes 147464 | tf_op jit(solution)/shard_map/ppermute | solution.py:35
  35.2 15.1 %collective-permute-start.5 = (f32[24,3072]{1,0:T(8,128)S(1)}, f32[24,3072]{1,0:T(8,128)S(1)}, u32[]{:S(2)}, u32[]{:S(2)}) collective-permute-start(f32[24,3072]{1,0:T(8,128)S(1)} %collective-permute-done.4.out), channel_id=1, source_target_pairs={{0,2},{1,3},{2,0},{3,1},{4,6},{5,7},{6,4},{7,5},{8,10},{9,11},{10,... | collective-permute-start | bytes 884744 | tf_op jit(solution)/shard_map/ppermute | solution.py:35
  50.3 1.9 %collective-permute-start.8 = (f32[48,128]{1,0:T(8,128)S(1)}, f32[48,128]{1,0:T(8,128)S(1)}, u32[]{:S(2)}, u32[]{:S(2)}) collective-permute-start(f32[48,128]{1,0:T(8,128)S(1)} %slice_select_fusion.out_strip), channel_id=1, source_target_pairs={{0,2},{1,3},{2,0},{3,1},{4,6},{5,7},{6,4},{7,5},{8,10},{9,11},{10,... | collective-permute-start | bytes 73736 | tf_op jit(solution)/shard_map/ppermute | solution.py:35
  52.3 1.1 collective-permute-done.8.far_strip
  53.5 0.6 copy-done.33
  54.1 2.5 %shard_map.166 = (f32[5,16,3200]{2,1,0:T(8,128)S(1)}, f32[16,3200]{1,0:T(8,128)S(1)}, f32[16,3200]{1,0:T(8,128)S(1)}, f32[8,3200]{1,0:T(8,128)S(1)}, f32[16,3200...) custom-call(s32[4]{0:T(128)S(1)} %pad_add_fusion.info, ...), custom_call_target="tpu_custom_call" | custom-call | tf_op jit(solution)/shard_map/pallas_call | solution.py:73
  56.6 0.7 copy-done.14
  57.3 0.7 copy-done.16
  58.0 0.7 copy-done.18
  58.6 0.6 copy-done.20
  59.3 0.6 copy-done.22
  59.9 0.6 copy-done.24
  60.6 0.6 copy-done.26
  61.2 0.6 copy-done.28
  61.8 2.1 %collective-permute-start.9 = (f32[8,3200]{1,0:T(8,128)S(1)}, f32[8,3200]{1,0:T(8,128)S(1)}, u32[]{:S(2)}, u32[]{:S(2)}) collective-permute-start(f32[8,3200]{1,0:T(8,128)S(1)} %get-tuple-element.61), channel_id=1, source_target_pairs={{0,2},{1,3},{2,0},{3,1},{4,6},{5,7},{6,4},{7,5},{8,10},{9,11},{10,... | collective-permute-start | bytes 307208 | tf_op jit(solution)/shard_map/ppermute | solution.py:35
  63.8 2.3 %collective-permute-start = (f32[2,64,768]{2,1,0:T(8,128)S(1)}, f32[2,64,768]{2,1,0:T(8,128)S(1)}, u32[]{:S(2)}, u32[]{:S(2)}) collective-permute-start(f32[2,64,768]{2,1,0:T(8,128)S(1)} %get-tuple-element.48.own), channel_id=1, source_target_pairs={{0,2},{1,3},{2,0},{3,1},{4,6},{5,7},{6,4},{7,5},{8,10},{9,11},{10,... | collective-permute-start | bytes 1179656 | tf_op jit(solution)/shard_map/ppermute | solution.py:35
  66.2 1.4 %scatter.9 = f32[8,3200]{1,0:T(8,128)} dynamic-update-slice(f32[8,3200]{1,0:T(8,128)} %copy-done.41, f32[1,896]{1,0:T(1,128)S(1)} %broadcast_select_fusion.2, s32[]{:T(128)} %constant.91.clone.1, s32[]{:T(128)} %constant.92.clone.1) | dynamic-update-slice | bytes 7172 | tf_op jit(solution)/shard_map/scatter | solution.py:563
  67.6 1.9 %collective-permute-start.10 = (f32[8,3200]{1,0:T(8,128)}, f32[8,3200]{1,0:T(8,128)S(1)}, u32[]{:S(2)}, u32[]{:S(2)}) collective-permute-start(f32[8,3200]{1,0:T(8,128)} %scatter.9), channel_id=1, source_target_pairs={{2,4},{3,5},{4,2},{5,3},{6,8},{7,9},{8,6},{9,7},{10,12},{11,13},{1... | collective-permute-start | bytes 307208 | tf_op jit(solution)/shard_map/ppermute | solution.py:35
  69.6 4.2 %collective-permute-done.10.out = f32[8,3200]{1,0:T(8,128)S(1)} collective-permute-done((f32[8,3200]{1,0:T(8,128)}, f32[8,3200]{1,0:T(8,128)S(1)}, u32[]{:S(2)}, u32[]{:S(2)}) %collective-permute-start.10) | collective-permute-done | bytes 102432 | tf_op jit(solution)/shard_map/ppermute | solution.py:35
  73.8 11.9 %collective-permute-start.11 = (f32[8,3200]{1,0:T(8,128)S(1)}, f32[8,3200]{1,0:T(8,128)S(1)}, u32[]{:S(2)}, u32[]{:S(2)}) collective-permute-start(f32[8,3200]{1,0:T(8,128)S(1)} %collective-permute-done.10.out), channel_id=1, source_target_pairs={{0,2},{1,3},{2,0},{3,1},{4,6},{5,7},{6,4},{7,5},{8,10},{9,11},{10,... | collective-permute-start | bytes 307208 | tf_op jit(solution)/shard_map/ppermute | solution.py:35
  85.8 1.0 pad_maximum_fusion
  86.7 1.9 %collective-permute-start.1 = (f32[4,64,768]{2,1,0:T(8,128)}, f32[4,64,768]{2,1,0:T(8,128)S(1)}, u32[]{:S(2)}, u32[]{:S(2)}) collective-permute-start(f32[4,64,768]{2,1,0:T(8,128)} %pad_maximum_fusion), channel_id=1, source_target_pairs={{2,4},{3,5},{4,2},{5,3},{6,8},{7,9},{8,6},{9,7},{10,12},{11,13},{1... | collective-permute-start | bytes 2359304 | tf_op jit(solution)/shard_map/ppermute | solution.py:35
  88.8 0.5 copy-done.31
  89.3 2.4 %shard_map.167 = (f32[8,3072]{1,0:T(8,128)}, f32[2,768]{1,0:T(2,128)}, f32[2,768]{1,0:T(2,128)S(1)}, f32[4,256]{1,0:T(4,128)S(1)}) custom-call(s32[4]{0:T(128)S(1)} %copy-done.31, f32[32]{0:T(128)S(1)} %copy-done.38, f32[32]{0:T(128)S(1)} %copy-done.40, s32[2,128]{1,0:T(2,128)S(1)} %bitcast.12, f32[5,16,3200]{2,1,0:T(8,128)S(1)} %get-tuple-element.53.coef, ...), custom_call_target="tpu_custom_call" | custom-call | tf_op jit(solution)/shard_map/pallas_call | solution.py:73
  91.7 0.7 copy-done.36
  92.5 1.9 %collective-permute-start.12 = (f32[16,256]{1,0:T(8,128)S(1)}, f32[16,256]{1,0:T(8,128)S(1)}, u32[]{:S(2)}, u32[]{:S(2)}) collective-permute-start(f32[16,256]{1,0:T(8,128)S(1)} %concatenate.64.own), channel_id=1, source_target_pairs={{0,32},{1,33},{2,34},{3,35},{4,36},{5,37},{6,38},{7,39},{8,40},{9,... | collective-permute-start | bytes 49160 | tf_op jit(solution)/shard_map/ppermute | solution.py:35
  94.4 4.7 %collective-permute-done.12 = f32[16,256]{1,0:T(8,128)S(1)} collective-permute-done((f32[16,256]{1,0:T(8,128)S(1)}, f32[16,256]{1,0:T(8,128)S(1)}, u32[]{:S(2)}, u32[]{:S(2)}) %collective-permute-start.12) | collective-permute-done | bytes 16416 | tf_op jit(solution)/shard_map/ppermute | solution.py:35
  99.0 0.8 broadcast_select_fusion
  99.8 9.7 %all-to-all-start = ((f32[16,16,256]{2,1,0:T(8,128)}), f32[16,16,256]{2,1,0:T(8,128)S(1)}, u32[]{:S(2)}, u32[]{:S(2)}) async-start(f32[16,16,256]{2,1,0:T(8,128)} %broadcast_select_fusion), calls=%async_computation | async-start | bytes 524288 | tf_op jit(solution)/shard_map/all_to_all | solution.py:578
  110.0 4.6 %collective-permute-start.2 = (f32[2,64,768]{2,1,0:T(8,128)S(1)}, f32[2,64,768]{2,1,0:T(8,128)S(1)}, u32[]{:S(2)}, u32[]{:S(2)}) collective-permute-start(f32[2,64,768]{2,1,0:T(8,128)S(1)} %slice.118), channel_id=1, source_target_pairs={{0,2},{1,3},{2,0},{3,1},{4,6},{5,7},{6,4},{7,5},{8,10},{9,11},{10,... | collective-permute-start | bytes 1179656 | tf_op jit(solution)/shard_map/ppermute | solution.py:35
  114.8 1.2 collective-permute-done.2.far
  116.1 5.1 %shard_map.168 = f32[64,2,768]{2,1,0:T(2,128)} custom-call(s32[4]{0:T(128)S(1)} %copy-done.31, f32[64,128]{1,0:T(8,128)S(1)} %broadcast_in_dim.52.u, f32[64,128]{1,0:T(8,128)S(1)} %broadcast_in_dim.54.v, f32[2,64,768]{2,1,0:T(8,128)S(1)} %get-tuple-element.48.own, f32[2,64,768]{2,1,0:T(8,128)S(1)} %collective-permute-done.pin, ...), custom_call_target="tpu_custom_call" | custom-call | tf_op jit(solution)/shard_map/pallas_call | solution.py:73
  121.2 5.4 %all-to-all-done.got = f32[16,16,256]{2,1,0:T(8,128)S(1)} async-done(((f32[16,16,256]{2,1,0:T(8,128)}), f32[16,16,256]{2,1,0:T(8,128)S(1)}, u32[]{:S(2)}, u32[]{:S(2)}) %all-to-all-start) | async-done | bytes 262176 | tf_op jit(solution)/shard_map/all_to_all | solution.py:578
  126.6 3.8 %shard_map.169 = f32[1,256]{1,0:T(1,128)} custom-call(s32[4]{0:T(128)S(1)} %copy-done.31, f32[16,256]{1,0:T(8,128)S(1)} %concatenate.64.own, f32[16,16,256]{2,1,0:T(8,128)S(1)} %all-to-all-done.got), custom_call_target="tpu_custom_call" | custom-call | tf_op jit(solution)/shard_map/pallas_call | solution.py:606
  (108 shorter events, 1.4 us)
Async XLA Ops:
  0.6 0.7 copy-start.32
  0.7 52.7 %copy-start.30 = (s32[4]{0:T(128)}, s32[4]{0:T(128)S(1)}, u32[]{:S(2)}) copy-start(s32[4]{0:T(128)S(1)} %pad_add_fusion.info) | copy-start | bytes 52
  1.3 1.0 copy-start
  2.3 0.9 copy-start.1
  3.2 0.9 copy-start.3
  4.1 0.9 copy-start.5
  5.0 0.9 copy-start.7
  5.9 0.9 copy-start.9
  6.8 0.9 copy-start.11
  7.7 0.9 copy-start.13
  8.6 44.8 %copy-start.8 = (s32[8,3072]{1,0:T(8,128)S(1)}, s32[8,3072]{1,0:T(8,128)}, u32[]{:S(2)}) copy-start(s32[8,3072]{1,0:T(8,128)} %mask.3) | copy-start | bytes 294916
  8.6 44.9 %copy-start.10 = (s32[8,3072]{1,0:T(8,128)S(1)}, s32[8,3072]{1,0:T(8,128)}, u32[]{:S(2)}) copy-start(s32[8,3072]{1,0:T(8,128)} %code.3) | copy-start | bytes 294916
  8.6 44.9 %copy-start.12 = (f32[8,3072]{1,0:T(8,128)S(1)}, f32[8,3072]{1,0:T(8,128)}, u32[]{:S(2)}) copy-start(f32[8,3072]{1,0:T(8,128)} %depth.3) | copy-start | bytes 294916
  9.5 3.9 %collective-permute-start.3 = (f32[32,3072]{1,0:T(8,128)S(1)}, f32[32,3072]{1,0:T(8,128)S(1)}, u32[]{:S(2)}, u32[]{:S(2)}) collective-permute-start(f32[32,3072]{1,0:T(8,128)S(1)} %get-tuple-element.50), channel_id=1, source_target_pairs={{0,2},{1,3},{2,0},{3,1},{4,6},{5,7},{6,4},{7,5},{8,10},{9,11},{10,... | collective-permute-start | bytes 1179656 | tf_op jit(solution)/shard_map/ppermute | solution.py:35
  13.4 40.1 %copy-start.6 = (f32[8,3072]{1,0:T(8,128)S(1)}, f32[8,3072]{1,0:T(8,128)}, u32[]{:S(2)}) copy-start(f32[8,3072]{1,0:T(8,128)} %rf.3) | copy-start | bytes 294916
  13.4 6.3 %collective-permute-start.6 = (f32[48,128]{1,0:T(8,128)S(1)}, f32[48,128]{1,0:T(8,128)S(1)}, u32[]{:S(2)}, u32[]{:S(2)}) collective-permute-start(f32[48,128]{1,0:T(8,128)S(1)} %pad_maximum_fusion.1), channel_id=1, source_target_pairs={{2,4},{3,5},{4,2},{5,3},{6,8},{7,9},{8,6},{9,7},{10,12},{11,13},{1... | collective-permute-start | bytes 73736 | tf_op jit(solution)/shard_map/ppermute | solution.py:35
  17.8 17.4 %collective-permute-start.4 = (f32[24,3072]{1,0:T(8,128)S(1)}, f32[24,3072]{1,0:T(8,128)S(1)}, u32[]{:S(2)}, u32[]{:S(2)}) collective-permute-start(f32[24,3072]{1,0:T(8,128)S(1)} %scatter.6.own_msg), channel_id=1, source_target_pairs={{2,4},{3,5},{4,2},{5,3},{6,8},{7,9},{8,6},{9,7},{10,12},{11,13},{1... | collective-permute-start | bytes 884744 | tf_op jit(solution)/shard_map/ppermute | solution.py:35
  19.7 33.8 %copy-start.4 = (f32[8,3072]{1,0:T(8,128)S(1)}, f32[8,3072]{1,0:T(8,128)}, u32[]{:S(2)}) copy-start(f32[8,3072]{1,0:T(8,128)} %cond.3) | copy-start | bytes 294916
  19.7 33.8 %copy-start.2 = (f32[8,3072]{1,0:T(8,128)S(1)}, f32[8,3072]{1,0:T(8,128)}, u32[]{:S(2)}) copy-start(f32[8,3072]{1,0:T(8,128)} %elev.3) | copy-start | bytes 294916
  19.7 30.6 %collective-permute-start.7 = (f32[96,128]{1,0:T(8,128)S(1)}, f32[96,128]{1,0:T(8,128)S(1)}, u32[]{:S(2)}, u32[]{:S(2)}) collective-permute-start(f32[96,128]{1,0:T(8,128)S(1)} %constant_dynamic-update-slice_fusion), channel_id=1, source_target_pairs={{0,1},{1,0},{2,3},{3,2},{4,5},{5,4},{6,7},{7,6},{8,9},{9,8},{10,11... | collective-permute-start | bytes 147464 | tf_op jit(solution)/shard_map/ppermute | solution.py:35
  35.2 18.2 %collective-permute-start.5 = (f32[24,3072]{1,0:T(8,128)S(1)}, f32[24,3072]{1,0:T(8,128)S(1)}, u32[]{:S(2)}, u32[]{:S(2)}) collective-permute-start(f32[24,3072]{1,0:T(8,128)S(1)} %collective-permute-done.4.out), channel_id=1, source_target_pairs={{0,2},{1,3},{2,0},{3,1},{4,6},{5,7},{6,4},{7,5},{8,10},{9,11},{10,... | collective-permute-start | bytes 884744 | tf_op jit(solution)/shard_map/ppermute | solution.py:35
  50.3 3.1 %collective-permute-start.8 = (f32[48,128]{1,0:T(8,128)S(1)}, f32[48,128]{1,0:T(8,128)S(1)}, u32[]{:S(2)}, u32[]{:S(2)}) collective-permute-start(f32[48,128]{1,0:T(8,128)S(1)} %slice_select_fusion.out_strip), channel_id=1, source_target_pairs={{0,2},{1,3},{2,0},{3,1},{4,6},{5,7},{6,4},{7,5},{8,10},{9,11},{10,... | collective-permute-start | bytes 73736 | tf_op jit(solution)/shard_map/ppermute | solution.py:35
  52.3 1.2 copy-start.39
  57.3 0.7 copy-start.16
  61.8 4.3 %copy-start.41 = (f32[8,3200]{1,0:T(8,128)}, f32[8,3200]{1,0:T(8,128)S(1)}, u32[]{:S(2)}) copy-start(f32[8,3200]{1,0:T(8,128)S(1)} %get-tuple-element.62) | copy-start | bytes 307204
  61.8 4.4 %copy-start.35 = (f32[4,256]{1,0:T(4,128)}, f32[4,256]{1,0:T(4,128)S(1)}, u32[]{:S(2)}) copy-start(f32[4,256]{1,0:T(4,128)S(1)} %get-tuple-element.66) | copy-start | bytes 12292
  61.8 4.3 %collective-permute-start.9 = (f32[8,3200]{1,0:T(8,128)S(1)}, f32[8,3200]{1,0:T(8,128)S(1)}, u32[]{:S(2)}, u32[]{:S(2)}) collective-permute-start(f32[8,3200]{1,0:T(8,128)S(1)} %get-tuple-element.61), channel_id=1, source_target_pairs={{0,2},{1,3},{2,0},{3,1},{4,6},{5,7},{6,4},{7,5},{8,10},{9,11},{10,... | collective-permute-start | bytes 307208 | tf_op jit(solution)/shard_map/ppermute | solution.py:35
  63.8 21.9 %collective-permute-start = (f32[2,64,768]{2,1,0:T(8,128)S(1)}, f32[2,64,768]{2,1,0:T(8,128)S(1)}, u32[]{:S(2)}, u32[]{:S(2)}) collective-permute-start(f32[2,64,768]{2,1,0:T(8,128)S(1)} %get-tuple-element.48.own), channel_id=1, source_target_pairs={{0,2},{1,3},{2,0},{3,1},{4,6},{5,7},{6,4},{7,5},{8,10},{9,11},{10,... | collective-permute-start | bytes 1179656 | tf_op jit(solution)/shard_map/ppermute | solution.py:35
  66.1 3.4 %copy-start.43 = (s32[256]{0:T(256)S(1)}, s32[256]{0:T(256)}, u32[]{:S(2)}) copy-start(s32[256]{0:T(256)} %param.30) | copy-start | bytes 3076
  67.6 6.2 %collective-permute-start.10 = (f32[8,3200]{1,0:T(8,128)}, f32[8,3200]{1,0:T(8,128)S(1)}, u32[]{:S(2)}, u32[]{:S(2)}) collective-permute-start(f32[8,3200]{1,0:T(8,128)} %scatter.9), channel_id=1, source_target_pairs={{2,4},{3,5},{4,2},{5,3},{6,8},{7,9},{8,6},{9,7},{10,12},{11,13},{1... | collective-permute-start | bytes 307208 | tf_op jit(solution)/shard_map/ppermute | solution.py:35
  69.5 19.1 %copy-start.15 = (f32[16,3200]{1,0:T(8,128)S(1)}, f32[16,3200]{1,0:T(8,128)}, u32[]{:S(2)}) copy-start(f32[16,3200]{1,0:T(8,128)} %copy-done.14) | copy-start | bytes 614404
  69.6 19.1 %copy-start.17 = (f32[16,3200]{1,0:T(8,128)S(1)}, f32[16,3200]{1,0:T(8,128)}, u32[]{:S(2)}) copy-start(f32[16,3200]{1,0:T(8,128)} %copy-done.16) | copy-start | bytes 614404
  69.6 19.1 %copy-start.19 = (f32[16,3200]{1,0:T(8,128)S(1)}, f32[16,3200]{1,0:T(8,128)}, u32[]{:S(2)}) copy-start(f32[16,3200]{1,0:T(8,128)} %copy-done.18) | copy-start | bytes 614404
  69.6 19.1 %copy-start.23 = (f32[8,3200]{1,0:T(8,128)S(1)}, f32[8,3200]{1,0:T(8,128)}, u32[]{:S(2)}) copy-start(f32[8,3200]{1,0:T(8,128)} %copy-done.22) | copy-start | bytes 307204
  69.6 19.1 %copy-start.25 = (f32[8,3200]{1,0:T(8,128)S(1)}, f32[8,3200]{1,0:T(8,128)}, u32[]{:S(2)}) copy-start(f32[8,3200]{1,0:T(8,128)} %copy-done.24) | copy-start | bytes 307204
  73.8 14.9 %collective-permute-start.11 = (f32[8,3200]{1,0:T(8,128)S(1)}, f32[8,3200]{1,0:T(8,128)S(1)}, u32[]{:S(2)}, u32[]{:S(2)}) collective-permute-start(f32[8,3200]{1,0:T(8,128)S(1)} %collective-permute-done.10.out), channel_id=1, source_target_pairs={{0,2},{1,3},{2,0},{3,1},{4,6},{5,7},{6,4},{7,5},{8,10},{9,11},{10,... | collective-permute-start | bytes 307208 | tf_op jit(solution)/shard_map/ppermute | solution.py:35
  85.7 3.0 %copy-start.21 = (f32[8,896]{1,0:T(8,128)S(1)}, f32[8,896]{1,0:T(8,128)}, u32[]{:S(2)}) copy-start(f32[8,896]{1,0:T(8,128)} %copy-done.20) | copy-start | bytes 86020
  85.7 3.0 %copy-start.27 = (f32[8,896]{1,0:T(8,128)S(1)}, f32[8,896]{1,0:T(8,128)}, u32[]{:S(2)}) copy-start(f32[8,896]{1,0:T(8,128)} %copy-done.26) | copy-start | bytes 86020
  85.7 3.0 %copy-start.29 = (f32[8,896]{1,0:T(8,128)S(1)}, f32[8,896]{1,0:T(8,128)}, u32[]{:S(2)}) copy-start(f32[8,896]{1,0:T(8,128)} %copy-done.28) | copy-start | bytes 86020
  85.7 3.0 %copy-start.38 = (f32[32]{0:T(128)S(1)}, f32[32]{0:T(128)}, u32[]{:S(2)}) copy-start(f32[32]{0:T(128)} %u.3) | copy-start | bytes 388
  85.7 3.0 %copy-start.40 = (f32[32]{0:T(128)S(1)}, f32[32]{0:T(128)}, u32[]{:S(2)}) copy-start(f32[32]{0:T(128)} %v.3) | copy-start | bytes 388
  86.7 23.3 %collective-permute-start.1 = (f32[4,64,768]{2,1,0:T(8,128)}, f32[4,64,768]{2,1,0:T(8,128)S(1)}, u32[]{:S(2)}, u32[]{:S(2)}) collective-permute-start(f32[4,64,768]{2,1,0:T(8,128)} %pad_maximum_fusion), channel_id=1, source_target_pairs={{2,4},{3,5},{4,2},{5,3},{6,8},{7,9},{8,6},{9,7},{10,12},{11,13},{1... | collective-permute-start | bytes 2359304 | tf_op jit(solution)/shard_map/ppermute | solution.py:35
  88.7 0.7 copy-start.34
  91.7 0.7 copy-start.36
  91.7 0.7 copy-start.42
  92.5 6.6 %collective-permute-start.12 = (f32[16,256]{1,0:T(8,128)S(1)}, f32[16,256]{1,0:T(8,128)S(1)}, u32[]{:S(2)}, u32[]{:S(2)}) collective-permute-start(f32[16,256]{1,0:T(8,128)S(1)} %concatenate.64.own), channel_id=1, source_target_pairs={{0,32},{1,33},{2,34},{3,35},{4,36},{5,37},{6,38},{7,39},{8,40},{9,... | collective-permute-start | bytes 49160 | tf_op jit(solution)/shard_map/ppermute | solution.py:35
  99.8 26.8 %all-to-all-start = ((f32[16,16,256]{2,1,0:T(8,128)}), f32[16,16,256]{2,1,0:T(8,128)S(1)}, u32[]{:S(2)}, u32[]{:S(2)}) async-start(f32[16,16,256]{2,1,0:T(8,128)} %broadcast_select_fusion), calls=%async_computation | async-start | bytes 524288 | tf_op jit(solution)/shard_map/all_to_all | solution.py:578
  110.0 5.9 %collective-permute-start.2 = (f32[2,64,768]{2,1,0:T(8,128)S(1)}, f32[2,64,768]{2,1,0:T(8,128)S(1)}, u32[]{:S(2)}, u32[]{:S(2)}) collective-permute-start(f32[2,64,768]{2,1,0:T(8,128)S(1)} %slice.118), channel_id=1, source_target_pairs={{0,2},{1,3},{2,0},{3,1},{4,6},{5,7},{6,4},{7,5},{8,10},{9,11},{10,... | collective-permute-start | bytes 1179656 | tf_op jit(solution)/shard_map/ppermute | solution.py:35
  (10 other events, 6.5 us)

commit v2 on v1

v2 whole, which is shorter than its diff:
```python
import jax
import jax.numpy as jnp
from jax import lax
from jax.experimental import pallas as pl
from jax.experimental.pallas import tpu as pltpu
from jax.sharding import PartitionSpec as P

ASTEPS = 2
HSTEPS = 4
COUPLE = 2
STEPS = HSTEPS * COUPLE

F32 = jnp.float32
BF16 = jnp.bfloat16
AXES = ("grp", "gx", "gy")
ROOM = 16 * 1024 * 1024
WHOLE = 60 * 1024 * 1024

LINKS = 256
TR = 8
TC = 3072
TW = TC + 128
AC = 768
AW = AC + 128
FL = 64
Q0 = 32


def exchange(value, partner):
    pairs = []
    for r in range(256):
        for g in range(2):
            t, h = partner(r, g)
            if 0 <= t < 256:
                pairs.append((r * 2 + g, t * 2 + h))
    return lax.ppermute(value, AXES, pairs)


def outer(r):
    return r + 1 if r % 2 else r - 1


def pair_swap(value):
    return exchange(value, lambda r, g: (r ^ 1, g))


def chip_swap(value):
    return exchange(value, lambda r, g: (outer(r), g))


def near_swap(value):
    return exchange(
        value, lambda r, g: (outer(r), g if outer(r) // 16 == r // 16 else 1 - g)
    )


def gy_swap(value):
    return exchange(value, lambda r, g: (r, 1 - g))


def grp_shift(value):
    return exchange(value, lambda r, g: (r + 16, g))


def vmem():
    return pl.BlockSpec(memory_space=pltpu.VMEM)


def smem():
    return pl.BlockSpec(memory_space=pltpu.SMEM)


def hbm():
    return pl.BlockSpec(memory_space=pltpu.HBM)


def call(body, outs, scalars, arrays, scratch=(), limit=ROOM, far=0):
    space = hbm() if far else vmem()
    return pl.pallas_call(
        body,
        out_shape=[jax.ShapeDtypeStruct(o, F32) for o in outs],
        in_specs=[smem()] * len(scalars) + [space] * len(arrays),
        out_specs=[hbm() if i < far else vmem() for i in range(len(outs))],
        scratch_shapes=[pltpu.VMEM(x, F32) if isinstance(x, tuple) else x for x in scratch],
        compiler_params=pltpu.CompilerParams(vmem_limit_bytes=limit),
    )(*scalars, *arrays)


BLOCK, EDGE = 104, 88
ELEV, COND, RAIN, MASK, CODE, DEPTH, SOIL = range(7)
EDGES = ((ELEV, 0, 4), (COND, 12, 3), (RAIN, 15, 3), (MASK, 18, 3), (CODE, 4, 4), (DEPTH, 8, 4))


def pack_body(
    info, air, kd, elev, cond, rf, mask, code, depth, soil,
    block_h,
    air_v, kd_v, elev_v, cond_v, rf_v, mask_v, code_v, depth_v, soil_v,
    block, sems, sent,
):
    right = info[1] == 1
    near = (kd_v, elev_v, cond_v, rf_v, mask_v, code_v, depth_v, soil_v, air_v)
    copies = [
        pltpu.make_async_copy(src, dst, sems.at[i])
        for i, (src, dst) in enumerate(
            zip((kd, elev, cond, rf, mask, code, depth, soil, air), near)
        )
    ]
    for c in copies:
        c.start()
    block[56:72, :] = jnp.zeros((16, TC), F32)
    for c in copies:
        c.wait()
    for i, ref in enumerate((elev_v, cond_v, rf_v, mask_v, code_v, depth_v, soil_v)):
        block[8 * i : 8 * i + 8, :] = ref[...].astype(F32)
    ends = []
    for r in range(2):
        rows = air_v[:, r, :]
        for h in range(2):
            at = slice((2 * h + r) * AC, (2 * h + r + 1) * AC)
            block[72:104, at] = rows[32 * h : 32 * h + 32, :]
        block[56:57, r * AC : (r + 1) * AC] = rows[Q0 : Q0 + 1, :]
        block[56:57, (2 + r) * AC : (3 + r) * AC] = rows[0:1, :]
        block[57:58, r * AC : (r + 1) * AC] = kd_v[r : r + 1, :]
        ends.append(jnp.where(right, rows[:, 0:128], rows[:, AC - 128 : AC]))
    land = jnp.where(right, block[0:56, 0:128], block[0:56, TC - 128 : TC])
    kblock = jnp.where(right, kd_v[:, 0:128], kd_v[:, AC - 128 : AC])
    square = jnp.concatenate([land, kblock, jnp.zeros((70, 128), F32)], axis=0).T
    strip = jnp.where(right, square[0:16], square[112:128])
    block[64:72, 0:128] = strip[0:8]
    block[64:72, 128:256] = strip[8:16]
    ablock = jnp.concatenate(ends, axis=0).T
    block[64:72, 256:384] = jnp.where(right, ablock[0:8], ablock[120:128])
    result = pltpu.make_async_copy(block, block_h, sent)
    result.start()
    result.wait()


def edge_body(info, block, pin, out, strips):
    odd = info[0] == 1
    for i, off, n in EDGES:
        top = block[8 * i : 8 * i + n, :]
        low = block[8 * i + 8 - n : 8 * i + 8, :]
        out[off : off + n, :] = jnp.where(odd, low, top)
    out[21:23, :] = block[56:58, :]
    out[23:24, :] = jnp.zeros((1, TC), F32)
    for i in range(2):
        a = pin[56 + i : 57 + i, AC : 2 * AC]
        b = pin[56 + i : 57 + i, 0:AC]
        out[22:23, (2 + i) * AC : (3 + i) * AC] = jnp.where(odd, a, b)
        lo, half = 24 + 32 * i, slice(2 * i * AC, 2 * (i + 1) * AC)
        out[lo : lo + 32, 0 : 2 * AC] = block[72:104, half]
        out[lo : lo + 32, 2 * AC : TC] = pin[72:104, half]
    lane = lax.broadcasted_iota(jnp.int32, (8, 128), 1)
    for b in range(2):
        at = slice(b * 128, (b + 1) * 128)
        pair = pltpu.roll(pin[64:72, at], 64, 1)
        strips[8 * b : 8 * b + 8, :] = jnp.where(lane < 64, block[64:72, at], pair)
    strips[16:24, :] = block[64:72, 256:384]
    strips[24:32, :] = pin[64:72, 256:384]


def both_body(strips, near, out):
    out[0:32, :] = strips[...]
    out[32:64, :] = near[...]


def pick_body(info, near, across, out):
    end = (info[3] == 0) | (info[3] == 15)
    out[...] = jnp.where(end, near[...], across[32:64, :])


def chunks_body(info, own, before, out):
    for i in range(16):
        out[i] = jnp.where(info[3] < i, own[...], before[...])


def land_strip(strip, right):
    zero = jnp.zeros((112, 128), F32)
    s = strip[0:16, :]
    return jnp.where(
        right, jnp.concatenate([zero, s], axis=0), jnp.concatenate([s, zero], axis=0)
    ).T


def air_strip(strip, right, lo):
    zero = jnp.zeros((120, 128), F32)
    s = strip[lo : lo + 8, :]
    return jnp.where(
        right, jnp.concatenate([zero, s], axis=0), jnp.concatenate([s, zero], axis=0)
    ).T


def lanes_inside(right, rows):
    lane = lax.broadcasted_iota(jnp.int32, (rows, AW), 1)
    edge = jnp.where(right, AW - 8, AC)
    halo = (lane >= edge) & (lane < edge + 8)
    return jnp.where((lane < AC) | halo, 1.0, 0.0).astype(F32)


def ring_mask(info, right):
    row = lax.broadcasted_iota(jnp.int32, (16, AW), 0)
    place = (info[2] - info[0]) * 2 + jnp.where(row < 8, row, row - 16)
    return jnp.where((place >= 0) & (place < 512), lanes_inside(right, 16), 0.0)


def ring_step(x, k, m, hu, hv):
    n = pltpu.roll(x, 1, 0)
    s = pltpu.roll(x, 15, 0)
    w = pltpu.roll(x, 1, 1)
    e = pltpu.roll(x, AW - 1, 1)
    return m * (x + k * (n + s + w + e - 4.0 * x) - hu * (e - w) - hv * (s - n))


def spread_matrix():
    i = lax.broadcasted_iota(jnp.int32, (128, 512), 0)
    j = lax.broadcasted_iota(jnp.int32, (128, 512), 1)
    return jnp.where(j // 4 == i, 1.0, 0.0).astype(BF16)


def two_parts(x):
    high = x.astype(BF16)
    low = (x - high.astype(F32)).astype(BF16)
    return jnp.concatenate([high, low], axis=0)


def spread_columns(rain, right):
    blocks = jnp.concatenate([rain[:, 128 * b : 128 * b + 128] for b in range(7)], axis=0)
    wide = jnp.dot(two_parts(blocks), spread_matrix(), preferred_element_type=F32)
    wide = wide[0:112] + wide[112:224]
    parts = [wide[16 * b : 16 * b + 16] for b in range(6)]
    last = wide[96:112]
    parts.append(jnp.where(right, last[:, 384:512], last[:, 0:128]))
    return jnp.concatenate(parts, axis=1)


def spread_rows(wide):
    row = lax.broadcasted_iota(jnp.int32, (8, TW), 0)
    return jnp.concatenate(
        [
            jnp.where(row < 4, wide[a : a + 1, :], wide[b : b + 1, :])
            for a, b in ((0, 1), (2, 3), (4, 15))
        ],
        axis=0,
    )


def soil_mean(soil, right):
    zero = jnp.zeros((16, 384), F32)
    last = soil[:, TC:TW]
    last = jnp.where(
        right,
        jnp.concatenate([zero, last], axis=1),
        jnp.concatenate([last, zero], axis=1),
    )
    blocks = jnp.concatenate([soil[:, 512 * b : 512 * b + 512] for b in range(6)] + [last], axis=0)
    sums = lax.dot_general(
        two_parts(blocks),
        spread_matrix(),
        (((1,), (1,)), ((), ())),
        preferred_element_type=F32,
    )
    sums = sums[0:112] + sums[112:224]
    wide = jnp.concatenate([sums[16 * b : 16 * b + 16] for b in range(7)], axis=1)
    wide = wide + pltpu.roll(wide, 15, 0)
    wide = wide + pltpu.roll(wide, 14, 0)
    row = lax.broadcasted_iota(jnp.int32, (16, AW), 0)
    mean = jnp.zeros((16, AW), F32)
    for i in range(4):
        mean = jnp.where(row == i, wide[4 * i : 4 * i + 1, :], mean)
    return mean * 0.0625


def lateral_of(depth, cells):
    row = lax.broadcasted_iota(jnp.int32, (8, 128), 0) * (TC // 128)
    out = []
    for h in range(2):
        cell = cells[h : h + 1, :]
        lane = jnp.broadcast_to(cell % 128, (8, 128))
        block = jnp.broadcast_to(cell // 128, (8, 128)) - row
        total = jnp.zeros((8, 128), F32)
        for b in range(TC // 128):
            got = jnp.take_along_axis(depth[:, 128 * b : 128 * b + 128], lane, axis=1)
            total = jnp.where(block == b, got, total)
        out.append(0.1 * jnp.sum(total, axis=0, keepdims=True))
    return out


def hydro(odd, coef, rq, ring, land, soil, cells, lat, base):
    for t in range(HSTEPS):
        d = ring[...]
        halves = lateral_of(jnp.where(odd, ring[8:16, 0:TC], ring[0:8, 0:TC]), cells)
        for h in range(2):
            lat[base + 2 * t + h : base + 2 * t + h + 1, :] = halves[h]
        soil[...] = soil[...] + 0.05 * land[...] * d[0:16] - 0.02 * soil[...]
        new = rq[...] + coef[0] * d
        new = new + coef[1] * pltpu.roll(d, 1, 1)
        new = new + coef[2] * pltpu.roll(d, TW - 1, 1)
        new = new + coef[3] * pltpu.roll(d, 1, 0)
        new = new + coef[4] * pltpu.roll(d, 23, 0)
        ring[...] = new


def rain_of(q):
    rain = 0.05 * q * q
    return rain, q - rain


def first_body(
    info, u, v, cells, block, pin, out, far, sp, nr, fs,
    coef, rain_w, static_w, land, ring, soil, lat, q_out, t_out, k_out, edge,
    grid, rq,
):
    odd = info[0] == 1
    right = info[1] == 1
    hu_t, hv_t = 0.5 * u[0], 0.5 * v[0]
    square = land_strip(sp, right)
    mine, pair = square[0:64], square[64:128]
    cols = (jnp.where(odd, pair, mine), jnp.where(odd, mine, pair))
    square = land_strip(nr, right)
    beyond, out2 = square[0:64], square[64:128]
    square = land_strip(fs, right)
    other, far2 = square[0:64], square[64:128]
    cols_s, cols_n = jnp.where(odd, beyond, other), jnp.where(odd, other, beyond)
    grid[...] = jnp.zeros_like(grid)

    def chip_rows(ref, i, lo):
        at = slice(8 * i, 8 * i + 8)
        ref[lo : lo + 8, 0:TC] = jnp.where(odd, pin[at, :], block[at, :])
        ref[lo + 8 : lo + 16, 0:TC] = jnp.where(odd, block[at, :], pin[at, :])
        ref[lo : lo + 8, TC:TW] = cols[0][at]
        ref[lo + 8 : lo + 16, TC:TW] = cols[1][at]

    for i, off, n in EDGES:
        chip_rows(grid, i, 24 * i)
        e_out = out[off : off + n, :]
        e_far = far[off : off + n, :]
        lo = 24 * i
        grid[lo + 16 : lo + 16 + n, 0:TC] = jnp.where(odd, e_out, e_far)
        grid[lo + 24 - n : lo + 24, 0:TC] = jnp.where(odd, e_far, e_out)
        grid[lo + 16 : lo + 16 + n, TC:TW] = cols_s[8 * i : 8 * i + n]
        grid[lo + 24 - n : lo + 24, TC:TW] = cols_n[8 * i + 8 - n : 8 * i + 8]
    chip_rows(soil, SOIL, 0)

    def field(i):
        return grid[24 * i : 24 * i + 24, :]

    m = field(MASK)
    land[...] = m[0:16]
    eta = field(ELEV)
    lap = (
        pltpu.roll(eta, 1, 1)
        + pltpu.roll(eta, TW - 1, 1)
        + pltpu.roll(eta, 1, 0)
        + pltpu.roll(eta, 23, 0)
        - 4.0 * eta
    )
    mc = m * field(COND)
    codes = field(CODE)
    share = 0.2 * m
    coef[0] = 0.75 * m - 4.0 * mc
    coef[1] = mc + jnp.where(pltpu.roll(codes, 1, 1) == 0.0, share, 0.0)
    coef[2] = mc + jnp.where(pltpu.roll(codes, TW - 1, 1) == 2.0, share, 0.0)
    coef[3] = mc + jnp.where(pltpu.roll(codes, 1, 0) == 3.0, share, 0.0)
    coef[4] = mc + jnp.where(pltpu.roll(codes, 23, 0) == 1.0, share, 0.0)
    rain_w[...] = m * field(RAIN)
    static_w[...] = mc * lap
    ring[...] = field(DEPTH)
    mine_a, pair_a = air_strip(sp, right, 16), air_strip(sp, right, 24)
    out_a, out2_a = air_strip(nr, right, 16), air_strip(nr, right, 24)
    far_a, far2_a = air_strip(fs, right, 16), air_strip(fs, right, 24)
    own_r, pair_r = block[56:64, :], pin[56:64, :]
    out_r, far_r = out[16:24, :], far[16:24, :]
    for ref in (q_out, t_out, k_out):
        ref[...] = jnp.zeros_like(ref)
    for odd_side, msg, first, air_s, col_s in (
        (None, jnp.where(odd, pair_r, own_r), 0, jnp.where(odd, pair_a, mine_a), cols[0]),
        (None, jnp.where(odd, own_r, pair_r), 2, jnp.where(odd, mine_a, pair_a), cols[1]),
        (False, jnp.where(odd, out_r, far_r), 4, jnp.where(odd, out_a, far_a), cols_s),
        (True, jnp.where(odd, far_r, out_r), 14, jnp.where(odd, far_a, out_a), cols_n),
    ):
        top = 0 if odd_side is None else 5
        for i in range(2):
            at = slice(first + i, first + i + 1)
            q_out[at, 0:AC] = msg[top : top + 1, i * AC : (i + 1) * AC]
            t_out[at, 0:AC] = msg[top : top + 1, (2 + i) * AC : (3 + i) * AC]
            k_out[at, 0:AC] = msg[top + 1 : top + 2, i * AC : (i + 1) * AC]
            q_out[at, AC:AW] = air_s[i * FL + Q0 : i * FL + Q0 + 1]
            t_out[at, AC:AW] = air_s[i * FL : i * FL + 1]
            k_out[at, AC:AW] = col_s[56 + i : 57 + i]
        if odd_side is not None:
            place = 13 if odd_side else 6
            i = 1 if odd_side else 0
            at = slice(place, place + 1)
            third_a = jnp.where(odd, far2_a, out2_a) if odd_side else jnp.where(odd, out2_a, far2_a)
            third = jnp.where(odd, far2, out2) if odd_side else jnp.where(odd, out2, far2)
            q_out[at, 0:AC] = msg[6:7, 2 * AC : 3 * AC]
            k_out[at, 0:AC] = msg[6:7, 3 * AC : 4 * AC]
            q_out[at, AC:AW] = third_a[i * FL + Q0 : i * FL + Q0 + 1]
            k_out[at, AC:AW] = third[56 + i : 57 + i]
    m8 = ring_mask(info, right)
    k = k_out[...]
    q, t = q_out[...], t_out[...]
    for _ in range(ASTEPS):
        q = ring_step(q, k, m8, hu_t, hv_t)
        t = ring_step(t, k, m8, hu_t, hv_t)
    rain, q = rain_of(q)
    rq[...] = static_w[...] + rain_w[...] * spread_rows(spread_columns(rain, right))
    lat[...] = jnp.zeros_like(lat)
    hydro(odd, coef, rq, ring, land, soil, cells[...], lat, 0)
    q = q + 0.1 * soil_mean(soil[...], right) * jax.nn.sigmoid(t)
    q_out[...] = q
    t_out[...] = t
    edge[0:4, :] = jnp.where(odd, ring[12:16, :], ring[0:4, :])
    edge[4:8, :] = jnp.zeros((4, TW), F32)
    for lane, a, b in ((0, 2, 0), (1, 3, 1), (2, 1, 2)):
        at = slice(lane * AW, (lane + 1) * AW)
        edge[4:5, at] = jnp.where(odd, q[a : a + 1], q[b : b + 1])
        if lane < 2:
            edge[5:6, at] = jnp.where(odd, t[a : a + 1], t[b : b + 1])


def second_body(
    info, u, v, cells, link_flow, link_down, coef, rain_w, static_w, land, ring0, soil0, lat0,
    q0, t0, k0, out, far,
    depth_out, coarse_out, q_out, lat,
    ring, soil, rq, q8, t8,
):
    odd = info[0] == 1
    right = info[1] == 1
    hu_t, hv_t = 0.5 * u[0], 0.5 * v[0]
    ring[0:16, :] = ring0[0:16, :]
    south = jnp.where(odd, out[...], far[...])
    north = jnp.where(odd, far[...], out[...])
    ring[16:20, :] = south[0:4]
    ring[20:24, :] = north[0:4]
    soil[...] = soil0[...]
    q8[...] = jnp.zeros_like(q8)
    t8[...] = jnp.zeros_like(t8)
    q8[0:4, :] = q0[0:4, :]
    t8[0:4, :] = t0[0:4, :]
    for places, msg in (((4, 5, 6), south), ((14, 15, 13), north)):
        for i, place in enumerate(places):
            q8[place : place + 1, :] = msg[4:5, i * AW : (i + 1) * AW]
            if i < 2:
                t8[place : place + 1, :] = msg[5:6, i * AW : (i + 1) * AW]
    m8 = ring_mask(info, right)
    k = k0[...]
    q, t = q8[...], t8[...]
    for _ in range(ASTEPS):
        q = ring_step(q, k, m8, hu_t, hv_t)
        t = ring_step(t, k, m8, hu_t, hv_t)
    rain, q = rain_of(q)
    rq[...] = static_w[...] + rain_w[...] * spread_rows(spread_columns(rain, right))
    lat[0:8, :] = lat0[...]
    lat[16:24, :] = jnp.zeros((8, 128), F32)
    lat[16:18, :] = link_flow[...]
    lat[18:20, :] = link_down[...].astype(F32)
    hydro(odd, coef, rq, ring, land, soil, cells[...], lat, 8)
    coarse = soil_mean(soil[...], right)
    q = q + 0.1 * coarse * jax.nn.sigmoid(t)
    depth_out[...] = jnp.where(odd, ring[8:16, 0:TC], ring[0:8, 0:TC])
    coarse_out[...] = jnp.where(odd, coarse[2:4, 0:AC], coarse[0:2, 0:AC])
    q_out[...] = jnp.where(odd, q[2:4, 0:AC], q[0:2, 0:AC])


def air_body(
    info, u, v, block, pin, out, far, k16, sp, nr, fs,
    air_out,
    strips,
):
    odd = info[0] == 1
    right = info[1] == 1
    r = info[2]
    for i, (ref, lo) in enumerate(((sp, 16), (sp, 24), (nr, 16), (nr, 24), (fs, 16))):
        strips[i] = air_strip(ref, right, lo)
    lanes = lanes_inside(right, 1)
    masks, kd = {}, {}
    for row in range(-3, 5):
        place = r * 2 + row
        masks[row] = lanes * jnp.where((place >= 0) & (place < 512), 1.0, 0.0)
        a, b = (2 + row) % 16, row % 16
        kd[row] = jnp.where(odd, k16[a : a + 1, :], k16[b : b + 1, :]) * masks[row]

    def group(half, g):
        at = pl.multiple_of(g * 8, 8)
        own8 = pl.ds(72 + at, 8)
        out8 = pl.ds(24 + 32 * half + at, 8)

        def whole(ref, rows, lane, strip, i):
            side = strips[strip, pl.ds(32 * half + i * FL + at, 8), :]
            return jnp.concatenate([ref[rows, lane * AC : (lane + 1) * AC], side], axis=1)

        x = {i: whole(block, own8, 2 * half + i, 0, i) for i in range(2)}
        p = [whole(pin, own8, 2 * half + i, 1, i) for i in range(2)]
        o = [whole(out, out8, i, 2, i) for i in range(2)]
        o2 = [whole(out, out8, 2 + i, 3, i) for i in range(2)]
        f = [whole(far, out8, i, 4, i) for i in range(2)]
        for i in range(2):
            x[2 + i] = jnp.where(odd, o[i], p[i])
            x[4 + i] = jnp.where(odd, o2[i], f[i])
            x[-2 + i] = jnp.where(odd, p[i], o[i])
            x[-4 + i] = jnp.where(odd, f[i], o2[i])
        row8 = lax.broadcasted_iota(jnp.int32, (8, AW), 0)
        hu = jnp.zeros((8, AW), F32)
        hv = jnp.zeros((8, AW), F32)
        for i in range(8):
            hu = jnp.where(row8 == i, 0.5 * u[at + i], hu)
            hv = jnp.where(row8 == i, 0.5 * v[at + i], hv)
        for step in range(ASTEPS * COUPLE):
            new = {}
            for row in range(-3 + step, 5 - step):
                c, n, s = x[row], x[row - 1], x[row + 1]
                w = pltpu.roll(c, 1, 1)
                e = pltpu.roll(c, AW - 1, 1)
                new[row] = (
                    masks[row] * (c - hu * (e - w) - hv * (s - n))
                    + kd[row] * (n + s + w + e - 4.0 * c)
                )
            x = new
        for i in range(2):
            air_out[pl.ds(32 * half + at, 8), i, :] = x[i][:, 0:AC]

    for half in range(2):
        lax.fori_loop(0, 4, lambda g, c, half=half: (group(half, g), c)[1], 0)


def route_body(info, own, got, flow_out, hot):
    j = info[3]
    target = lax.broadcasted_iota(jnp.int32, (2 * LINKS, LINKS), 0).astype(F32)
    data = [own[...]] + [got[lax.rem(j - k + 16, 16)] for k in range(1, STEPS + 1)]

    def wide(d, i):
        return jnp.concatenate([d[2 * i : 2 * i + 1, :], d[2 * i + 1 : 2 * i + 2, :]], axis=1)

    flow = [wide(d, 8) for d in data]
    for k in range(STEPS + 1):
        hot[k] = jnp.where(target == wide(data[k], 9), 1.0, 0.0).astype(BF16)
    for t in range(STEPS):
        routed = []
        for k in range(STEPS - t + 1):
            f = flow[k]
            f1 = f.astype(BF16)
            rest = f - f1.astype(F32)
            f2 = rest.astype(BF16)
            f3 = (rest - f2.astype(F32)).astype(BF16)
            lhs = jnp.concatenate([f1, f2, f3, jnp.zeros((13, LINKS), BF16)], axis=0)
            first = 0 if k < STEPS - t else LINKS
            last = 2 * LINKS if k > 0 else LINKS
            y = lax.dot_general(
                lhs,
                hot[k, first:last, :],
                (((1,), (1,)), ((), ())),
                preferred_element_type=F32,
            )
            y = y[0:1] + y[1:2] + y[2:3]
            local = None if first else y[:, 0:LINKS]
            down = y[:, LINKS - first :] if last > LINKS else None
            routed.append((local, down))
        new = []
        for k in range(STEPS - t):
            arrived = routed[k][0] + routed[k + 1][1]
            new.append(flow[k] + 0.5 * (arrived - flow[k]) + wide(data[k], t))
        flow = new
    flow_out[...] = flow[0]


def shards(
    air, kdiff, u_wind, v_wind, elev, cond, rain_factor, land_mask, flow_code,
    depth_init, soil_init, link_cell, link_down, link_flow,
):
    gx = lax.axis_index("gx")
    odd = gx % 2
    row = lax.axis_index("grp") * 16 + gx
    info = jnp.stack([odd, lax.axis_index("gy"), row, gx]).astype(jnp.int32)
    pairs = link_cell.reshape(2, 128), link_flow.reshape(2, 128), link_down.reshape(2, 128)

    land_v = pltpu.VMEM((TR, TC), F32)
    code_v = pltpu.VMEM((TR, TC), jnp.int32)
    (block,) = call(
        pack_body,
        [(BLOCK, TC)],
        [info],
        [air.reshape(FL, 2, AC), kdiff, elev, cond, rain_factor, land_mask, flow_code, depth_init, soil_init],
        [(FL, 2, AC), (2, AC), land_v, land_v, land_v, code_v, code_v, land_v, land_v, (BLOCK, TC),
         pltpu.SemaphoreType.DMA((9,)), pltpu.SemaphoreType.DMA],
        limit=WHOLE,
        far=1,
    )
    pin = pair_swap(block)
    edge, strips = call(edge_body, [(EDGE, TC), (32, 128)], [info], [block, pin])
    near = near_swap(strips)
    out = chip_swap(edge)
    (both,) = call(both_body, [(64, 128)], [], [strips, near])
    sp = gy_swap(both)
    (nr,) = call(pick_body, [(32, 128)], [info], [near, sp])
    ready, _ = lax.optimization_barrier((out, sp))
    far = pair_swap(ready)
    fs = pair_swap(nr)

    wide, chip, flat = (24, TW), (16, TW), (16, AW)
    (coef, rain_w, static_w, land, ring, soil, lat, q, t, k16, edge) = call(
        first_body,
        [(5, 24, TW), wide, wide, chip, wide, chip, (8, 128), flat, flat, flat, (8, TW)],
        [info, u_wind, v_wind],
        [pairs[0], block, pin, out, far, sp, nr, fs],
        [(144, TW), wide],
    )
    outb = chip_swap(edge)
    farb = pair_swap(outb)
    depth, coarse, qf, own = call(
        second_body,
        [(TR, TC), (2, AC), (2, AC), (24, 128)],
        [info, u_wind, v_wind],
        [*pairs, coef, rain_w, static_w, land, ring, soil, lat, q, t, k16, outb, farb],
        [wide, chip, wide, flat, flat],
    )
    before = grp_shift(own)
    (chunks,) = call(chunks_body, [(16, 24, 128)], [info], [own, before])
    got = lax.all_to_all(chunks, "gx", 0, 0)
    (air_new,) = call(
        air_body,
        [(FL, 2, AC)],
        [info, u_wind, v_wind],
        [block, pin, out, far, k16, sp, nr, fs],
        [(5, 128, 128)],
    )
    air_new = air_new.at[Q0].set(qf)

    got, air_new = lax.optimization_barrier((got, air_new))
    (flow,) = call(
        route_body,
        [(1, LINKS)],
        [info],
        [own, got],
        [pltpu.VMEM((STEPS + 1, 2 * LINKS, LINKS), BF16)],
    )
    return (air_new.reshape(2, 32, 2, AC), depth, coarse, flow.reshape(LINKS))


def solution(mesh):
    placed = (
        P(None, None, ("grp", "gx"), "gy"),
        P(("grp", "gx"), "gy"),
        P(),
        P(),
        P(("grp", "gx"), "gy"),
        P(("grp", "gx"), "gy"),
        P(("grp", "gx"), "gy"),
        P(("grp", "gx"), "gy"),
        P(("grp", "gx"), "gy"),
        P(("grp", "gx"), "gy"),
        P(("grp", "gx"), "gy"),
        P(AXES),
        P(AXES),
        P(AXES),
    )
    return jax.shard_map(
        shards,
        mesh=mesh,
        in_specs=placed,
        out_specs=(
            P(None, None, ("grp", "gx"), "gy"),
            P(("grp", "gx"), "gy"),
            P(("grp", "gx"), "gy"),
            P(AXES),
        ),
        check_vma=False,
    )
```

time: 133 us -> 127 us (0.955); the launches traced: 130 us -> 126 us
  waiting for transfers between devices: 17.9 us -> 35.2 us
  starting transfers between devices: 77.2 us -> 64.1 us
  local copies, waits for them, and re-layouts: 17.2 us -> 4.41 us
  Pallas kernels: 14.7 us -> 21 us
  other arithmetic: 2.17 us -> 0.62 us
    ppermute x13 -> x9, waiting for transfers between devices: 12.5 us -> 28.6 us  [exchange(): return lax.ppermute(value, AXES, pairs)]
    ppermute x13 -> x9, starting transfers between devices: 67.4 us -> 54.2 us  [exchange(): return lax.ppermute(value, AXES, pairs)]
    unnamed x91 -> x24, local copies, waits for them, and re-layouts: 15 us -> 3.81 us
    pallas_call x5 -> x9, Pallas kernels: 14.7 us -> 21 us  [call(): pl.pallas_call(body, out_shape=[jax.ShapeDtypeStruct(o, F32) for o in out...]
  transfers between devices with their start and end apart: 14 -> 10, of which waited for: 6 -> 8; matrix products, arithmetic and copies ran while one was open for 3% -> 0% of each run, Pallas kernels for 6% -> 4%
where the time goes in v2:
time: 127 us; the launch traced here: 126 us
  starting transfers between devices  64.1 us (50%)
  waiting for transfers between devices  35.2 us (28%)
  Pallas kernels  21 us (17%)
  local copies, waits for them, and re-layouts  4.41 us (3%)
    ppermute x9, starting transfers between devices, exchange(): return lax.ppermute(value, AXES, pairs)  54.2 us
    ppermute x9, waiting for transfers between devices, exchange(): return lax.ppermute(value, AXES, pairs)  28.6 us
    pallas_call x9, Pallas kernels, call(): pl.pallas_call(body, out_shape=[jax.ShapeDtypeStruct(o, F32) for o in out...  21 us
    all_to_all x1, starting transfers between devices, shards(): got = lax.all_to_all(chunks, 'gx', 0, 0)  9.86 us
    all_to_all x1, waiting for transfers between devices, shards(): got = lax.all_to_all(chunks, 'gx', 0, 0)  6.6 us
    unnamed x24, local copies, waits for them, and re-layouts  3.81 us
  transfers between devices with their start and end apart: 10, of which 8 were waited for; matrix products, arithmetic and copies ran while one was open for 0% of the time, Pallas kernels for 4%

profile of v2, /device:TPU:7, one launch (start us, length us, event | category | flops | bytes accessed | tf_op | source)
XLA Modules:
  0.0 126.1 jit_solution(3510287970933442340)
XLA Ops:
  0.6 0.6 pad_add_fusion.info
  1.3 0.0 copy-start.6
  1.3 0.0 copy-start.7
  1.3 0.0 copy-start.8
  1.3 0.0 copy-start.9
  1.3 3.5 %shard_map.165.block = f32[104,3072]{1,0:T(8,128)} custom-call(s32[4]{0:T(128)} %pad_add_fusion.info, f32[64,2,768]{2,1,0:T(2,128)} %bitcast.17, f32[2,768]{1,0:T(2,128)} %kd.1, f32[8,3072]{1,0:T(8,128)} %elev.1, f32[8,3072]{1,0:T(8,128)} %cond.1, f32[8,3072]{1,0:T(8,128)} %rf.1, s32[8,3072]{1,0:T(8,128)} %mask.1, s32[8,3072]{1,0:T(8,128)} %code.1, ...), custom_call_target="tpu_custom_call" | custom-call | tf_op jit(solution)/shard_map/pallas_call | solution.py:79
  4.8 2.6 %collective-permute-start = (f32[104,3072]{1,0:T(8,128)}, f32[104,3072]{1,0:T(8,128)S(1)}, u32[]{:S(2)}, u32[]{:S(2)}) collective-permute-start(f32[104,3072]{1,0:T(8,128)} %shard_map.165.block), channel_id=1, source_target_pairs={{0,2},{1,3},{2,0},{3,1},{4,6},{5,7},{6,4},{7,5},{8,10},{9,11},{10,... | collective-permute-start | bytes 3833864 | tf_op jit(solution)/shard_map/ppermute | solution.py:36
  7.4 2.8 %collective-permute-done.pin = f32[104,3072]{1,0:T(8,128)S(1)} collective-permute-done((f32[104,3072]{1,0:T(8,128)}, f32[104,3072]{1,0:T(8,128)S(1)}, u32[]{:S(2)}, u32[]{:S(2)}) %collective-permute-start) | collective-permute-done | bytes 1277984 | tf_op jit(solution)/shard_map/ppermute | solution.py:36
  10.2 0.0 copy-done.6
  10.2 1.3 %copy-done = f32[104,3072]{1,0:T(8,128)S(1)} copy-done((f32[104,3072]{1,0:T(8,128)S(1)}, f32[104,3072]{1,0:T(8,128)}, u32[]{:S(2)}) %copy-start) | copy-done | bytes 1277976
  11.5 0.7 shard_map.166
  12.2 3.8 %collective-permute-start.1 = (f32[88,3072]{1,0:T(8,128)S(1)}, f32[88,3072]{1,0:T(8,128)S(1)}, u32[]{:S(2)}, u32[]{:S(2)}) collective-permute-start(f32[88,3072]{1,0:T(8,128)S(1)} %get-tuple-element.36), channel_id=1, source_target_pairs={{2,4},{3,5},{4,2},{5,3},{6,8},{7,9},{8,6},{9,7},{10,12},{11,13},{1... | collective-permute-start | bytes 3244040 | tf_op jit(solution)/shard_map/ppermute | solution.py:36
  16.0 1.9 %collective-permute-start.2 = (f32[32,128]{1,0:T(8,128)S(1)}, f32[32,128]{1,0:T(8,128)S(1)}, u32[]{:S(2)}, u32[]{:S(2)}) collective-permute-start(f32[32,128]{1,0:T(8,128)S(1)} %get-tuple-element.37.strips), channel_id=1, source_target_pairs={{2,4},{3,5},{4,2},{5,3},{6,8},{7,9},{8,6},{9,7},{10,12},{11,13},{1... | collective-permute-start | bytes 49160 | tf_op jit(solution)/shard_map/ppermute | solution.py:36
  17.9 14.8 %collective-permute-done.2.near = f32[32,128]{1,0:T(8,128)S(1)} collective-permute-done((f32[32,128]{1,0:T(8,128)S(1)}, f32[32,128]{1,0:T(8,128)S(1)}, u32[]{:S(2)}, u32[]{:S(2)}) %collective-permute-start.2) | collective-permute-done | bytes 16416 | tf_op jit(solution)/shard_map/ppermute | solution.py:36
  32.8 16.2 %collective-permute-start.3 = (f32[64,128]{1,0:T(8,128)S(1)}, f32[64,128]{1,0:T(8,128)S(1)}, u32[]{:S(2)}, u32[]{:S(2)}) collective-permute-start(f32[64,128]{1,0:T(8,128)S(1)} %shard_map.167), channel_id=1, source_target_pairs={{0,1},{1,0},{2,3},{3,2},{4,5},{5,4},{6,7},{7,6},{8,9},{9,8},{10,11... | collective-permute-start | bytes 98312 | tf_op jit(solution)/shard_map/ppermute | solution.py:36
  49.0 2.0 %collective-permute-done.3.across.sp = f32[64,128]{1,0:T(8,128)S(1)} collective-permute-done((f32[64,128]{1,0:T(8,128)S(1)}, f32[64,128]{1,0:T(8,128)S(1)}, u32[]{:S(2)}, u32[]{:S(2)}) %collective-permute-start.3) | collective-permute-done | bytes 32800 | tf_op jit(solution)/shard_map/ppermute | solution.py:36
  51.0 0.0 collective-permute-done.1.out
  51.0 5.3 %collective-permute-start.4 = (f32[88,3072]{1,0:T(8,128)S(1)}, f32[88,3072]{1,0:T(8,128)S(1)}, u32[]{:S(2)}, u32[]{:S(2)}) collective-permute-start(f32[88,3072]{1,0:T(8,128)S(1)} %collective-permute-done.1.out), channel_id=1, source_target_pairs={{0,2},{1,3},{2,0},{3,1},{4,6},{5,7},{6,4},{7,5},{8,10},{9,11},{10,... | collective-permute-start | bytes 3244040 | tf_op jit(solution)/shard_map/ppermute | solution.py:36
  56.3 0.5 shard_map.168.nr
  56.9 1.9 %collective-permute-start.5 = (f32[32,128]{1,0:T(8,128)S(1)}, f32[32,128]{1,0:T(8,128)S(1)}, u32[]{:S(2)}, u32[]{:S(2)}) collective-permute-start(f32[32,128]{1,0:T(8,128)S(1)} %shard_map.168.nr), channel_id=1, source_target_pairs={{0,2},{1,3},{2,0},{3,1},{4,6},{5,7},{6,4},{7,5},{8,10},{9,11},{10,... | collective-permute-start | bytes 49160 | tf_op jit(solution)/shard_map/ppermute | solution.py:36
  58.8 1.1 collective-permute-done.5.fs
  60.0 0.0 collective-permute-done.4.far
  60.0 0.0 copy-done.7
  60.0 0.0 copy-done.8
  60.0 0.0 copy-done.9
  60.0 0.0 copy-done.1
  60.0 0.0 copy-start.10
  60.0 0.0 copy-start.11
  60.0 3.3 %shard_map.169 = (f32[5,24,3200]{2,1,0:T(8,128)S(1)}, f32[24,3200]{1,0:T(8,128)S(1)}, f32[24,3200]{1,0:T(8,128)S(1)}, f32[16,3200]{1,0:T(8,128)S(1)}, f32[24,320...) custom-call(s32[4]{0:T(128)S(1)} %copy-done.6, ...), custom_call_target="tpu_custom_call" | custom-call | tf_op jit(solution)/shard_map/pallas_call | solution.py:79
  63.3 0.0 copy-done.2
  63.3 0.0 copy-done.4
  63.3 5.6 %collective-permute-start.6 = (f32[8,3200]{1,0:T(8,128)S(1)}, f32[8,3200]{1,0:T(8,128)S(1)}, u32[]{:S(2)}, u32[]{:S(2)}) collective-permute-start(f32[8,3200]{1,0:T(8,128)S(1)} %get-tuple-element.49), channel_id=1, source_target_pairs={{2,4},{3,5},{4,2},{5,3},{6,8},{7,9},{8,6},{9,7},{10,12},{11,13},{1... | collective-permute-start | bytes 307208 | tf_op jit(solution)/shard_map/ppermute | solution.py:36
  69.0 2.3 %collective-permute-done.6.out = f32[8,3200]{1,0:T(8,128)S(1)} collective-permute-done((f32[8,3200]{1,0:T(8,128)S(1)}, f32[8,3200]{1,0:T(8,128)S(1)}, u32[]{:S(2)}, u32[]{:S(2)}) %collective-permute-start.6) | collective-permute-done | bytes 102432 | tf_op jit(solution)/shard_map/ppermute | solution.py:36
  71.3 14.9 %collective-permute-start.7 = (f32[8,3200]{1,0:T(8,128)S(1)}, f32[8,3200]{1,0:T(8,128)S(1)}, u32[]{:S(2)}, u32[]{:S(2)}) collective-permute-start(f32[8,3200]{1,0:T(8,128)S(1)} %collective-permute-done.6.out), channel_id=1, source_target_pairs={{0,2},{1,3},{2,0},{3,1},{4,6},{5,7},{6,4},{7,5},{8,10},{9,11},{10,... | collective-permute-start | bytes 307208 | tf_op jit(solution)/shard_map/ppermute | solution.py:36
  86.2 0.9 collective-permute-done.7.far
  87.1 0.0 copy-done.10
  87.1 0.0 copy-done.11
  87.1 2.9 %shard_map.170 = (f32[8,3072]{1,0:T(8,128)}, f32[2,768]{1,0:T(2,128)}, f32[2,768]{1,0:T(2,128)S(1)}, f32[24,128]{1,0:T(8,128)S(1)}) custom-call(s32[4]{0:T(128)S(1)} %copy-done.6, f32[32]{0:T(128)S(1)} %copy-done.7, f32[32]{0:T(128)S(1)} %copy-done.8, s32[2,128]{1,0:T(2,128)S(1)} %bitcast.13, f32[2,128]{1,0:T(2,128)S(1)} %bitcast.14, s32[2,128]{1,0:T(2,128)S(1)} %bitcast.15, ...), custom_call_target="tpu_custom_call" | custom-call | tf_op jit(solution)/shard_map/pallas_call | solution.py:79
  90.0 1.9 %collective-permute-start.8 = (f32[24,128]{1,0:T(8,128)S(1)}, f32[24,128]{1,0:T(8,128)S(1)}, u32[]{:S(2)}, u32[]{:S(2)}) collective-permute-start(f32[24,128]{1,0:T(8,128)S(1)} %get-tuple-element.50.own), channel_id=1, source_target_pairs={{0,32},{1,33},{2,34},{3,35},{4,36},{5,37},{6,38},{7,39},{8,40},{9,... | collective-permute-start | bytes 36872 | tf_op jit(solution)/shard_map/ppermute | solution.py:36
  91.9 4.6 %collective-permute-done.8.before = f32[24,128]{1,0:T(8,128)S(1)} collective-permute-done((f32[24,128]{1,0:T(8,128)S(1)}, f32[24,128]{1,0:T(8,128)S(1)}, u32[]{:S(2)}, u32[]{:S(2)}) %collective-permute-start.8) | collective-permute-done | bytes 12320 | tf_op jit(solution)/shard_map/ppermute | solution.py:36
  96.6 1.2 shard_map.171
  97.8 9.9 %all-to-all-start = ((f32[16,24,128]{2,1,0:T(8,128)}), f32[16,24,128]{2,1,0:T(8,128)S(1)}, u32[]{:S(2)}, u32[]{:S(2)}) async-start(f32[16,24,128]{2,1,0:T(8,128)} %shard_map.171), calls=%async_computation | async-start | bytes 393216 | tf_op jit(solution)/shard_map/all_to_all | solution.py:619
  107.7 1.2 copy-done.3
  108.9 1.2 copy-done.5
  110.1 5.0 %shard_map.172 = f32[64,2,768]{2,1,0:T(2,128)} custom-call(s32[4]{0:T(128)S(1)} %copy-done.6, f32[32]{0:T(128)S(1)} %copy-done.7, f32[32]{0:T(128)S(1)} %copy-done.8, f32[104,3072]{1,0:T(8,128)S(1)} %copy-done.1, f32[104,3072]{1,0:T(8,128)S(1)} %collective-permute-done.pin, f32[88,3072]{1,0:T(8,128)S(1)} %copy-done.3, f32[88,3072]{1,0:T(8,128)S(1)} %copy-done.5, ...), custom_call_target="tpu_custom_call" | custom-call | tf_op jit(solution)/shard_map/pallas_call | solution.py:79
  115.1 0.6 bitcast_dynamic-update-slice_fusion
  115.7 6.6 %all-to-all-done.got = f32[16,24,128]{2,1,0:T(8,128)S(1)} async-done(((f32[16,24,128]{2,1,0:T(8,128)}), f32[16,24,128]{2,1,0:T(8,128)S(1)}, u32[]{:S(2)}, u32[]{:S(2)}) %all-to-all-start) | async-done | bytes 196640 | tf_op jit(solution)/shard_map/all_to_all | solution.py:619
  122.3 3.8 %shard_map.173 = f32[1,256]{1,0:T(1,128)} custom-call(s32[4]{0:T(128)S(1)} %copy-done.6, f32[24,128]{1,0:T(8,128)S(1)} %get-tuple-element.50.own, f32[16,24,128]{2,1,0:T(8,128)S(1)} %all-to-all-done.got), custom_call_target="tpu_custom_call" | custom-call | tf_op jit(solution)/shard_map/pallas_call | solution.py:79
  (7 shorter events, 0.0 us)
Async XLA Ops:
  1.3 8.9 %copy-start.6 = (s32[4]{0:T(128)S(1)}, s32[4]{0:T(128)}, u32[]{:S(2)}) copy-start(s32[4]{0:T(128)} %pad_add_fusion.info) | copy-start | bytes 52
  1.3 58.7 %copy-start.7 = (f32[32]{0:T(128)S(1)}, f32[32]{0:T(128)}, u32[]{:S(2)}) copy-start(f32[32]{0:T(128)} %u.5) | copy-start | bytes 388
  1.3 58.7 %copy-start.8 = (f32[32]{0:T(128)S(1)}, f32[32]{0:T(128)}, u32[]{:S(2)}) copy-start(f32[32]{0:T(128)} %v.5) | copy-start | bytes 388
  1.3 58.7 %copy-start.9 = (s32[256]{0:T(256)S(1)}, s32[256]{0:T(256)}, u32[]{:S(2)}) copy-start(s32[256]{0:T(256)} %param.27) | copy-start | bytes 3076
  4.8 5.4 %collective-permute-start = (f32[104,3072]{1,0:T(8,128)}, f32[104,3072]{1,0:T(8,128)S(1)}, u32[]{:S(2)}, u32[]{:S(2)}) collective-permute-start(f32[104,3072]{1,0:T(8,128)} %shard_map.165.block), channel_id=1, source_target_pairs={{0,2},{1,3},{2,0},{3,1},{4,6},{5,7},{6,4},{7,5},{8,10},{9,11},{10,... | collective-permute-start | bytes 3833864 | tf_op jit(solution)/shard_map/ppermute | solution.py:36
  10.2 1.3 %copy-start = (f32[104,3072]{1,0:T(8,128)S(1)}, f32[104,3072]{1,0:T(8,128)}, u32[]{:S(2)}) copy-start(f32[104,3072]{1,0:T(8,128)} %shard_map.165.block) | copy-start | bytes 3833860
  11.5 48.5 %copy-start.1 = (f32[104,3072]{1,0:T(8,128)S(1)}, f32[104,3072]{1,0:T(8,128)}, u32[]{:S(2)}) copy-start(f32[104,3072]{1,0:T(8,128)} %shard_map.165.block) | copy-start | bytes 3833860
  12.2 38.8 %collective-permute-start.1 = (f32[88,3072]{1,0:T(8,128)S(1)}, f32[88,3072]{1,0:T(8,128)S(1)}, u32[]{:S(2)}, u32[]{:S(2)}) collective-permute-start(f32[88,3072]{1,0:T(8,128)S(1)} %get-tuple-element.36), channel_id=1, source_target_pairs={{2,4},{3,5},{4,2},{5,3},{6,8},{7,9},{8,6},{9,7},{10,12},{11,13},{1... | collective-permute-start | bytes 3244040 | tf_op jit(solution)/shard_map/ppermute | solution.py:36
  16.0 16.7 %collective-permute-start.2 = (f32[32,128]{1,0:T(8,128)S(1)}, f32[32,128]{1,0:T(8,128)S(1)}, u32[]{:S(2)}, u32[]{:S(2)}) collective-permute-start(f32[32,128]{1,0:T(8,128)S(1)} %get-tuple-element.37.strips), channel_id=1, source_target_pairs={{2,4},{3,5},{4,2},{5,3},{6,8},{7,9},{8,6},{9,7},{10,12},{11,13},{1... | collective-permute-start | bytes 49160 | tf_op jit(solution)/shard_map/ppermute | solution.py:36
  32.8 18.2 %collective-permute-start.3 = (f32[64,128]{1,0:T(8,128)S(1)}, f32[64,128]{1,0:T(8,128)S(1)}, u32[]{:S(2)}, u32[]{:S(2)}) collective-permute-start(f32[64,128]{1,0:T(8,128)S(1)} %shard_map.167), channel_id=1, source_target_pairs={{0,1},{1,0},{2,3},{3,2},{4,5},{5,4},{6,7},{7,6},{8,9},{9,8},{10,11... | collective-permute-start | bytes 98312 | tf_op jit(solution)/shard_map/ppermute | solution.py:36
  51.0 12.3 %copy-start.2 = (f32[88,3072]{1,0:T(8,128)}, f32[88,3072]{1,0:T(8,128)S(1)}, u32[]{:S(2)}) copy-start(f32[88,3072]{1,0:T(8,128)S(1)} %collective-permute-done.1.out) | copy-start | bytes 3244036
  51.0 9.0 %collective-permute-start.4 = (f32[88,3072]{1,0:T(8,128)S(1)}, f32[88,3072]{1,0:T(8,128)S(1)}, u32[]{:S(2)}, u32[]{:S(2)}) collective-permute-start(f32[88,3072]{1,0:T(8,128)S(1)} %collective-permute-done.1.out), channel_id=1, source_target_pairs={{0,2},{1,3},{2,0},{3,1},{4,6},{5,7},{6,4},{7,5},{8,10},{9,11},{10,... | collective-permute-start | bytes 3244040 | tf_op jit(solution)/shard_map/ppermute | solution.py:36
  56.9 3.1 %collective-permute-start.5 = (f32[32,128]{1,0:T(8,128)S(1)}, f32[32,128]{1,0:T(8,128)S(1)}, u32[]{:S(2)}, u32[]{:S(2)}) collective-permute-start(f32[32,128]{1,0:T(8,128)S(1)} %shard_map.168.nr), channel_id=1, source_target_pairs={{0,2},{1,3},{2,0},{3,1},{4,6},{5,7},{6,4},{7,5},{8,10},{9,11},{10,... | collective-permute-start | bytes 49160 | tf_op jit(solution)/shard_map/ppermute | solution.py:36
  60.0 3.4 %copy-start.4 = (f32[88,3072]{1,0:T(8,128)}, f32[88,3072]{1,0:T(8,128)S(1)}, u32[]{:S(2)}) copy-start(f32[88,3072]{1,0:T(8,128)S(1)} %collective-permute-done.4.far) | copy-start | bytes 3244036
  60.0 27.1 %copy-start.10 = (f32[256]{0:T(256)S(1)}, f32[256]{0:T(256)}, u32[]{:S(2)}) copy-start(f32[256]{0:T(256)} %param.29) | copy-start | bytes 3076
  60.0 27.1 %copy-start.11 = (s32[256]{0:T(256)S(1)}, s32[256]{0:T(256)}, u32[]{:S(2)}) copy-start(s32[256]{0:T(256)} %param.28) | copy-start | bytes 3076
  63.3 8.0 %collective-permute-start.6 = (f32[8,3200]{1,0:T(8,128)S(1)}, f32[8,3200]{1,0:T(8,128)S(1)}, u32[]{:S(2)}, u32[]{:S(2)}) collective-permute-start(f32[8,3200]{1,0:T(8,128)S(1)} %get-tuple-element.49), channel_id=1, source_target_pairs={{2,4},{3,5},{4,2},{5,3},{6,8},{7,9},{8,6},{9,7},{10,12},{11,13},{1... | collective-permute-start | bytes 307208 | tf_op jit(solution)/shard_map/ppermute | solution.py:36
  71.3 15.8 %collective-permute-start.7 = (f32[8,3200]{1,0:T(8,128)S(1)}, f32[8,3200]{1,0:T(8,128)S(1)}, u32[]{:S(2)}, u32[]{:S(2)}) collective-permute-start(f32[8,3200]{1,0:T(8,128)S(1)} %collective-permute-done.6.out), channel_id=1, source_target_pairs={{0,2},{1,3},{2,0},{3,1},{4,6},{5,7},{6,4},{7,5},{8,10},{9,11},{10,... | collective-permute-start | bytes 307208 | tf_op jit(solution)/shard_map/ppermute | solution.py:36
  90.0 6.5 %collective-permute-start.8 = (f32[24,128]{1,0:T(8,128)S(1)}, f32[24,128]{1,0:T(8,128)S(1)}, u32[]{:S(2)}, u32[]{:S(2)}) collective-permute-start(f32[24,128]{1,0:T(8,128)S(1)} %get-tuple-element.50.own), channel_id=1, source_target_pairs={{0,32},{1,33},{2,34},{3,35},{4,36},{5,37},{6,38},{7,39},{8,40},{9,... | collective-permute-start | bytes 36872 | tf_op jit(solution)/shard_map/ppermute | solution.py:36
  97.8 24.5 %all-to-all-start = ((f32[16,24,128]{2,1,0:T(8,128)}), f32[16,24,128]{2,1,0:T(8,128)S(1)}, u32[]{:S(2)}, u32[]{:S(2)}) async-start(f32[16,24,128]{2,1,0:T(8,128)} %shard_map.171), calls=%async_computation | async-start | bytes 393216 | tf_op jit(solution)/shard_map/all_to_all | solution.py:619
  107.7 1.2 copy-start.3
  108.9 1.2 copy-start.5

commit v3 on v2

--- a/solution.py
+++ b/solution.py
@@ -86,23 +86,23 @@
     )(*scalars, *arrays)
 
 
-BLOCK, EDGE = 104, 88
+BLOCK, EDGE = 104, 56
 ELEV, COND, RAIN, MASK, CODE, DEPTH, SOIL = range(7)
 EDGES = ((ELEV, 0, 4), (COND, 12, 3), (RAIN, 15, 3), (MASK, 18, 3), (CODE, 4, 4), (DEPTH, 8, 4))
 
 
 def pack_body(
-    info, air, kd, elev, cond, rf, mask, code, depth, soil,
+    info, air, kd, elev, cond, rf, mask, code, depth, soil, links,
     block_h,
-    air_v, kd_v, elev_v, cond_v, rf_v, mask_v, code_v, depth_v, soil_v,
+    links_v, air_v, kd_v, elev_v, cond_v, rf_v, mask_v, code_v, depth_v, soil_v,
     block, sems, sent,
 ):
     right = info[1] == 1
-    near = (kd_v, elev_v, cond_v, rf_v, mask_v, code_v, depth_v, soil_v, air_v)
+    near = (kd_v, elev_v, cond_v, rf_v, mask_v, code_v, depth_v, soil_v, air_v, links_v)
     copies = [
         pltpu.make_async_copy(src, dst, sems.at[i])
         for i, (src, dst) in enumerate(
-            zip((kd, elev, cond, rf, mask, code, depth, soil, air), near)
+            zip((kd, elev, cond, rf, mask, code, depth, soil, air, links), near)
         )
     ]
     for c in copies:
@@ -112,6 +112,7 @@
         c.wait()
     for i, ref in enumerate((elev_v, cond_v, rf_v, mask_v, code_v, depth_v, soil_v)):
         block[8 * i : 8 * i + 8, :] = ref[...].astype(F32)
+    block[58:59, 0:LINKS] = links_v[...]
     ends = []
     for r in range(2):
         rows = air_v[:, r, :]
@@ -141,15 +142,12 @@
         top = block[8 * i : 8 * i + n, :]
         low = block[8 * i + 8 - n : 8 * i + 8, :]
         out[off : off + n, :] = jnp.where(odd, low, top)
-    out[21:23, :] = block[56:58, :]
-    out[23:24, :] = jnp.zeros((1, TC), F32)
+    out[21:24, :] = block[56:59, :]
     for i in range(2):
         a = pin[56 + i : 57 + i, AC : 2 * AC]
         b = pin[56 + i : 57 + i, 0:AC]
         out[22:23, (2 + i) * AC : (3 + i) * AC] = jnp.where(odd, a, b)
-        lo, half = 24 + 32 * i, slice(2 * i * AC, 2 * (i + 1) * AC)
-        out[lo : lo + 32, 0 : 2 * AC] = block[72:104, half]
-        out[lo : lo + 32, 2 * AC : TC] = pin[72:104, half]
+    out[24:56, :] = block[72:104, :]
     lane = lax.broadcasted_iota(jnp.int32, (8, 128), 1)
     for b in range(2):
         at = slice(b * 128, (b + 1) * 128)
@@ -159,6 +157,10 @@
     strips[24:32, :] = pin[64:72, 256:384]
 
 
+def pair_air_body(edge, pin, out):
+    out[...] = pin[72:104, :]
+
+
 def both_body(strips, near, out):
     out[0:32, :] = strips[...]
     out[32:64, :] = near[...]
@@ -171,7 +173,10 @@
 
 def chunks_body(info, own, before, out):
     for i in range(16):
-        out[i] = jnp.where(info[3] < i, own[...], before[...])
+        src = jnp.where(info[3] < i, own[...], before[...])
+        out[i, 0:12, :] = src[0:12]
+        out[i, 12:14, :] = jnp.where(info[3] == (i + 15) % 16, src[12:14], src[16:18])
+        out[i, 14:16, :] = src[18:20]
 
 
 def land_strip(strip, right):
@@ -307,7 +312,7 @@
 
 def first_body(
     info, u, v, cells, block, pin, out, far, sp, nr, fs,
-    coef, rain_w, static_w, land, ring, soil, lat, q_out, t_out, k_out, edge,
+    coef, rain_w, static_w, land, ring, soil, lat, q_out, t_out, k_out, edge, above,
     grid, rq,
 ):
     odd = info[0] == 1
@@ -403,6 +408,9 @@
     for _ in range(ASTEPS):
         q = ring_step(q, k, m8, hu_t, hv_t)
         t = ring_step(t, k, m8, hu_t, hv_t)
+    for h in range(2):
+        at = slice(128 * h, 128 * h + 128)
+        above[h : h + 1, :] = jnp.where(odd, pin[58:59, at], out[23:24, at])
     rain, q = rain_of(q)
     rq[...] = static_w[...] + rain_w[...] * spread_rows(spread_columns(rain, right))
     lat[...] = jnp.zeros_like(lat)
@@ -464,7 +472,7 @@
 
 
 def air_body(
-    info, u, v, block, pin, out, far, k16, sp, nr, fs,
+    info, u, v, block, pin, out, second, far, k16, sp, nr, fs,
     air_out,
     strips,
 ):
@@ -484,7 +492,7 @@
     def group(half, g):
         at = pl.multiple_of(g * 8, 8)
         own8 = pl.ds(72 + at, 8)
-        out8 = pl.ds(24 + 32 * half + at, 8)
+        out8 = pl.ds(24 + at, 8)
 
         def whole(ref, rows, lane, strip, i):
             side = strips[strip, pl.ds(32 * half + i * FL + at, 8), :]
@@ -492,9 +500,9 @@
 
         x = {i: whole(block, own8, 2 * half + i, 0, i) for i in range(2)}
         p = [whole(pin, own8, 2 * half + i, 1, i) for i in range(2)]
-        o = [whole(out, out8, i, 2, i) for i in range(2)]
-        o2 = [whole(out, out8, 2 + i, 3, i) for i in range(2)]
-        f = [whole(far, out8, i, 4, i) for i in range(2)]
+        o = [whole(out, out8, 2 * half + i, 2, i) for i in range(2)]
+        o2 = [whole(second, pl.ds(at, 8), 2 * half + i, 3, i) for i in range(2)]
+        f = [whole(far, out8, 2 * half + i, 4, i) for i in range(2)]
         for i in range(2):
             x[2 + i] = jnp.where(odd, o[i], p[i])
             x[4 + i] = jnp.where(odd, o2[i], f[i])
@@ -524,7 +532,7 @@
         lax.fori_loop(0, 4, lambda g, c, half=half: (group(half, g), c)[1], 0)
 
 
-def route_body(info, own, got, flow_out, hot):
+def route_body(info, own, got, above, flow_out, hot):
     j = info[3]
     target = lax.broadcasted_iota(jnp.int32, (2 * LINKS, LINKS), 0).astype(F32)
     data = [own[...]] + [got[lax.rem(j - k + 16, 16)] for k in range(1, STEPS + 1)]
@@ -532,9 +540,9 @@
     def wide(d, i):
         return jnp.concatenate([d[2 * i : 2 * i + 1, :], d[2 * i + 1 : 2 * i + 2, :]], axis=1)
 
-    flow = [wide(d, 8) for d in data]
+    flow = [wide(own[...], 8), wide(above[...], 0)] + [wide(d, 6) for d in data[2:]]
     for k in range(STEPS + 1):
-        hot[k] = jnp.where(target == wide(data[k], 9), 1.0, 0.0).astype(BF16)
+        hot[k] = jnp.where(target == wide(data[k], 7 if k else 9), 1.0, 0.0).astype(BF16)
     for t in range(STEPS):
         routed = []
         for k in range(STEPS - t + 1):
@@ -580,9 +588,10 @@
         pack_body,
         [(BLOCK, TC)],
         [info],
-        [air.reshape(FL, 2, AC), kdiff, elev, cond, rain_factor, land_mask, flow_code, depth_init, soil_init],
-        [(FL, 2, AC), (2, AC), land_v, land_v, land_v, code_v, code_v, land_v, land_v, (BLOCK, TC),
-         pltpu.SemaphoreType.DMA((9,)), pltpu.SemaphoreType.DMA],
+        [air.reshape(FL, 2, AC), kdiff, elev, cond, rain_factor, land_mask, flow_code, depth_init, soil_init,
+         link_flow.reshape(1, LINKS)],
+        [(1, LINKS), (FL, 2, AC), (2, AC), land_v, land_v, land_v, code_v, code_v, land_v, land_v, (BLOCK, TC),
+         pltpu.SemaphoreType.DMA((10,)), pltpu.SemaphoreType.DMA],
         limit=WHOLE,
         far=1,
     )
@@ -598,14 +607,16 @@
     fs = pair_swap(nr)
 
     wide, chip, flat = (24, TW), (16, TW), (16, AW)
-    (coef, rain_w, static_w, land, ring, soil, lat, q, t, k16, edge) = call(
+    (coef, rain_w, static_w, land, ring, soil, lat, q, t, k16, edge, above) = call(
         first_body,
-        [(5, 24, TW), wide, wide, chip, wide, chip, (8, 128), flat, flat, flat, (8, TW)],
+        [(5, 24, TW), wide, wide, chip, wide, chip, (8, 128), flat, flat, flat, (8, TW), (2, 128)],
         [info, u_wind, v_wind],
         [pairs[0], block, pin, out, far, sp, nr, fs],
         [(144, TW), wide],
     )
     outb = chip_swap(edge)
+    (second,) = call(pair_air_body, [(32, TC)], [], [edge, pin])
+    second = chip_swap(second)
     farb = pair_swap(outb)
     depth, coarse, qf, own = call(
         second_body,
@@ -615,13 +626,13 @@
         [wide, chip, wide, flat, flat],
     )
     before = grp_shift(own)
-    (chunks,) = call(chunks_body, [(16, 24, 128)], [info], [own, before])
+    (chunks,) = call(chunks_body, [(16, 16, 128)], [info], [own, before])
     got = lax.all_to_all(chunks, "gx", 0, 0)
     (air_new,) = call(
         air_body,
         [(FL, 2, AC)],
         [info, u_wind, v_wind],
-        [block, pin, out, far, k16, sp, nr, fs],
+        [block, pin, out, second, far, k16, sp, nr, fs],
         [(5, 128, 128)],
     )
     air_new = air_new.at[Q0].set(qf)
@@ -631,7 +642,7 @@
         route_body,
         [(1, LINKS)],
         [info],
-        [own, got],
+        [own, got, above],
         [pltpu.VMEM((STEPS + 1, 2 * LINKS, LINKS), BF16)],
     )
     return (air_new.reshape(2, 32, 2, AC), depth, coarse, flow.reshape(LINKS))

time: 127 us -> 116 us (0.913)
  waiting for transfers between devices: 35.2 us -> 25.8 us
  Pallas kernels: 21 us -> 22.5 us
  local copies, waits for them, and re-layouts: 4.41 us -> 3.03 us
    ppermute x9 -> x10, waiting for transfers between devices: 28.6 us -> 21 us  [exchange(): return lax.ppermute(value, AXES, pairs)]
    all_to_all x1, starting transfers between devices: 9.86 us -> 6.35 us  [shards(): got = lax.all_to_all(chunks, 'gx', 0, 0)]
    ppermute x9 -> x10, starting transfers between devices: 54.2 us -> 56.6 us  [exchange(): return lax.ppermute(value, AXES, pairs)]
    all_to_all x1, waiting for transfers between devices: 6.6 us -> 4.84 us  [shards(): got = lax.all_to_all(chunks, 'gx', 0, 0)]
    pallas_call x9 -> x10, Pallas kernels: 21 us -> 22.5 us  [call(): pl.pallas_call(body, out_shape=[jax.ShapeDtypeStruct(o, F32) for o in out...]
    unnamed x24 -> x20, local copies, waits for them, and re-layouts: 3.81 us -> 2.43 us
  transfers between devices with their start and end apart: 10 -> 11, of which waited for: 8 -> 7; matrix products, arithmetic and copies ran while one was open for 0% -> 1% of each run, Pallas kernels for 4% -> 10%
where the time goes in v3:
time: 116 us
  starting transfers between devices  62.9 us (54%)
  waiting for transfers between devices  25.8 us (22%)
  Pallas kernels  22.5 us (19%)
  local copies, waits for them, and re-layouts  3.03 us (3%)
    ppermute x10, starting transfers between devices, exchange(): return lax.ppermute(value, AXES, pairs)  56.6 us
    pallas_call x10, Pallas kernels, call(): pl.pallas_call(body, out_shape=[jax.ShapeDtypeStruct(o, F32) for o in out...  22.5 us
    ppermute x10, waiting for transfers between devices, exchange(): return lax.ppermute(value, AXES, pairs)  21 us
    all_to_all x1, starting transfers between devices, shards(): got = lax.all_to_all(chunks, 'gx', 0, 0)  6.35 us
    all_to_all x1, waiting for transfers between devices, shards(): got = lax.all_to_all(chunks, 'gx', 0, 0)  4.84 us
    unnamed x20, local copies, waits for them, and re-layouts  2.43 us
  transfers between devices with their start and end apart: 11, of which 7 were waited for; matrix products, arithmetic and copies ran while one was open for 1% of the time, Pallas kernels for 10%

profile of v3, /device:TPU:7, one launch (start us, length us, event | category | flops | bytes accessed | tf_op | source)
XLA Modules:
  0.0 115.8 jit_solution(907755428479947693)
XLA Ops:
  0.6 0.7 pad_add_fusion.info
  1.3 0.0 copy-start.4
  1.3 0.0 copy-start.5
  1.3 3.5 %shard_map.165.block = f32[104,3072]{1,0:T(8,128)} custom-call(s32[4]{0:T(128)} %pad_add_fusion.info, f32[64,2,768]{2,1,0:T(2,128)} %bitcast.19, f32[2,768]{1,0:T(2,128)} %kd.1, f32[8,3072]{1,0:T(8,128)} %elev.1, f32[8,3072]{1,0:T(8,128)} %cond.1, f32[8,3072]{1,0:T(8,128)} %rf.1, s32[8,3072]{1,0:T(8,128)} %mask.1, s32[8,3072]{1,0:T(8,128)} %code.1, ...), custom_call_target="tpu_custom_call" | custom-call | tf_op jit(solution)/shard_map/pallas_call | solution.py:79
  4.8 2.6 %collective-permute-start = (f32[104,3072]{1,0:T(8,128)}, f32[104,3072]{1,0:T(8,128)S(1)}, u32[]{:S(2)}, u32[]{:S(2)}) collective-permute-start(f32[104,3072]{1,0:T(8,128)} %shard_map.165.block), channel_id=1, source_target_pairs={{0,2},{1,3},{2,0},{3,1},{4,6},{5,7},{6,4},{7,5},{8,10},{9,11},{10,... | collective-permute-start | bytes 3833864 | tf_op jit(solution)/shard_map/ppermute | solution.py:36
  7.4 2.8 %collective-permute-done.pin = f32[104,3072]{1,0:T(8,128)S(1)} collective-permute-done((f32[104,3072]{1,0:T(8,128)}, f32[104,3072]{1,0:T(8,128)S(1)}, u32[]{:S(2)}, u32[]{:S(2)}) %collective-permute-start) | collective-permute-done | bytes 1277984 | tf_op jit(solution)/shard_map/ppermute | solution.py:36
  10.2 0.0 copy-done.4
  10.2 1.3 %copy-done = f32[104,3072]{1,0:T(8,128)S(1)} copy-done((f32[104,3072]{1,0:T(8,128)S(1)}, f32[104,3072]{1,0:T(8,128)}, u32[]{:S(2)}) %copy-start) | copy-done | bytes 1277976
  11.5 0.7 shard_map.166
  12.2 3.8 %collective-permute-start.1 = (f32[56,3072]{1,0:T(8,128)S(1)}, f32[56,3072]{1,0:T(8,128)S(1)}, u32[]{:S(2)}, u32[]{:S(2)}) collective-permute-start(f32[56,3072]{1,0:T(8,128)S(1)} %get-tuple-element.37), channel_id=1, source_target_pairs={{2,4},{3,5},{4,2},{5,3},{6,8},{7,9},{8,6},{9,7},{10,12},{11,13},{1... | collective-permute-start | bytes 2064392 | tf_op jit(solution)/shard_map/ppermute | solution.py:36
  16.0 1.9 %collective-permute-start.2 = (f32[32,128]{1,0:T(8,128)S(1)}, f32[32,128]{1,0:T(8,128)S(1)}, u32[]{:S(2)}, u32[]{:S(2)}) collective-permute-start(f32[32,128]{1,0:T(8,128)S(1)} %get-tuple-element.38.strips), channel_id=1, source_target_pairs={{2,4},{3,5},{4,2},{5,3},{6,8},{7,9},{8,6},{9,7},{10,12},{11,13},{1... | collective-permute-start | bytes 49160 | tf_op jit(solution)/shard_map/ppermute | solution.py:36
  18.0 6.9 %collective-permute-done.2.near = f32[32,128]{1,0:T(8,128)S(1)} collective-permute-done((f32[32,128]{1,0:T(8,128)S(1)}, f32[32,128]{1,0:T(8,128)S(1)}, u32[]{:S(2)}, u32[]{:S(2)}) %collective-permute-start.2) | collective-permute-done | bytes 16416 | tf_op jit(solution)/shard_map/ppermute | solution.py:36
  24.8 15.5 %collective-permute-start.3 = (f32[64,128]{1,0:T(8,128)S(1)}, f32[64,128]{1,0:T(8,128)S(1)}, u32[]{:S(2)}, u32[]{:S(2)}) collective-permute-start(f32[64,128]{1,0:T(8,128)S(1)} %shard_map.167), channel_id=1, source_target_pairs={{0,1},{1,0},{2,3},{3,2},{4,5},{5,4},{6,7},{7,6},{8,9},{9,8},{10,11... | collective-permute-start | bytes 98312 | tf_op jit(solution)/shard_map/ppermute | solution.py:36
  40.3 2.0 %collective-permute-done.3.across.sp = f32[64,128]{1,0:T(8,128)S(1)} collective-permute-done((f32[64,128]{1,0:T(8,128)S(1)}, f32[64,128]{1,0:T(8,128)S(1)}, u32[]{:S(2)}, u32[]{:S(2)}) %collective-permute-start.3) | collective-permute-done | bytes 32800 | tf_op jit(solution)/shard_map/ppermute | solution.py:36
  42.3 0.0 collective-permute-done.1.out
  42.3 11.7 %collective-permute-start.4 = (f32[56,3072]{1,0:T(8,128)S(1)}, f32[56,3072]{1,0:T(8,128)S(1)}, u32[]{:S(2)}, u32[]{:S(2)}) collective-permute-start(f32[56,3072]{1,0:T(8,128)S(1)} %collective-permute-done.1.out), channel_id=1, source_target_pairs={{0,2},{1,3},{2,0},{3,1},{4,6},{5,7},{6,4},{7,5},{8,10},{9,11},{10,... | collective-permute-start | bytes 2064392 | tf_op jit(solution)/shard_map/ppermute | solution.py:36
  54.0 0.5 shard_map.168.nr
  54.6 1.9 %collective-permute-start.5 = (f32[32,128]{1,0:T(8,128)S(1)}, f32[32,128]{1,0:T(8,128)S(1)}, u32[]{:S(2)}, u32[]{:S(2)}) collective-permute-start(f32[32,128]{1,0:T(8,128)S(1)} %shard_map.168.nr), channel_id=1, source_target_pairs={{0,2},{1,3},{2,0},{3,1},{4,6},{5,7},{6,4},{7,5},{8,10},{9,11},{10,... | collective-permute-start | bytes 49160 | tf_op jit(solution)/shard_map/ppermute | solution.py:36
  56.5 1.1 collective-permute-done.5.fs
  57.7 0.0 collective-permute-done.4.far
  57.7 0.0 copy-done.5
  57.7 0.0 copy-done.6
  57.7 0.0 copy-done.8
  57.7 0.0 copy-done.1
  57.7 3.4 %shard_map.169 = (f32[5,24,3200]{2,1,0:T(8,128)S(1)}, f32[24,3200]{1,0:T(8,128)S(1)}, f32[24,3200]{1,0:T(8,128)S(1)}, f32[16,3200]{1,0:T(8,128)S(1)}, f32[24,320...) custom-call(s32[4]{0:T(128)S(1)} %copy-done.4, ...), custom_call_target="tpu_custom_call" | custom-call | tf_op jit(solution)/shard_map/pallas_call | solution.py:79
  61.1 0.0 copy-done.2
  61.1 0.0 copy-start.7
  61.1 0.0 copy-start.9
  61.1 1.9 %collective-permute-start.6 = (f32[8,3200]{1,0:T(8,128)S(1)}, f32[8,3200]{1,0:T(8,128)S(1)}, u32[]{:S(2)}, u32[]{:S(2)}) collective-permute-start(f32[8,3200]{1,0:T(8,128)S(1)} %get-tuple-element.50.edge), channel_id=1, source_target_pairs={{2,4},{3,5},{4,2},{5,3},{6,8},{7,9},{8,6},{9,7},{10,12},{11,13},{1... | collective-permute-start | bytes 307208 | tf_op jit(solution)/shard_map/ppermute | solution.py:36
  63.0 0.8 shard_map.172
  63.8 3.6 %collective-permute-start.9 = (f32[32,3072]{1,0:T(8,128)}, f32[32,3072]{1,0:T(8,128)}, u32[]{:S(2)}, u32[]{:S(2)}) collective-permute-start(f32[32,3072]{1,0:T(8,128)} %shard_map.172), channel_id=1, source_target_pairs={{2,4},{3,5},{4,2},{5,3},{6,8},{7,9},{8,6},{9,7},{10,12},{11,13},{1... | collective-permute-start | bytes 1179656 | tf_op jit(solution)/shard_map/ppermute | solution.py:36
  67.5 0.0 collective-permute-done.6.out
  67.5 11.7 %collective-permute-start.7 = (f32[8,3200]{1,0:T(8,128)S(1)}, f32[8,3200]{1,0:T(8,128)S(1)}, u32[]{:S(2)}, u32[]{:S(2)}) collective-permute-start(f32[8,3200]{1,0:T(8,128)S(1)} %collective-permute-done.6.out), channel_id=1, source_target_pairs={{0,2},{1,3},{2,0},{3,1},{4,6},{5,7},{6,4},{7,5},{8,10},{9,11},{10,... | collective-permute-start | bytes 307208 | tf_op jit(solution)/shard_map/ppermute | solution.py:36
  79.2 0.9 collective-permute-done.7.far
  80.1 0.0 copy-done.7
  80.1 0.0 copy-done.9
  80.1 3.1 %shard_map.170 = (f32[8,3072]{1,0:T(8,128)}, f32[2,768]{1,0:T(2,128)}, f32[2,768]{1,0:T(2,128)S(1)}, f32[24,128]{1,0:T(8,128)S(1)}) custom-call(s32[4]{0:T(128)S(1)} %copy-done.4, f32[32]{0:T(128)S(1)} %copy-done.5, f32[32]{0:T(128)S(1)} %copy-done.6, s32[2,128]{1,0:T(2,128)S(1)} %bitcast.16, f32[2,128]{1,0:T(2,128)S(1)} %bitcast.14, s32[2,128]{1,0:T(2,128)S(1)} %bitcast.17, ...), custom_call_target="tpu_custom_call" | custom-call | tf_op jit(solution)/shard_map/pallas_call | solution.py:79
  83.2 1.9 %collective-permute-start.8 = (f32[24,128]{1,0:T(8,128)S(1)}, f32[24,128]{1,0:T(8,128)S(1)}, u32[]{:S(2)}, u32[]{:S(2)}) collective-permute-start(f32[24,128]{1,0:T(8,128)S(1)} %get-tuple-element.51.own), channel_id=1, source_target_pairs={{0,32},{1,33},{2,34},{3,35},{4,36},{5,37},{6,38},{7,39},{8,40},{9,... | collective-permute-start | bytes 36872 | tf_op jit(solution)/shard_map/ppermute | solution.py:36
  85.1 7.2 %collective-permute-done.8.before = f32[24,128]{1,0:T(8,128)S(1)} collective-permute-done((f32[24,128]{1,0:T(8,128)S(1)}, f32[24,128]{1,0:T(8,128)S(1)}, u32[]{:S(2)}, u32[]{:S(2)}) %collective-permute-start.8) | collective-permute-done | bytes 12320 | tf_op jit(solution)/shard_map/ppermute | solution.py:36
  92.4 1.2 %shard_map.171 = f32[16,16,128]{2,1,0:T(8,128)} custom-call(s32[4]{0:T(128)S(1)} %copy-done.4, f32[24,128]{1,0:T(8,128)S(1)} %get-tuple-element.51.own, f32[24,128]{1,0:T(8,128)S(1)} %collective-permute-done.8.before), custom_call_target="tpu_custom_call" | custom-call | tf_op jit(solution)/shard_map/pallas_call | solution.py:79
  93.6 6.3 %all-to-all-start = ((f32[16,16,128]{2,1,0:T(8,128)}), f32[16,16,128]{2,1,0:T(8,128)S(1)}, u32[]{:S(2)}, u32[]{:S(2)}) async-start(f32[16,16,128]{2,1,0:T(8,128)} %shard_map.171), calls=%async_computation | async-start | bytes 262144 | tf_op jit(solution)/shard_map/all_to_all | solution.py:630
  99.9 0.0 collective-permute-done.9.second
  99.9 0.0 copy-start.3
  100.0 1.1 copy-done.3
  101.0 5.5 %shard_map.173 = f32[64,2,768]{2,1,0:T(2,128)} custom-call(s32[4]{0:T(128)S(1)} %copy-done.4, f32[32]{0:T(128)S(1)} %copy-done.5, f32[32]{0:T(128)S(1)} %copy-done.6, f32[104,3072]{1,0:T(8,128)S(1)} %copy-done.1, f32[104,3072]{1,0:T(8,128)S(1)} %collective-permute-done.pin, f32[56,3072]{1,0:T(8,128)S(1)} %collective-permute-done.1.out, ...), custom_call_target="tpu_custom_call" | custom-call | tf_op jit(solution)/shard_map/pallas_call | solution.py:79
  106.5 0.6 bitcast_dynamic-update-slice_fusion
  107.1 4.8 %all-to-all-done.got = f32[16,16,128]{2,1,0:T(8,128)S(1)} async-done(((f32[16,16,128]{2,1,0:T(8,128)}), f32[16,16,128]{2,1,0:T(8,128)S(1)}, u32[]{:S(2)}, u32[]{:S(2)}) %all-to-all-start) | async-done | bytes 131104 | tf_op jit(solution)/shard_map/all_to_all | solution.py:630
  112.0 3.8 %shard_map.174 = f32[1,256]{1,0:T(1,128)} custom-call(s32[4]{0:T(128)S(1)} %copy-done.4, f32[24,128]{1,0:T(8,128)S(1)} %get-tuple-element.51.own, f32[16,16,128]{2,1,0:T(8,128)S(1)} %all-to-all-done.got, f32[2,128]{1,0:T(2,128)S(1)} %get-tuple-element.57.above), custom_call_target="tpu_custom_call" | custom-call | tf_op jit(solution)/shard_map/pallas_call | solution.py:79
  (6 shorter events, 0.0 us)
Async XLA Ops:
  1.3 8.9 %copy-start.4 = (s32[4]{0:T(128)S(1)}, s32[4]{0:T(128)}, u32[]{:S(2)}) copy-start(s32[4]{0:T(128)} %pad_add_fusion.info) | copy-start | bytes 52
  1.3 56.4 %copy-start.5 = (f32[32]{0:T(128)S(1)}, f32[32]{0:T(128)}, u32[]{:S(2)}) copy-start(f32[32]{0:T(128)} %u.5) | copy-start | bytes 388
  1.3 56.4 %copy-start.6 = (f32[32]{0:T(128)S(1)}, f32[32]{0:T(128)}, u32[]{:S(2)}) copy-start(f32[32]{0:T(128)} %v.5) | copy-start | bytes 388
  1.3 56.4 %copy-start.8 = (s32[256]{0:T(256)S(1)}, s32[256]{0:T(256)}, u32[]{:S(2)}) copy-start(s32[256]{0:T(256)} %param.27) | copy-start | bytes 3076
  4.8 5.4 %collective-permute-start = (f32[104,3072]{1,0:T(8,128)}, f32[104,3072]{1,0:T(8,128)S(1)}, u32[]{:S(2)}, u32[]{:S(2)}) collective-permute-start(f32[104,3072]{1,0:T(8,128)} %shard_map.165.block), channel_id=1, source_target_pairs={{0,2},{1,3},{2,0},{3,1},{4,6},{5,7},{6,4},{7,5},{8,10},{9,11},{10,... | collective-permute-start | bytes 3833864 | tf_op jit(solution)/shard_map/ppermute | solution.py:36
  10.2 1.3 %copy-start = (f32[104,3072]{1,0:T(8,128)S(1)}, f32[104,3072]{1,0:T(8,128)}, u32[]{:S(2)}) copy-start(f32[104,3072]{1,0:T(8,128)} %shard_map.165.block) | copy-start | bytes 3833860
  11.5 46.2 %copy-start.1 = (f32[104,3072]{1,0:T(8,128)S(1)}, f32[104,3072]{1,0:T(8,128)}, u32[]{:S(2)}) copy-start(f32[104,3072]{1,0:T(8,128)} %shard_map.165.block) | copy-start | bytes 3833860
  12.2 30.1 %collective-permute-start.1 = (f32[56,3072]{1,0:T(8,128)S(1)}, f32[56,3072]{1,0:T(8,128)S(1)}, u32[]{:S(2)}, u32[]{:S(2)}) collective-permute-start(f32[56,3072]{1,0:T(8,128)S(1)} %get-tuple-element.37), channel_id=1, source_target_pairs={{2,4},{3,5},{4,2},{5,3},{6,8},{7,9},{8,6},{9,7},{10,12},{11,13},{1... | collective-permute-start | bytes 2064392 | tf_op jit(solution)/shard_map/ppermute | solution.py:36
  16.0 8.8 %collective-permute-start.2 = (f32[32,128]{1,0:T(8,128)S(1)}, f32[32,128]{1,0:T(8,128)S(1)}, u32[]{:S(2)}, u32[]{:S(2)}) collective-permute-start(f32[32,128]{1,0:T(8,128)S(1)} %get-tuple-element.38.strips), channel_id=1, source_target_pairs={{2,4},{3,5},{4,2},{5,3},{6,8},{7,9},{8,6},{9,7},{10,12},{11,13},{1... | collective-permute-start | bytes 49160 | tf_op jit(solution)/shard_map/ppermute | solution.py:36
  24.8 17.5 %collective-permute-start.3 = (f32[64,128]{1,0:T(8,128)S(1)}, f32[64,128]{1,0:T(8,128)S(1)}, u32[]{:S(2)}, u32[]{:S(2)}) collective-permute-start(f32[64,128]{1,0:T(8,128)S(1)} %shard_map.167), channel_id=1, source_target_pairs={{0,1},{1,0},{2,3},{3,2},{4,5},{5,4},{6,7},{7,6},{8,9},{9,8},{10,11... | collective-permute-start | bytes 98312 | tf_op jit(solution)/shard_map/ppermute | solution.py:36
  42.3 15.3 %collective-permute-start.4 = (f32[56,3072]{1,0:T(8,128)S(1)}, f32[56,3072]{1,0:T(8,128)S(1)}, u32[]{:S(2)}, u32[]{:S(2)}) collective-permute-start(f32[56,3072]{1,0:T(8,128)S(1)} %collective-permute-done.1.out), channel_id=1, source_target_pairs={{0,2},{1,3},{2,0},{3,1},{4,6},{5,7},{6,4},{7,5},{8,10},{9,11},{10,... | collective-permute-start | bytes 2064392 | tf_op jit(solution)/shard_map/ppermute | solution.py:36
  54.6 3.1 %collective-permute-start.5 = (f32[32,128]{1,0:T(8,128)S(1)}, f32[32,128]{1,0:T(8,128)S(1)}, u32[]{:S(2)}, u32[]{:S(2)}) collective-permute-start(f32[32,128]{1,0:T(8,128)S(1)} %shard_map.168.nr), channel_id=1, source_target_pairs={{0,2},{1,3},{2,0},{3,1},{4,6},{5,7},{6,4},{7,5},{8,10},{9,11},{10,... | collective-permute-start | bytes 49160 | tf_op jit(solution)/shard_map/ppermute | solution.py:36
  57.7 3.4 %copy-start.2 = (f32[56,3072]{1,0:T(8,128)}, f32[56,3072]{1,0:T(8,128)S(1)}, u32[]{:S(2)}) copy-start(f32[56,3072]{1,0:T(8,128)S(1)} %collective-permute-done.4.far) | copy-start | bytes 2064388
  61.1 19.0 %copy-start.7 = (f32[256]{0:T(256)S(1)}, f32[256]{0:T(256)}, u32[]{:S(2)}) copy-start(f32[256]{0:T(256)} %param.29) | copy-start | bytes 3076
  61.1 19.0 %copy-start.9 = (s32[256]{0:T(256)S(1)}, s32[256]{0:T(256)}, u32[]{:S(2)}) copy-start(s32[256]{0:T(256)} %param.28) | copy-start | bytes 3076
  61.1 6.3 %collective-permute-start.6 = (f32[8,3200]{1,0:T(8,128)S(1)}, f32[8,3200]{1,0:T(8,128)S(1)}, u32[]{:S(2)}, u32[]{:S(2)}) collective-permute-start(f32[8,3200]{1,0:T(8,128)S(1)} %get-tuple-element.50.edge), channel_id=1, source_target_pairs={{2,4},{3,5},{4,2},{5,3},{6,8},{7,9},{8,6},{9,7},{10,12},{11,13},{1... | collective-permute-start | bytes 307208 | tf_op jit(solution)/shard_map/ppermute | solution.py:36
  63.8 36.1 %collective-permute-start.9 = (f32[32,3072]{1,0:T(8,128)}, f32[32,3072]{1,0:T(8,128)}, u32[]{:S(2)}, u32[]{:S(2)}) collective-permute-start(f32[32,3072]{1,0:T(8,128)} %shard_map.172), channel_id=1, source_target_pairs={{2,4},{3,5},{4,2},{5,3},{6,8},{7,9},{8,6},{9,7},{10,12},{11,13},{1... | collective-permute-start | bytes 1179656 | tf_op jit(solution)/shard_map/ppermute | solution.py:36
  67.5 12.6 %collective-permute-start.7 = (f32[8,3200]{1,0:T(8,128)S(1)}, f32[8,3200]{1,0:T(8,128)S(1)}, u32[]{:S(2)}, u32[]{:S(2)}) collective-permute-start(f32[8,3200]{1,0:T(8,128)S(1)} %collective-permute-done.6.out), channel_id=1, source_target_pairs={{0,2},{1,3},{2,0},{3,1},{4,6},{5,7},{6,4},{7,5},{8,10},{9,11},{10,... | collective-permute-start | bytes 307208 | tf_op jit(solution)/shard_map/ppermute | solution.py:36
  83.2 9.2 %collective-permute-start.8 = (f32[24,128]{1,0:T(8,128)S(1)}, f32[24,128]{1,0:T(8,128)S(1)}, u32[]{:S(2)}, u32[]{:S(2)}) collective-permute-start(f32[24,128]{1,0:T(8,128)S(1)} %get-tuple-element.51.own), channel_id=1, source_target_pairs={{0,32},{1,33},{2,34},{3,35},{4,36},{5,37},{6,38},{7,39},{8,40},{9,... | collective-permute-start | bytes 36872 | tf_op jit(solution)/shard_map/ppermute | solution.py:36
  93.6 18.4 %all-to-all-start = ((f32[16,16,128]{2,1,0:T(8,128)}), f32[16,16,128]{2,1,0:T(8,128)S(1)}, u32[]{:S(2)}, u32[]{:S(2)}) async-start(f32[16,16,128]{2,1,0:T(8,128)} %shard_map.171), calls=%async_computation | async-start | bytes 262144 | tf_op jit(solution)/shard_map/all_to_all | solution.py:630
  99.9 1.1 copy-start.3

commit v4 on v3

--- a/solution.py
+++ b/solution.py
@@ -48,14 +48,20 @@
     return exchange(value, lambda r, g: (outer(r), g))
 
 
+def beside(r, t, g):
+    return (t, g if t // 16 == r // 16 else 1 - g)
+
+
 def near_swap(value):
-    return exchange(
-        value, lambda r, g: (outer(r), g if outer(r) // 16 == r // 16 else 1 - g)
-    )
+    return exchange(value, lambda r, g: beside(r, outer(r), g))
+
+
+def second_shift(value):
+    return exchange(value, lambda r, g: beside(r, r - 2 if r % 2 else r + 2, g))
 
 
 def gy_swap(value):
-    return exchange(value, lambda r, g: (r, 1 - g))
+    return exchange(value, lambda r, g: (r if 0 < r % 16 < 15 else -1, 1 - g))
 
 
 def grp_shift(value):
@@ -93,9 +99,9 @@
 
 def pack_body(
     info, air, kd, elev, cond, rf, mask, code, depth, soil, links,
-    block_h,
+    block_h, strip_h,
     links_v, air_v, kd_v, elev_v, cond_v, rf_v, mask_v, code_v, depth_v, soil_v,
-    block, sems, sent,
+    block, strip, sems, sent,
 ):
     right = info[1] == 1
     near = (kd_v, elev_v, cond_v, rf_v, mask_v, code_v, depth_v, soil_v, air_v, links_v)
@@ -126,17 +132,22 @@
     land = jnp.where(right, block[0:56, 0:128], block[0:56, TC - 128 : TC])
     kblock = jnp.where(right, kd_v[:, 0:128], kd_v[:, AC - 128 : AC])
     square = jnp.concatenate([land, kblock, jnp.zeros((70, 128), F32)], axis=0).T
-    strip = jnp.where(right, square[0:16], square[112:128])
-    block[64:72, 0:128] = strip[0:8]
-    block[64:72, 128:256] = strip[8:16]
+    strip[0:16, :] = jnp.where(right, square[0:16], square[112:128])
     ablock = jnp.concatenate(ends, axis=0).T
-    block[64:72, 256:384] = jnp.where(right, ablock[0:8], ablock[120:128])
-    result = pltpu.make_async_copy(block, block_h, sent)
-    result.start()
-    result.wait()
-
-
-def edge_body(info, block, pin, out, strips):
+    strip[16:24, :] = jnp.where(right, ablock[0:8], ablock[120:128])
+    for b in range(3):
+        block[64:72, b * 128 : (b + 1) * 128] = strip[8 * b : 8 * b + 8, :]
+    results = [
+        pltpu.make_async_copy(src, dst, sent.at[i])
+        for i, (src, dst) in enumerate(((strip, strip_h), (block, block_h)))
+    ]
+    for c in results:
+        c.start()
+    for c in results:
+        c.wait()
+
+
+def edge_body(info, block, pin, near, near2, out, strips, beyond):
     odd = info[0] == 1
     for i, off, n in EDGES:
         top = block[8 * i : 8 * i + n, :]
@@ -150,25 +161,25 @@
     out[24:56, :] = block[72:104, :]
     lane = lax.broadcasted_iota(jnp.int32, (8, 128), 1)
     for b in range(2):
-        at = slice(b * 128, (b + 1) * 128)
+        at, rows = slice(b * 128, (b + 1) * 128), slice(8 * b, 8 * b + 8)
         pair = pltpu.roll(pin[64:72, at], 64, 1)
-        strips[8 * b : 8 * b + 8, :] = jnp.where(lane < 64, block[64:72, at], pair)
+        strips[rows, :] = jnp.where(lane < 64, block[64:72, at], pair)
+        beyond[rows, :] = jnp.where(lane < 64, near[rows, :], pltpu.roll(near2[rows, :], 64, 1))
     strips[16:24, :] = block[64:72, 256:384]
     strips[24:32, :] = pin[64:72, 256:384]
+    beyond[16:24, :] = near[16:24, :]
+    beyond[24:32, :] = near2[16:24, :]
+    strips[32:64, :] = beyond[...]
 
 
 def pair_air_body(edge, pin, out):
     out[...] = pin[72:104, :]
 
 
-def both_body(strips, near, out):
-    out[0:32, :] = strips[...]
-    out[32:64, :] = near[...]
-
-
 def pick_body(info, near, across, out):
     end = (info[3] == 0) | (info[3] == 15)
-    out[...] = jnp.where(end, near[...], across[32:64, :])
+    out[0:32, :] = across[0:32, :]
+    out[32:64, :] = jnp.where(end, near[...], across[32:64, :])
 
 
 def chunks_body(info, own, before, out):
@@ -311,13 +322,18 @@
 
 
 def first_body(
-    info, u, v, cells, block, pin, out, far, sp, nr, fs,
-    coef, rain_w, static_w, land, ring, soil, lat, q_out, t_out, k_out, edge, above,
+    info, u, v, cells, block, pin, out, far, strips, far_strips,
+    coef, rain_w, static_w, land, ring, soil, lat, q_out, t_out, k_out, edge, above, sp,
     grid, rq,
 ):
     odd = info[0] == 1
     right = info[1] == 1
     hu_t, hv_t = 0.5 * u[0], 0.5 * v[0]
+    end = (info[3] == 0) | (info[3] == 15)
+    sp[0:16, :] = jnp.where(end, pltpu.roll(far_strips[0:16, :], 64, 1), strips[0:16, :])
+    sp[16:24, :] = jnp.where(end, far_strips[24:32, :], strips[16:24, :])
+    sp[24:32, :] = jnp.where(end, far_strips[16:24, :], strips[24:32, :])
+    nr, fs = strips.at[32:64, :], far_strips.at[32:64, :]
     square = land_strip(sp, right)
     mine, pair = square[0:64], square[64:128]
     cols = (jnp.where(odd, pair, mine), jnp.where(odd, mine, pair))
@@ -479,7 +495,7 @@
     odd = info[0] == 1
     right = info[1] == 1
     r = info[2]
-    for i, (ref, lo) in enumerate(((sp, 16), (sp, 24), (nr, 16), (nr, 24), (fs, 16))):
+    for i, (ref, lo) in enumerate(((sp, 16), (sp, 24), (nr, 48), (nr, 56), (fs, 48))):
         strips[i] = air_strip(ref, right, lo)
     lanes = lanes_inside(right, 1)
     masks, kd = {}, {}
@@ -584,34 +600,35 @@
 
     land_v = pltpu.VMEM((TR, TC), F32)
     code_v = pltpu.VMEM((TR, TC), jnp.int32)
-    (block,) = call(
+    block, strip = call(
         pack_body,
-        [(BLOCK, TC)],
+        [(BLOCK, TC), (24, 128)],
         [info],
         [air.reshape(FL, 2, AC), kdiff, elev, cond, rain_factor, land_mask, flow_code, depth_init, soil_init,
          link_flow.reshape(1, LINKS)],
-        [(1, LINKS), (FL, 2, AC), (2, AC), land_v, land_v, land_v, code_v, code_v, land_v, land_v, (BLOCK, TC),
-         pltpu.SemaphoreType.DMA((10,)), pltpu.SemaphoreType.DMA],
+        [(1, LINKS), (FL, 2, AC), (2, AC), land_v, land_v, land_v, code_v, code_v, land_v, land_v, (BLOCK, TC), (24, 128),
+         pltpu.SemaphoreType.DMA((10,)), pltpu.SemaphoreType.DMA((2,))],
         limit=WHOLE,
-        far=1,
+        far=2,
     )
     pin = pair_swap(block)
-    edge, strips = call(edge_body, [(EDGE, TC), (32, 128)], [info], [block, pin])
-    near = near_swap(strips)
+    near, near2 = near_swap(strip), second_shift(strip)
+    edge, strips, near = call(
+        edge_body, [(EDGE, TC), (64, 128), (32, 128)], [info], [block, pin, near, near2]
+    )
     out = chip_swap(edge)
-    (both,) = call(both_body, [(64, 128)], [], [strips, near])
-    sp = gy_swap(both)
-    (nr,) = call(pick_body, [(32, 128)], [info], [near, sp])
-    ready, _ = lax.optimization_barrier((out, sp))
+    sp = gy_swap(strips)
+    (strips,) = call(pick_body, [(64, 128)], [info], [near, sp])
+    far_strips = pair_swap(strips)
+    ready, _ = lax.optimization_barrier((out, far_strips))
     far = pair_swap(ready)
-    fs = pair_swap(nr)
 
     wide, chip, flat = (24, TW), (16, TW), (16, AW)
-    (coef, rain_w, static_w, land, ring, soil, lat, q, t, k16, edge, above) = call(
+    (coef, rain_w, static_w, land, ring, soil, lat, q, t, k16, edge, above, sp) = call(
         first_body,
-        [(5, 24, TW), wide, wide, chip, wide, chip, (8, 128), flat, flat, flat, (8, TW), (2, 128)],
+        [(5, 24, TW), wide, wide, chip, wide, chip, (8, 128), flat, flat, flat, (8, TW), (2, 128), (32, 128)],
         [info, u_wind, v_wind],
-        [pairs[0], block, pin, out, far, sp, nr, fs],
+        [pairs[0], block, pin, out, far, strips, far_strips],
         [(144, TW), wide],
     )
     outb = chip_swap(edge)
@@ -632,7 +649,7 @@
         air_body,
         [(FL, 2, AC)],
         [info, u_wind, v_wind],
-        [block, pin, out, second, far, k16, sp, nr, fs],
+        [block, pin, out, second, far, k16, sp, strips, far_strips],
         [(5, 128, 128)],
     )
     air_new = air_new.at[Q0].set(qf)

time: 116 us -> 114 us (0.983)
  starting transfers between devices: 62.9 us -> 61.4 us
    all_to_all x1, starting transfers between devices: 6.35 us -> 4.81 us  [shards(): got = lax.all_to_all(chunks, 'gx', 0, 0)]
    ppermute x10 -> x11, waiting for transfers between devices: 21 us -> 19.8 us  [exchange(): return lax.ppermute(value, AXES, pairs)]
    unnamed x20 -> x22, local copies, waits for them, and re-layouts: 2.43 us -> 3.11 us
    pallas_call x10 -> x9, Pallas kernels: 22.5 us -> 22.1 us  [call(): pl.pallas_call(body, out_shape=[jax.ShapeDtypeStruct(o, F32) for o in out...]
    ppermute x10 -> x11, starting transfers between devices: 56.6 us -> 56.6 us  [exchange(): return lax.ppermute(value, AXES, pairs)]
  transfers between devices with their start and end apart: 11 -> 12, of which waited for: 7 -> 7; matrix products, arithmetic and copies ran while one was open for 1% -> 1% of each run, Pallas kernels for 10% -> 10%
where the time goes in v4:
time: 114 us
  starting transfers between devices  61.4 us (54%)
  waiting for transfers between devices  24.7 us (22%)
  Pallas kernels  22.1 us (19%)
  local copies, waits for them, and re-layouts  3.71 us (3%)
    ppermute x11, starting transfers between devices, exchange(): return lax.ppermute(value, AXES, pairs)  56.6 us
    pallas_call x9, Pallas kernels, call(): pl.pallas_call(body, out_shape=[jax.ShapeDtypeStruct(o, F32) for o in out...  22.1 us
    ppermute x11, waiting for transfers between devices, exchange(): return lax.ppermute(value, AXES, pairs)  19.8 us
    all_to_all x1, waiting for transfers between devices, shards(): got = lax.all_to_all(chunks, 'gx', 0, 0)  4.89 us
    all_to_all x1, starting transfers between devices, shards(): got = lax.all_to_all(chunks, 'gx', 0, 0)  4.81 us
    unnamed x22, local copies, waits for them, and re-layouts  3.11 us
  transfers between devices with their start and end apart: 12, of which 7 were waited for; matrix products, arithmetic and copies ran while one was open for 1% of the time, Pallas kernels for 10%

profile of v4, /device:TPU:7, one launch (start us, length us, event | category | flops | bytes accessed | tf_op | source)
XLA Modules:
  0.0 113.5 jit_solution(11087046222159450023)
XLA Ops:
  0.6 0.7 pad_add_fusion.info
  1.3 3.4 %shard_map.165 = (f32[104,3072]{1,0:T(8,128)}, f32[24,128]{1,0:T(8,128)}) custom-call(s32[4]{0:T(128)} %pad_add_fusion.info, f32[64,2,768]{2,1,0:T(2,128)} %bitcast.19, f32[2,768]{1,0:T(2,128)} %kd.1, f32[8,3072]{1,0:T(8,128)} %elev.1, f32[8,3072]{1,0:T(8,128)} %cond.1, f32[8,3072]{1,0:T(8,128)} %rf.1, s32[8,3072]{1,0:T(8,128)} %mask.1, s32[8,3072]{1,0:T(8,128)} %code.1, ...), custom_call_target="tpu_custom_call" | custom-call | tf_op jit(solution)/shard_map/pallas_call | solution.py:85
  4.7 0.0 copy-start.9
  4.7 2.6 %collective-permute-start = (f32[104,3072]{1,0:T(8,128)}, f32[104,3072]{1,0:T(8,128)S(1)}, u32[]{:S(2)}, u32[]{:S(2)}) collective-permute-start(f32[104,3072]{1,0:T(8,128)} %get-tuple-element.41.block), channel_id=1, source_target_pairs={{0,2},{1,3},{2,0},{3,1},{4,6},{5,7},{6,4},{7,5},{8,10},{9,11},{10,... | collective-permute-start | bytes 3833864 | tf_op jit(solution)/shard_map/ppermute | solution.py:36
  7.3 0.0 copy-start.6
  7.3 0.0 copy-start.7
  7.3 13.8 %collective-permute-start.2 = (f32[24,128]{1,0:T(8,128)}, f32[24,128]{1,0:T(8,128)S(1)}, u32[]{:S(2)}, u32[]{:S(2)}) collective-permute-start(f32[24,128]{1,0:T(8,128)} %get-tuple-element.42), channel_id=1, source_target_pairs={{0,4},{1,5},{4,8},{5,9},{6,2},{7,3},{8,12},{9,13},{10,6},{11,7},{1... | collective-permute-start | bytes 36872 | tf_op jit(solution)/shard_map/ppermute | solution.py:36
  21.2 1.9 %collective-permute-start.1 = (f32[24,128]{1,0:T(8,128)}, f32[24,128]{1,0:T(8,128)S(1)}, u32[]{:S(2)}, u32[]{:S(2)}) collective-permute-start(f32[24,128]{1,0:T(8,128)} %get-tuple-element.42), channel_id=1, source_target_pairs={{2,4},{3,5},{4,2},{5,3},{6,8},{7,9},{8,6},{9,7},{10,12},{11,13},{1... | collective-permute-start | bytes 36872 | tf_op jit(solution)/shard_map/ppermute | solution.py:36
  23.1 0.0 collective-permute-done.2.near2
  23.1 3.3 %collective-permute-done.1.near = f32[24,128]{1,0:T(8,128)S(1)} collective-permute-done((f32[24,128]{1,0:T(8,128)}, f32[24,128]{1,0:T(8,128)S(1)}, u32[]{:S(2)}, u32[]{:S(2)}) %collective-permute-start.1) | collective-permute-done | bytes 12320 | tf_op jit(solution)/shard_map/ppermute | solution.py:36
  26.4 0.0 collective-permute-done.pin
  26.4 1.3 %copy-done = f32[104,3072]{1,0:T(8,128)S(1)} copy-done((f32[104,3072]{1,0:T(8,128)S(1)}, f32[104,3072]{1,0:T(8,128)}, u32[]{:S(2)}) %copy-start) | copy-done | bytes 1277976
  27.7 0.7 copy-done.4
  28.4 0.7 shard_map.166
  29.1 1.9 %collective-permute-start.3 = (f32[56,3072]{1,0:T(8,128)S(1)}, f32[56,3072]{1,0:T(8,128)S(1)}, u32[]{:S(2)}, u32[]{:S(2)}) collective-permute-start(f32[56,3072]{1,0:T(8,128)S(1)} %get-tuple-element.43), channel_id=1, source_target_pairs={{2,4},{3,5},{4,2},{5,3},{6,8},{7,9},{8,6},{9,7},{10,12},{11,13},{1... | collective-permute-start | bytes 2064392 | tf_op jit(solution)/shard_map/ppermute | solution.py:36
  31.0 6.3 %collective-permute-start.4 = (f32[64,128]{1,0:T(8,128)S(1)}, f32[64,128]{1,0:T(8,128)S(1)}, u32[]{:S(2)}, u32[]{:S(2)}) collective-permute-start(f32[64,128]{1,0:T(8,128)S(1)} %get-tuple-element.45), channel_id=1, source_target_pairs={{2,3},{3,2},{4,5},{5,4},{6,7},{7,6},{8,9},{9,8},{10,11},{11,10},{1... | collective-permute-start | bytes 98312 | tf_op jit(solution)/shard_map/ppermute | solution.py:36
  37.4 8.0 %collective-permute-done.4.across = f32[64,128]{1,0:T(8,128)S(1)} collective-permute-done((f32[64,128]{1,0:T(8,128)S(1)}, f32[64,128]{1,0:T(8,128)S(1)}, u32[]{:S(2)}, u32[]{:S(2)}) %collective-permute-start.4) | collective-permute-done | bytes 32800 | tf_op jit(solution)/shard_map/ppermute | solution.py:36
  45.4 0.5 shard_map.167.strips.nr
  45.9 1.9 %collective-permute-start.5 = (f32[64,128]{1,0:T(8,128)S(1)}, f32[64,128]{1,0:T(8,128)S(1)}, u32[]{:S(2)}, u32[]{:S(2)}) collective-permute-start(f32[64,128]{1,0:T(8,128)S(1)} %shard_map.167.strips.nr), channel_id=1, source_target_pairs={{0,2},{1,3},{2,0},{3,1},{4,6},{5,7},{6,4},{7,5},{8,10},{9,11},{10,... | collective-permute-start | bytes 98312 | tf_op jit(solution)/shard_map/ppermute | solution.py:36
  47.9 1.2 %collective-permute-done.5.far_strips.fs = f32[64,128]{1,0:T(8,128)S(1)} collective-permute-done((f32[64,128]{1,0:T(8,128)S(1)}, f32[64,128]{1,0:T(8,128)S(1)}, u32[]{:S(2)}, u32[]{:S(2)}) %collective-permute-start.5) | collective-permute-done | bytes 32800 | tf_op jit(solution)/shard_map/ppermute | solution.py:36
  49.0 0.0 collective-permute-done.3.out
  49.0 8.0 %collective-permute-start.6 = (f32[56,3072]{1,0:T(8,128)S(1)}, f32[56,3072]{1,0:T(8,128)S(1)}, u32[]{:S(2)}, u32[]{:S(2)}) collective-permute-start(f32[56,3072]{1,0:T(8,128)S(1)} %collective-permute-done.3.out), channel_id=1, source_target_pairs={{0,2},{1,3},{2,0},{3,1},{4,6},{5,7},{6,4},{7,5},{8,10},{9,11},{10,... | collective-permute-start | bytes 2064392 | tf_op jit(solution)/shard_map/ppermute | solution.py:36
  57.1 1.7 %collective-permute-done.6.far = f32[56,3072]{1,0:T(8,128)S(1)} collective-permute-done((f32[56,3072]{1,0:T(8,128)S(1)}, f32[56,3072]{1,0:T(8,128)S(1)}, u32[]{:S(2)}, u32[]{:S(2)}) %collective-permute-start.6) | collective-permute-done | bytes 688160 | tf_op jit(solution)/shard_map/ppermute | solution.py:36
  58.8 0.0 copy-done.7
  58.8 0.0 copy-done.1
  58.9 3.3 %shard_map.168 = (f32[5,24,3200]{2,1,0:T(8,128)S(1)}, f32[24,3200]{1,0:T(8,128)S(1)}, f32[24,3200]{1,0:T(8,128)S(1)}, f32[16,3200]{1,0:T(8,128)S(1)}, f32[24,320...) custom-call(s32[4]{0:T(128)S(1)} %copy-done.4, ...), custom_call_target="tpu_custom_call" | custom-call | tf_op jit(solution)/shard_map/pallas_call | solution.py:85
  62.2 0.0 copy-done.2
  62.2 0.0 copy-start.8
  62.2 0.0 copy-start.10
  62.2 1.9 %collective-permute-start.7 = (f32[8,3200]{1,0:T(8,128)S(1)}, f32[8,3200]{1,0:T(8,128)S(1)}, u32[]{:S(2)}, u32[]{:S(2)}) collective-permute-start(f32[8,3200]{1,0:T(8,128)S(1)} %get-tuple-element.57.edge), channel_id=1, source_target_pairs={{2,4},{3,5},{4,2},{5,3},{6,8},{7,9},{8,6},{9,7},{10,12},{11,13},{1... | collective-permute-start | bytes 307208 | tf_op jit(solution)/shard_map/ppermute | solution.py:36
  64.1 0.8 shard_map.171
  64.9 3.6 %collective-permute-start.10 = (f32[32,3072]{1,0:T(8,128)}, f32[32,3072]{1,0:T(8,128)}, u32[]{:S(2)}, u32[]{:S(2)}) collective-permute-start(f32[32,3072]{1,0:T(8,128)} %shard_map.171), channel_id=1, source_target_pairs={{2,4},{3,5},{4,2},{5,3},{6,8},{7,9},{8,6},{9,7},{10,12},{11,13},{1... | collective-permute-start | bytes 1179656 | tf_op jit(solution)/shard_map/ppermute | solution.py:36
  68.5 0.0 collective-permute-done.7.out
  68.6 12.6 %collective-permute-start.8 = (f32[8,3200]{1,0:T(8,128)S(1)}, f32[8,3200]{1,0:T(8,128)S(1)}, u32[]{:S(2)}, u32[]{:S(2)}) collective-permute-start(f32[8,3200]{1,0:T(8,128)S(1)} %collective-permute-done.7.out), channel_id=1, source_target_pairs={{0,2},{1,3},{2,0},{3,1},{4,6},{5,7},{6,4},{7,5},{8,10},{9,11},{10,... | collective-permute-start | bytes 307208 | tf_op jit(solution)/shard_map/ppermute | solution.py:36
  81.2 0.9 collective-permute-done.8.far
  82.1 0.0 copy-done.8
  82.1 2.9 %shard_map.169 = (f32[8,3072]{1,0:T(8,128)}, f32[2,768]{1,0:T(2,128)}, f32[2,768]{1,0:T(2,128)S(1)}, f32[24,128]{1,0:T(8,128)S(1)}) custom-call(s32[4]{0:T(128)S(1)} %copy-done.4, f32[32]{0:T(128)S(1)} %copy-done.6, f32[32]{0:T(128)S(1)} %copy-done.7, s32[2,128]{1,0:T(2,128)S(1)} %bitcast.16, f32[2,128]{1,0:T(2,128)S(1)} %bitcast.14, s32[2,128]{1,0:T(2,128)S(1)} %bitcast.17, ...), custom_call_target="tpu_custom_call" | custom-call | tf_op jit(solution)/shard_map/pallas_call | solution.py:85
  85.0 1.9 %collective-permute-start.9 = (f32[24,128]{1,0:T(8,128)S(1)}, f32[24,128]{1,0:T(8,128)S(1)}, u32[]{:S(2)}, u32[]{:S(2)}) collective-permute-start(f32[24,128]{1,0:T(8,128)S(1)} %get-tuple-element.58.own), channel_id=1, source_target_pairs={{0,32},{1,33},{2,34},{3,35},{4,36},{5,37},{6,38},{7,39},{8,40},{9,... | collective-permute-start | bytes 36872 | tf_op jit(solution)/shard_map/ppermute | solution.py:36
  86.9 4.6 %collective-permute-done.9.before = f32[24,128]{1,0:T(8,128)S(1)} collective-permute-done((f32[24,128]{1,0:T(8,128)S(1)}, f32[24,128]{1,0:T(8,128)S(1)}, u32[]{:S(2)}, u32[]{:S(2)}) %collective-permute-start.9) | collective-permute-done | bytes 12320 | tf_op jit(solution)/shard_map/ppermute | solution.py:36
  91.6 1.2 %shard_map.170 = f32[16,16,128]{2,1,0:T(8,128)} custom-call(s32[4]{0:T(128)S(1)} %copy-done.4, f32[24,128]{1,0:T(8,128)S(1)} %get-tuple-element.58.own, f32[24,128]{1,0:T(8,128)S(1)} %collective-permute-done.9.before), custom_call_target="tpu_custom_call" | custom-call | tf_op jit(solution)/shard_map/pallas_call | solution.py:85
  92.8 4.8 %all-to-all-start = ((f32[16,16,128]{2,1,0:T(8,128)}), f32[16,16,128]{2,1,0:T(8,128)S(1)}, u32[]{:S(2)}, u32[]{:S(2)}) async-start(f32[16,16,128]{2,1,0:T(8,128)} %shard_map.170), calls=%async_computation | async-start | bytes 262144 | tf_op jit(solution)/shard_map/all_to_all | solution.py:647
  97.6 0.0 collective-permute-done.10.second
  97.6 0.0 copy-done.5
  97.6 1.1 copy-done.3
  98.7 5.5 %shard_map.172 = f32[64,2,768]{2,1,0:T(2,128)} custom-call(s32[4]{0:T(128)S(1)} %copy-done.5, f32[32]{0:T(128)S(1)} %copy-done.6, f32[32]{0:T(128)S(1)} %copy-done.7, f32[104,3072]{1,0:T(8,128)S(1)} %copy-done.1, f32[104,3072]{1,0:T(8,128)S(1)} %collective-permute-done.pin, f32[56,3072]{1,0:T(8,128)S(1)} %collective-permute-done.3.out, ...), custom_call_target="tpu_custom_call" | custom-call | tf_op jit(solution)/shard_map/pallas_call | solution.py:85
  104.2 0.6 bitcast_dynamic-update-slice_fusion
  104.8 4.9 %all-to-all-done.got = f32[16,16,128]{2,1,0:T(8,128)S(1)} async-done(((f32[16,16,128]{2,1,0:T(8,128)}), f32[16,16,128]{2,1,0:T(8,128)S(1)}, u32[]{:S(2)}, u32[]{:S(2)}) %all-to-all-start) | async-done | bytes 131104 | tf_op jit(solution)/shard_map/all_to_all | solution.py:647
  109.7 3.8 %shard_map.173 = f32[1,256]{1,0:T(1,128)} custom-call(s32[4]{0:T(128)S(1)} %copy-done.5, f32[24,128]{1,0:T(8,128)S(1)} %get-tuple-element.58.own, f32[16,16,128]{2,1,0:T(8,128)S(1)} %all-to-all-done.got, f32[2,128]{1,0:T(2,128)S(1)} %get-tuple-element.65.above), custom_call_target="tpu_custom_call" | custom-call | tf_op jit(solution)/shard_map/pallas_call | solution.py:85
  (9 shorter events, 0.0 us)
Async XLA Ops:
  4.7 54.1 %copy-start.9 = (s32[256]{0:T(256)S(1)}, s32[256]{0:T(256)}, u32[]{:S(2)}) copy-start(s32[256]{0:T(256)} %param.27) | copy-start | bytes 3076
  4.7 21.7 %collective-permute-start = (f32[104,3072]{1,0:T(8,128)}, f32[104,3072]{1,0:T(8,128)S(1)}, u32[]{:S(2)}, u32[]{:S(2)}) collective-permute-start(f32[104,3072]{1,0:T(8,128)} %get-tuple-element.41.block), channel_id=1, source_target_pairs={{0,2},{1,3},{2,0},{3,1},{4,6},{5,7},{6,4},{7,5},{8,10},{9,11},{10,... | collective-permute-start | bytes 3833864 | tf_op jit(solution)/shard_map/ppermute | solution.py:36
  7.3 51.5 %copy-start.6 = (f32[32]{0:T(128)S(1)}, f32[32]{0:T(128)}, u32[]{:S(2)}) copy-start(f32[32]{0:T(128)} %u.5) | copy-start | bytes 388
  7.3 51.5 %copy-start.7 = (f32[32]{0:T(128)S(1)}, f32[32]{0:T(128)}, u32[]{:S(2)}) copy-start(f32[32]{0:T(128)} %v.5) | copy-start | bytes 388
  7.3 15.8 %collective-permute-start.2 = (f32[24,128]{1,0:T(8,128)}, f32[24,128]{1,0:T(8,128)S(1)}, u32[]{:S(2)}, u32[]{:S(2)}) collective-permute-start(f32[24,128]{1,0:T(8,128)} %get-tuple-element.42), channel_id=1, source_target_pairs={{0,4},{1,5},{4,8},{5,9},{6,2},{7,3},{8,12},{9,13},{10,6},{11,7},{1... | collective-permute-start | bytes 36872 | tf_op jit(solution)/shard_map/ppermute | solution.py:36
  21.2 5.2 %collective-permute-start.1 = (f32[24,128]{1,0:T(8,128)}, f32[24,128]{1,0:T(8,128)S(1)}, u32[]{:S(2)}, u32[]{:S(2)}) collective-permute-start(f32[24,128]{1,0:T(8,128)} %get-tuple-element.42), channel_id=1, source_target_pairs={{2,4},{3,5},{4,2},{5,3},{6,8},{7,9},{8,6},{9,7},{10,12},{11,13},{1... | collective-permute-start | bytes 36872 | tf_op jit(solution)/shard_map/ppermute | solution.py:36
  26.4 1.3 %copy-start = (f32[104,3072]{1,0:T(8,128)S(1)}, f32[104,3072]{1,0:T(8,128)}, u32[]{:S(2)}) copy-start(f32[104,3072]{1,0:T(8,128)} %get-tuple-element.41.block) | copy-start | bytes 3833860
  27.7 0.7 copy-start.4
  28.4 30.5 %copy-start.1 = (f32[104,3072]{1,0:T(8,128)S(1)}, f32[104,3072]{1,0:T(8,128)}, u32[]{:S(2)}) copy-start(f32[104,3072]{1,0:T(8,128)} %get-tuple-element.41.block) | copy-start | bytes 3833860
  29.1 20.0 %collective-permute-start.3 = (f32[56,3072]{1,0:T(8,128)S(1)}, f32[56,3072]{1,0:T(8,128)S(1)}, u32[]{:S(2)}, u32[]{:S(2)}) collective-permute-start(f32[56,3072]{1,0:T(8,128)S(1)} %get-tuple-element.43), channel_id=1, source_target_pairs={{2,4},{3,5},{4,2},{5,3},{6,8},{7,9},{8,6},{9,7},{10,12},{11,13},{1... | collective-permute-start | bytes 2064392 | tf_op jit(solution)/shard_map/ppermute | solution.py:36
  31.0 14.4 %collective-permute-start.4 = (f32[64,128]{1,0:T(8,128)S(1)}, f32[64,128]{1,0:T(8,128)S(1)}, u32[]{:S(2)}, u32[]{:S(2)}) collective-permute-start(f32[64,128]{1,0:T(8,128)S(1)} %get-tuple-element.45), channel_id=1, source_target_pairs={{2,3},{3,2},{4,5},{5,4},{6,7},{7,6},{8,9},{9,8},{10,11},{11,10},{1... | collective-permute-start | bytes 98312 | tf_op jit(solution)/shard_map/ppermute | solution.py:36
  45.9 3.1 %collective-permute-start.5 = (f32[64,128]{1,0:T(8,128)S(1)}, f32[64,128]{1,0:T(8,128)S(1)}, u32[]{:S(2)}, u32[]{:S(2)}) collective-permute-start(f32[64,128]{1,0:T(8,128)S(1)} %shard_map.167.strips.nr), channel_id=1, source_target_pairs={{0,2},{1,3},{2,0},{3,1},{4,6},{5,7},{6,4},{7,5},{8,10},{9,11},{10,... | collective-permute-start | bytes 98312 | tf_op jit(solution)/shard_map/ppermute | solution.py:36
  49.0 9.8 %collective-permute-start.6 = (f32[56,3072]{1,0:T(8,128)S(1)}, f32[56,3072]{1,0:T(8,128)S(1)}, u32[]{:S(2)}, u32[]{:S(2)}) collective-permute-start(f32[56,3072]{1,0:T(8,128)S(1)} %collective-permute-done.3.out), channel_id=1, source_target_pairs={{0,2},{1,3},{2,0},{3,1},{4,6},{5,7},{6,4},{7,5},{8,10},{9,11},{10,... | collective-permute-start | bytes 2064392 | tf_op jit(solution)/shard_map/ppermute | solution.py:36
  58.8 3.3 %copy-start.2 = (f32[56,3072]{1,0:T(8,128)}, f32[56,3072]{1,0:T(8,128)S(1)}, u32[]{:S(2)}) copy-start(f32[56,3072]{1,0:T(8,128)S(1)} %collective-permute-done.6.far) | copy-start | bytes 2064388
  62.2 19.9 %copy-start.8 = (f32[256]{0:T(256)S(1)}, f32[256]{0:T(256)}, u32[]{:S(2)}) copy-start(f32[256]{0:T(256)} %param.29) | copy-start | bytes 3076
  62.2 19.9 %copy-start.10 = (s32[256]{0:T(256)S(1)}, s32[256]{0:T(256)}, u32[]{:S(2)}) copy-start(s32[256]{0:T(256)} %param.28) | copy-start | bytes 3076
  62.2 6.3 %collective-permute-start.7 = (f32[8,3200]{1,0:T(8,128)S(1)}, f32[8,3200]{1,0:T(8,128)S(1)}, u32[]{:S(2)}, u32[]{:S(2)}) collective-permute-start(f32[8,3200]{1,0:T(8,128)S(1)} %get-tuple-element.57.edge), channel_id=1, source_target_pairs={{2,4},{3,5},{4,2},{5,3},{6,8},{7,9},{8,6},{9,7},{10,12},{11,13},{1... | collective-permute-start | bytes 307208 | tf_op jit(solution)/shard_map/ppermute | solution.py:36
  64.9 32.7 %collective-permute-start.10 = (f32[32,3072]{1,0:T(8,128)}, f32[32,3072]{1,0:T(8,128)}, u32[]{:S(2)}, u32[]{:S(2)}) collective-permute-start(f32[32,3072]{1,0:T(8,128)} %shard_map.171), channel_id=1, source_target_pairs={{2,4},{3,5},{4,2},{5,3},{6,8},{7,9},{8,6},{9,7},{10,12},{11,13},{1... | collective-permute-start | bytes 1179656 | tf_op jit(solution)/shard_map/ppermute | solution.py:36
  68.6 13.5 %collective-permute-start.8 = (f32[8,3200]{1,0:T(8,128)S(1)}, f32[8,3200]{1,0:T(8,128)S(1)}, u32[]{:S(2)}, u32[]{:S(2)}) collective-permute-start(f32[8,3200]{1,0:T(8,128)S(1)} %collective-permute-done.7.out), channel_id=1, source_target_pairs={{0,2},{1,3},{2,0},{3,1},{4,6},{5,7},{6,4},{7,5},{8,10},{9,11},{10,... | collective-permute-start | bytes 307208 | tf_op jit(solution)/shard_map/ppermute | solution.py:36
  82.1 15.5 %copy-start.5 = (s32[4]{0:T(128)S(1)}, s32[4]{0:T(128)}, u32[]{:S(2)}) copy-start(s32[4]{0:T(128)} %pad_add_fusion.info) | copy-start | bytes 52
  85.0 6.5 %collective-permute-start.9 = (f32[24,128]{1,0:T(8,128)S(1)}, f32[24,128]{1,0:T(8,128)S(1)}, u32[]{:S(2)}, u32[]{:S(2)}) collective-permute-start(f32[24,128]{1,0:T(8,128)S(1)} %get-tuple-element.58.own), channel_id=1, source_target_pairs={{0,32},{1,33},{2,34},{3,35},{4,36},{5,37},{6,38},{7,39},{8,40},{9,... | collective-permute-start | bytes 36872 | tf_op jit(solution)/shard_map/ppermute | solution.py:36
  92.8 16.9 %all-to-all-start = ((f32[16,16,128]{2,1,0:T(8,128)}), f32[16,16,128]{2,1,0:T(8,128)S(1)}, u32[]{:S(2)}, u32[]{:S(2)}) async-start(f32[16,16,128]{2,1,0:T(8,128)} %shard_map.170), calls=%async_computation | async-start | bytes 262144 | tf_op jit(solution)/shard_map/all_to_all | solution.py:647
  97.6 1.1 copy-start.3

commit v5 on v4

--- a/solution.py
+++ b/solution.py
@@ -114,10 +114,15 @@
     for c in copies:
         c.start()
     block[56:72, :] = jnp.zeros((16, TC), F32)
-    for c in copies:
-        c.wait()
+    parts = ((block.at[0:56], block_h.at[0:56]), (block.at[72:104], block_h.at[72:104]),
+             (block.at[56:72], block_h.at[56:72]), (strip, strip_h))
+    results = [pltpu.make_async_copy(a, b, sent.at[i]) for i, (a, b) in enumerate(parts)]
     for i, ref in enumerate((elev_v, cond_v, rf_v, mask_v, code_v, depth_v, soil_v)):
+        copies[i + 1].wait()
         block[8 * i : 8 * i + 8, :] = ref[...].astype(F32)
+    results[0].start()
+    for i in (0, 8, 9):
+        copies[i].wait()
     block[58:59, 0:LINKS] = links_v[...]
     ends = []
     for r in range(2):
@@ -129,6 +134,7 @@
         block[56:57, (2 + r) * AC : (3 + r) * AC] = rows[0:1, :]
         block[57:58, r * AC : (r + 1) * AC] = kd_v[r : r + 1, :]
         ends.append(jnp.where(right, rows[:, 0:128], rows[:, AC - 128 : AC]))
+    results[1].start()
     land = jnp.where(right, block[0:56, 0:128], block[0:56, TC - 128 : TC])
     kblock = jnp.where(right, kd_v[:, 0:128], kd_v[:, AC - 128 : AC])
     square = jnp.concatenate([land, kblock, jnp.zeros((70, 128), F32)], axis=0).T
@@ -137,12 +143,8 @@
     strip[16:24, :] = jnp.where(right, ablock[0:8], ablock[120:128])
     for b in range(3):
         block[64:72, b * 128 : (b + 1) * 128] = strip[8 * b : 8 * b + 8, :]
-    results = [
-        pltpu.make_async_copy(src, dst, sent.at[i])
-        for i, (src, dst) in enumerate(((strip, strip_h), (block, block_h)))
-    ]
-    for c in results:
-        c.start()
+    results[2].start()
+    results[3].start()
     for c in results:
         c.wait()
 
@@ -607,7 +609,7 @@
         [air.reshape(FL, 2, AC), kdiff, elev, cond, rain_factor, land_mask, flow_code, depth_init, soil_init,
          link_flow.reshape(1, LINKS)],
         [(1, LINKS), (FL, 2, AC), (2, AC), land_v, land_v, land_v, code_v, code_v, land_v, land_v, (BLOCK, TC), (24, 128),
-         pltpu.SemaphoreType.DMA((10,)), pltpu.SemaphoreType.DMA((2,))],
+         pltpu.SemaphoreType.DMA((10,)), pltpu.SemaphoreType.DMA((4,))],
         limit=WHOLE,
         far=2,
     )

time: 114 us -> 114 us (level)
  no operation moved by 1% of the time
where the time goes in v5:
time: 114 us; the launch traced here: 113 us
  starting transfers between devices  61.4 us (54%)
  waiting for transfers between devices  24.7 us (22%)
  Pallas kernels  21.9 us (19%)
  local copies, waits for them, and re-layouts  3.71 us (3%)
    ppermute x11, starting transfers between devices, exchange(): return lax.ppermute(value, AXES, pairs)  56.6 us
    pallas_call x9, Pallas kernels, call(): pl.pallas_call(body, out_shape=[jax.ShapeDtypeStruct(o, F32) for o in out...  21.9 us
    ppermute x11, waiting for transfers between devices, exchange(): return lax.ppermute(value, AXES, pairs)  19.8 us
    all_to_all x1, waiting for transfers between devices, shards(): got = lax.all_to_all(chunks, 'gx', 0, 0)  4.89 us
    all_to_all x1, starting transfers between devices, shards(): got = lax.all_to_all(chunks, 'gx', 0, 0)  4.81 us
    unnamed x22, local copies, waits for them, and re-layouts  3.11 us
  transfers between devices with their start and end apart: 12, of which 7 were waited for; matrix products, arithmetic and copies ran while one was open for 1% of the time, Pallas kernels for 10%

profile of v5, /device:TPU:7, one launch (start us, length us, event | category | flops | bytes accessed | tf_op | source)
XLA Modules:
  0.0 113.2 jit_solution(1997525199625723582)
XLA Ops:
  0.6 0.7 pad_add_fusion.info
  1.3 3.1 %shard_map.165 = (f32[104,3072]{1,0:T(8,128)}, f32[24,128]{1,0:T(8,128)}) custom-call(s32[4]{0:T(128)} %pad_add_fusion.info, f32[64,2,768]{2,1,0:T(2,128)} %bitcast.19, f32[2,768]{1,0:T(2,128)} %kd.1, f32[8,3072]{1,0:T(8,128)} %elev.1, f32[8,3072]{1,0:T(8,128)} %cond.1, f32[8,3072]{1,0:T(8,128)} %rf.1, s32[8,3072]{1,0:T(8,128)} %mask.1, s32[8,3072]{1,0:T(8,128)} %code.1, ...), custom_call_target="tpu_custom_call" | custom-call | tf_op jit(solution)/shard_map/pallas_call | solution.py:85
  4.4 0.0 copy-start.9
  4.4 2.6 %collective-permute-start = (f32[104,3072]{1,0:T(8,128)}, f32[104,3072]{1,0:T(8,128)S(1)}, u32[]{:S(2)}, u32[]{:S(2)}) collective-permute-start(f32[104,3072]{1,0:T(8,128)} %get-tuple-element.41.block), channel_id=1, source_target_pairs={{0,2},{1,3},{2,0},{3,1},{4,6},{5,7},{6,4},{7,5},{8,10},{9,11},{10,... | collective-permute-start | bytes 3833864 | tf_op jit(solution)/shard_map/ppermute | solution.py:36
  7.0 0.0 copy-start.6
  7.0 0.0 copy-start.7
  7.0 13.8 %collective-permute-start.2 = (f32[24,128]{1,0:T(8,128)}, f32[24,128]{1,0:T(8,128)S(1)}, u32[]{:S(2)}, u32[]{:S(2)}) collective-permute-start(f32[24,128]{1,0:T(8,128)} %get-tuple-element.42), channel_id=1, source_target_pairs={{0,4},{1,5},{4,8},{5,9},{6,2},{7,3},{8,12},{9,13},{10,6},{11,7},{1... | collective-permute-start | bytes 36872 | tf_op jit(solution)/shard_map/ppermute | solution.py:36
  20.9 1.9 %collective-permute-start.1 = (f32[24,128]{1,0:T(8,128)}, f32[24,128]{1,0:T(8,128)S(1)}, u32[]{:S(2)}, u32[]{:S(2)}) collective-permute-start(f32[24,128]{1,0:T(8,128)} %get-tuple-element.42), channel_id=1, source_target_pairs={{2,4},{3,5},{4,2},{5,3},{6,8},{7,9},{8,6},{9,7},{10,12},{11,13},{1... | collective-permute-start | bytes 36872 | tf_op jit(solution)/shard_map/ppermute | solution.py:36
  22.8 0.0 collective-permute-done.2.near2
  22.8 3.3 %collective-permute-done.1.near = f32[24,128]{1,0:T(8,128)S(1)} collective-permute-done((f32[24,128]{1,0:T(8,128)}, f32[24,128]{1,0:T(8,128)S(1)}, u32[]{:S(2)}, u32[]{:S(2)}) %collective-permute-start.1) | collective-permute-done | bytes 12320 | tf_op jit(solution)/shard_map/ppermute | solution.py:36
  26.1 0.0 collective-permute-done.pin
  26.1 1.3 %copy-done = f32[104,3072]{1,0:T(8,128)S(1)} copy-done((f32[104,3072]{1,0:T(8,128)S(1)}, f32[104,3072]{1,0:T(8,128)}, u32[]{:S(2)}) %copy-start) | copy-done | bytes 1277976
  27.4 0.7 copy-done.4
  28.1 0.7 shard_map.166
  28.8 1.9 %collective-permute-start.3 = (f32[56,3072]{1,0:T(8,128)S(1)}, f32[56,3072]{1,0:T(8,128)S(1)}, u32[]{:S(2)}, u32[]{:S(2)}) collective-permute-start(f32[56,3072]{1,0:T(8,128)S(1)} %get-tuple-element.43), channel_id=1, source_target_pairs={{2,4},{3,5},{4,2},{5,3},{6,8},{7,9},{8,6},{9,7},{10,12},{11,13},{1... | collective-permute-start | bytes 2064392 | tf_op jit(solution)/shard_map/ppermute | solution.py:36
  30.7 6.3 %collective-permute-start.4 = (f32[64,128]{1,0:T(8,128)S(1)}, f32[64,128]{1,0:T(8,128)S(1)}, u32[]{:S(2)}, u32[]{:S(2)}) collective-permute-start(f32[64,128]{1,0:T(8,128)S(1)} %get-tuple-element.45), channel_id=1, source_target_pairs={{2,3},{3,2},{4,5},{5,4},{6,7},{7,6},{8,9},{9,8},{10,11},{11,10},{1... | collective-permute-start | bytes 98312 | tf_op jit(solution)/shard_map/ppermute | solution.py:36
  37.1 8.0 %collective-permute-done.4.across = f32[64,128]{1,0:T(8,128)S(1)} collective-permute-done((f32[64,128]{1,0:T(8,128)S(1)}, f32[64,128]{1,0:T(8,128)S(1)}, u32[]{:S(2)}, u32[]{:S(2)}) %collective-permute-start.4) | collective-permute-done | bytes 32800 | tf_op jit(solution)/shard_map/ppermute | solution.py:36
  45.1 0.5 shard_map.167.strips.nr
  45.7 1.9 %collective-permute-start.5 = (f32[64,128]{1,0:T(8,128)S(1)}, f32[64,128]{1,0:T(8,128)S(1)}, u32[]{:S(2)}, u32[]{:S(2)}) collective-permute-start(f32[64,128]{1,0:T(8,128)S(1)} %shard_map.167.strips.nr), channel_id=1, source_target_pairs={{0,2},{1,3},{2,0},{3,1},{4,6},{5,7},{6,4},{7,5},{8,10},{9,11},{10,... | collective-permute-start | bytes 98312 | tf_op jit(solution)/shard_map/ppermute | solution.py:36
  47.6 1.2 %collective-permute-done.5.far_strips.fs = f32[64,128]{1,0:T(8,128)S(1)} collective-permute-done((f32[64,128]{1,0:T(8,128)S(1)}, f32[64,128]{1,0:T(8,128)S(1)}, u32[]{:S(2)}, u32[]{:S(2)}) %collective-permute-start.5) | collective-permute-done | bytes 32800 | tf_op jit(solution)/shard_map/ppermute | solution.py:36
  48.8 0.0 collective-permute-done.3.out
  48.8 8.0 %collective-permute-start.6 = (f32[56,3072]{1,0:T(8,128)S(1)}, f32[56,3072]{1,0:T(8,128)S(1)}, u32[]{:S(2)}, u32[]{:S(2)}) collective-permute-start(f32[56,3072]{1,0:T(8,128)S(1)} %collective-permute-done.3.out), channel_id=1, source_target_pairs={{0,2},{1,3},{2,0},{3,1},{4,6},{5,7},{6,4},{7,5},{8,10},{9,11},{10,... | collective-permute-start | bytes 2064392 | tf_op jit(solution)/shard_map/ppermute | solution.py:36
  56.8 1.7 %collective-permute-done.6.far = f32[56,3072]{1,0:T(8,128)S(1)} collective-permute-done((f32[56,3072]{1,0:T(8,128)S(1)}, f32[56,3072]{1,0:T(8,128)S(1)}, u32[]{:S(2)}, u32[]{:S(2)}) %collective-permute-start.6) | collective-permute-done | bytes 688160 | tf_op jit(solution)/shard_map/ppermute | solution.py:36
  58.6 0.0 copy-done.9
  58.6 0.0 copy-done.6
  58.6 0.0 copy-done.7
  58.6 0.0 copy-done.1
  58.6 3.3 %shard_map.168 = (f32[5,24,3200]{2,1,0:T(8,128)S(1)}, f32[24,3200]{1,0:T(8,128)S(1)}, f32[24,3200]{1,0:T(8,128)S(1)}, f32[16,3200]{1,0:T(8,128)S(1)}, f32[24,320...) custom-call(s32[4]{0:T(128)S(1)} %copy-done.4, ...), custom_call_target="tpu_custom_call" | custom-call | tf_op jit(solution)/shard_map/pallas_call | solution.py:85
  61.9 0.0 copy-start.8
  61.9 0.0 copy-start.10
  61.9 1.9 %collective-permute-start.7 = (f32[8,3200]{1,0:T(8,128)S(1)}, f32[8,3200]{1,0:T(8,128)S(1)}, u32[]{:S(2)}, u32[]{:S(2)}) collective-permute-start(f32[8,3200]{1,0:T(8,128)S(1)} %get-tuple-element.57.edge), channel_id=1, source_target_pairs={{2,4},{3,5},{4,2},{5,3},{6,8},{7,9},{8,6},{9,7},{10,12},{11,13},{1... | collective-permute-start | bytes 307208 | tf_op jit(solution)/shard_map/ppermute | solution.py:36
  63.9 0.8 shard_map.171
  64.6 3.6 %collective-permute-start.10 = (f32[32,3072]{1,0:T(8,128)}, f32[32,3072]{1,0:T(8,128)}, u32[]{:S(2)}, u32[]{:S(2)}) collective-permute-start(f32[32,3072]{1,0:T(8,128)} %shard_map.171), channel_id=1, source_target_pairs={{2,4},{3,5},{4,2},{5,3},{6,8},{7,9},{8,6},{9,7},{10,12},{11,13},{1... | collective-permute-start | bytes 1179656 | tf_op jit(solution)/shard_map/ppermute | solution.py:36
  68.3 0.0 collective-permute-done.7.out
  68.3 12.6 %collective-permute-start.8 = (f32[8,3200]{1,0:T(8,128)S(1)}, f32[8,3200]{1,0:T(8,128)S(1)}, u32[]{:S(2)}, u32[]{:S(2)}) collective-permute-start(f32[8,3200]{1,0:T(8,128)S(1)} %collective-permute-done.7.out), channel_id=1, source_target_pairs={{0,2},{1,3},{2,0},{3,1},{4,6},{5,7},{6,4},{7,5},{8,10},{9,11},{10,... | collective-permute-start | bytes 307208 | tf_op jit(solution)/shard_map/ppermute | solution.py:36
  80.9 0.9 collective-permute-done.8.far
  81.8 0.0 copy-done.10
  81.8 2.9 %shard_map.169 = (f32[8,3072]{1,0:T(8,128)}, f32[2,768]{1,0:T(2,128)}, f32[2,768]{1,0:T(2,128)S(1)}, f32[24,128]{1,0:T(8,128)S(1)}) custom-call(s32[4]{0:T(128)S(1)} %copy-done.4, f32[32]{0:T(128)S(1)} %copy-done.6, f32[32]{0:T(128)S(1)} %copy-done.7, s32[2,128]{1,0:T(2,128)S(1)} %bitcast.16, f32[2,128]{1,0:T(2,128)S(1)} %bitcast.14, s32[2,128]{1,0:T(2,128)S(1)} %bitcast.17, ...), custom_call_target="tpu_custom_call" | custom-call | tf_op jit(solution)/shard_map/pallas_call | solution.py:85
  84.7 1.9 %collective-permute-start.9 = (f32[24,128]{1,0:T(8,128)S(1)}, f32[24,128]{1,0:T(8,128)S(1)}, u32[]{:S(2)}, u32[]{:S(2)}) collective-permute-start(f32[24,128]{1,0:T(8,128)S(1)} %get-tuple-element.58.own), channel_id=1, source_target_pairs={{0,32},{1,33},{2,34},{3,35},{4,36},{5,37},{6,38},{7,39},{8,40},{9,... | collective-permute-start | bytes 36872 | tf_op jit(solution)/shard_map/ppermute | solution.py:36
  86.7 4.6 %collective-permute-done.9.before = f32[24,128]{1,0:T(8,128)S(1)} collective-permute-done((f32[24,128]{1,0:T(8,128)S(1)}, f32[24,128]{1,0:T(8,128)S(1)}, u32[]{:S(2)}, u32[]{:S(2)}) %collective-permute-start.9) | collective-permute-done | bytes 12320 | tf_op jit(solution)/shard_map/ppermute | solution.py:36
  91.3 1.2 %shard_map.170 = f32[16,16,128]{2,1,0:T(8,128)} custom-call(s32[4]{0:T(128)S(1)} %copy-done.4, f32[24,128]{1,0:T(8,128)S(1)} %get-tuple-element.58.own, f32[24,128]{1,0:T(8,128)S(1)} %collective-permute-done.9.before), custom_call_target="tpu_custom_call" | custom-call | tf_op jit(solution)/shard_map/pallas_call | solution.py:85
  92.5 4.8 %all-to-all-start = ((f32[16,16,128]{2,1,0:T(8,128)}), f32[16,16,128]{2,1,0:T(8,128)S(1)}, u32[]{:S(2)}, u32[]{:S(2)}) async-start(f32[16,16,128]{2,1,0:T(8,128)} %shard_map.170), calls=%async_computation | async-start | bytes 262144 | tf_op jit(solution)/shard_map/all_to_all | solution.py:649
  97.3 0.0 collective-permute-done.10.second
  97.3 1.1 copy-done.3
  98.4 5.5 %shard_map.172 = f32[64,2,768]{2,1,0:T(2,128)} custom-call(s32[4]{0:T(128)S(1)} %copy-done.5, f32[32]{0:T(128)S(1)} %copy-done.6, f32[32]{0:T(128)S(1)} %copy-done.7, f32[104,3072]{1,0:T(8,128)S(1)} %copy-done.1, f32[104,3072]{1,0:T(8,128)S(1)} %collective-permute-done.pin, f32[56,3072]{1,0:T(8,128)S(1)} %collective-permute-done.3.out, ...), custom_call_target="tpu_custom_call" | custom-call | tf_op jit(solution)/shard_map/pallas_call | solution.py:85
  103.9 0.6 bitcast_dynamic-update-slice_fusion
  104.5 4.9 %all-to-all-done.got = f32[16,16,128]{2,1,0:T(8,128)S(1)} async-done(((f32[16,16,128]{2,1,0:T(8,128)}), f32[16,16,128]{2,1,0:T(8,128)S(1)}, u32[]{:S(2)}, u32[]{:S(2)}) %all-to-all-start) | async-done | bytes 131104 | tf_op jit(solution)/shard_map/all_to_all | solution.py:649
  109.4 3.8 %shard_map.173 = f32[1,256]{1,0:T(1,128)} custom-call(s32[4]{0:T(128)S(1)} %copy-done.5, f32[24,128]{1,0:T(8,128)S(1)} %get-tuple-element.58.own, f32[16,16,128]{2,1,0:T(8,128)S(1)} %all-to-all-done.got, f32[2,128]{1,0:T(2,128)S(1)} %get-tuple-element.65.above), custom_call_target="tpu_custom_call" | custom-call | tf_op jit(solution)/shard_map/pallas_call | solution.py:85
  (9 shorter events, 0.0 us)
Async XLA Ops:
  4.4 54.1 %copy-start.9 = (s32[256]{0:T(256)S(1)}, s32[256]{0:T(256)}, u32[]{:S(2)}) copy-start(s32[256]{0:T(256)} %param.27) | copy-start | bytes 3076
  4.4 21.7 %collective-permute-start = (f32[104,3072]{1,0:T(8,128)}, f32[104,3072]{1,0:T(8,128)S(1)}, u32[]{:S(2)}, u32[]{:S(2)}) collective-permute-start(f32[104,3072]{1,0:T(8,128)} %get-tuple-element.41.block), channel_id=1, source_target_pairs={{0,2},{1,3},{2,0},{3,1},{4,6},{5,7},{6,4},{7,5},{8,10},{9,11},{10,... | collective-permute-start | bytes 3833864 | tf_op jit(solution)/shard_map/ppermute | solution.py:36
  7.0 51.5 %copy-start.6 = (f32[32]{0:T(128)S(1)}, f32[32]{0:T(128)}, u32[]{:S(2)}) copy-start(f32[32]{0:T(128)} %u.5) | copy-start | bytes 388
  7.0 51.5 %copy-start.7 = (f32[32]{0:T(128)S(1)}, f32[32]{0:T(128)}, u32[]{:S(2)}) copy-start(f32[32]{0:T(128)} %v.5) | copy-start | bytes 388
  7.0 15.8 %collective-permute-start.2 = (f32[24,128]{1,0:T(8,128)}, f32[24,128]{1,0:T(8,128)S(1)}, u32[]{:S(2)}, u32[]{:S(2)}) collective-permute-start(f32[24,128]{1,0:T(8,128)} %get-tuple-element.42), channel_id=1, source_target_pairs={{0,4},{1,5},{4,8},{5,9},{6,2},{7,3},{8,12},{9,13},{10,6},{11,7},{1... | collective-permute-start | bytes 36872 | tf_op jit(solution)/shard_map/ppermute | solution.py:36
  20.9 5.2 %collective-permute-start.1 = (f32[24,128]{1,0:T(8,128)}, f32[24,128]{1,0:T(8,128)S(1)}, u32[]{:S(2)}, u32[]{:S(2)}) collective-permute-start(f32[24,128]{1,0:T(8,128)} %get-tuple-element.42), channel_id=1, source_target_pairs={{2,4},{3,5},{4,2},{5,3},{6,8},{7,9},{8,6},{9,7},{10,12},{11,13},{1... | collective-permute-start | bytes 36872 | tf_op jit(solution)/shard_map/ppermute | solution.py:36
  26.1 1.3 %copy-start = (f32[104,3072]{1,0:T(8,128)S(1)}, f32[104,3072]{1,0:T(8,128)}, u32[]{:S(2)}) copy-start(f32[104,3072]{1,0:T(8,128)} %get-tuple-element.41.block) | copy-start | bytes 3833860
  27.4 0.7 copy-start.4
  28.1 30.5 %copy-start.1 = (f32[104,3072]{1,0:T(8,128)S(1)}, f32[104,3072]{1,0:T(8,128)}, u32[]{:S(2)}) copy-start(f32[104,3072]{1,0:T(8,128)} %get-tuple-element.41.block) | copy-start | bytes 3833860
  28.8 20.0 %collective-permute-start.3 = (f32[56,3072]{1,0:T(8,128)S(1)}, f32[56,3072]{1,0:T(8,128)S(1)}, u32[]{:S(2)}, u32[]{:S(2)}) collective-permute-start(f32[56,3072]{1,0:T(8,128)S(1)} %get-tuple-element.43), channel_id=1, source_target_pairs={{2,4},{3,5},{4,2},{5,3},{6,8},{7,9},{8,6},{9,7},{10,12},{11,13},{1... | collective-permute-start | bytes 2064392 | tf_op jit(solution)/shard_map/ppermute | solution.py:36
  30.7 14.4 %collective-permute-start.4 = (f32[64,128]{1,0:T(8,128)S(1)}, f32[64,128]{1,0:T(8,128)S(1)}, u32[]{:S(2)}, u32[]{:S(2)}) collective-permute-start(f32[64,128]{1,0:T(8,128)S(1)} %get-tuple-element.45), channel_id=1, source_target_pairs={{2,3},{3,2},{4,5},{5,4},{6,7},{7,6},{8,9},{9,8},{10,11},{11,10},{1... | collective-permute-start | bytes 98312 | tf_op jit(solution)/shard_map/ppermute | solution.py:36
  45.7 3.1 %collective-permute-start.5 = (f32[64,128]{1,0:T(8,128)S(1)}, f32[64,128]{1,0:T(8,128)S(1)}, u32[]{:S(2)}, u32[]{:S(2)}) collective-permute-start(f32[64,128]{1,0:T(8,128)S(1)} %shard_map.167.strips.nr), channel_id=1, source_target_pairs={{0,2},{1,3},{2,0},{3,1},{4,6},{5,7},{6,4},{7,5},{8,10},{9,11},{10,... | collective-permute-start | bytes 98312 | tf_op jit(solution)/shard_map/ppermute | solution.py:36
  48.8 9.8 %collective-permute-start.6 = (f32[56,3072]{1,0:T(8,128)S(1)}, f32[56,3072]{1,0:T(8,128)S(1)}, u32[]{:S(2)}, u32[]{:S(2)}) collective-permute-start(f32[56,3072]{1,0:T(8,128)S(1)} %collective-permute-done.3.out), channel_id=1, source_target_pairs={{0,2},{1,3},{2,0},{3,1},{4,6},{5,7},{6,4},{7,5},{8,10},{9,11},{10,... | collective-permute-start | bytes 2064392 | tf_op jit(solution)/shard_map/ppermute | solution.py:36
  58.6 3.3 %copy-start.2 = (f32[56,3072]{1,0:T(8,128)}, f32[56,3072]{1,0:T(8,128)S(1)}, u32[]{:S(2)}) copy-start(f32[56,3072]{1,0:T(8,128)S(1)} %collective-permute-done.6.far) | copy-start | bytes 2064388
  61.9 19.9 %copy-start.8 = (f32[256]{0:T(256)S(1)}, f32[256]{0:T(256)}, u32[]{:S(2)}) copy-start(f32[256]{0:T(256)} %param.29) | copy-start | bytes 3076
  61.9 19.9 %copy-start.10 = (s32[256]{0:T(256)S(1)}, s32[256]{0:T(256)}, u32[]{:S(2)}) copy-start(s32[256]{0:T(256)} %param.28) | copy-start | bytes 3076
  61.9 6.3 %collective-permute-start.7 = (f32[8,3200]{1,0:T(8,128)S(1)}, f32[8,3200]{1,0:T(8,128)S(1)}, u32[]{:S(2)}, u32[]{:S(2)}) collective-permute-start(f32[8,3200]{1,0:T(8,128)S(1)} %get-tuple-element.57.edge), channel_id=1, source_target_pairs={{2,4},{3,5},{4,2},{5,3},{6,8},{7,9},{8,6},{9,7},{10,12},{11,13},{1... | collective-permute-start | bytes 307208 | tf_op jit(solution)/shard_map/ppermute | solution.py:36
  64.6 32.7 %collective-permute-start.10 = (f32[32,3072]{1,0:T(8,128)}, f32[32,3072]{1,0:T(8,128)}, u32[]{:S(2)}, u32[]{:S(2)}) collective-permute-start(f32[32,3072]{1,0:T(8,128)} %shard_map.171), channel_id=1, source_target_pairs={{2,4},{3,5},{4,2},{5,3},{6,8},{7,9},{8,6},{9,7},{10,12},{11,13},{1... | collective-permute-start | bytes 1179656 | tf_op jit(solution)/shard_map/ppermute | solution.py:36
  68.3 13.5 %collective-permute-start.8 = (f32[8,3200]{1,0:T(8,128)S(1)}, f32[8,3200]{1,0:T(8,128)S(1)}, u32[]{:S(2)}, u32[]{:S(2)}) collective-permute-start(f32[8,3200]{1,0:T(8,128)S(1)} %collective-permute-done.7.out), channel_id=1, source_target_pairs={{0,2},{1,3},{2,0},{3,1},{4,6},{5,7},{6,4},{7,5},{8,10},{9,11},{10,... | collective-permute-start | bytes 307208 | tf_op jit(solution)/shard_map/ppermute | solution.py:36
  81.8 15.5 %copy-start.5 = (s32[4]{0:T(128)S(1)}, s32[4]{0:T(128)}, u32[]{:S(2)}) copy-start(s32[4]{0:T(128)} %pad_add_fusion.info) | copy-start | bytes 52
  84.7 6.5 %collective-permute-start.9 = (f32[24,128]{1,0:T(8,128)S(1)}, f32[24,128]{1,0:T(8,128)S(1)}, u32[]{:S(2)}, u32[]{:S(2)}) collective-permute-start(f32[24,128]{1,0:T(8,128)S(1)} %get-tuple-element.58.own), channel_id=1, source_target_pairs={{0,32},{1,33},{2,34},{3,35},{4,36},{5,37},{6,38},{7,39},{8,40},{9,... | collective-permute-start | bytes 36872 | tf_op jit(solution)/shard_map/ppermute | solution.py:36
  92.5 16.9 %all-to-all-start = ((f32[16,16,128]{2,1,0:T(8,128)}), f32[16,16,128]{2,1,0:T(8,128)S(1)}, u32[]{:S(2)}, u32[]{:S(2)}) async-start(f32[16,16,128]{2,1,0:T(8,128)} %shard_map.170), calls=%async_computation | async-start | bytes 262144 | tf_op jit(solution)/shard_map/all_to_all | solution.py:649
  97.3 1.1 copy-start.3
